TPU v7x, 512 devices: a whole 4x8x8 slice. The times are simulated.
512 devices in a mesh: dp: 32 (over x_hi, y, core), layer: 8 (over z), query: 2 (over x_lo).
Axes of the slice: x: 4 (x_hi: 2, x_lo: 2; x = x_hi * 2 + x_lo), y: 8, z: 8, core: 2. Of those that a mesh axis runs over, the one named last changes fastest.
Arguments:
- stored_grads: bfloat16 [8192, 8, 4096], P(('dp', 'query'), 'layer'), may hold values from -6 to 6
- query_grads: bfloat16 [1024, 8, 4096], P('query', 'layer', 'dp'), may hold values from -6 to 6
- fisher_inverse: bfloat16 [8, 4096, 4096], P('layer', 'dp'), as said below
Outputs:
- influence: float32 [8192, 1024], P(('dp', 'query'))
Inputs may be any that keep to these rules, and one draw needn't show every extreme that they name: fisher_inverse[l] is symmetric for every layer l, its diagonal entries lie between 0.5 and 1.6 and its other entries are under 0.03 in size.
All inputs are finite; a program needn't handle non-finite values.
Results may differ from a plain program's by a relative error of at most 0.0029.
Values may be sent and summed in bfloat16 or wider, within the bound.
No kernel may reach another device: no remote copies, remote signals or barrier semaphores. Data moves between devices by JAX's collectives and lax.ppermute only.
A program may use at most 64 MiB of HBM per device.

v0:
```python
import math

import jax
import jax.numpy as jnp
from jax import lax
from jax.sharding import PartitionSpec as P


def precondition(query_grads, fisher_inverse):
    folded = lax.dot_general(
        lax.all_gather(query_grads, "dp", axis=2, tiled=True),
        fisher_inverse,
        (((2,), (2,)), ((1,), (0,))),
        preferred_element_type=jnp.float32,
    )
    return folded.astype(jnp.bfloat16)


def score_rows(stored_rows, precond):
    return lax.dot_general(
        stored_rows,
        lax.all_gather(precond, "dp", axis=2, tiled=True),
        (((1, 2), (0, 2)), ((), ())),
        preferred_element_type=jnp.float32,
    )


def shards(stored_grads, query_grads, fisher_inverse):
    precond = precondition(query_grads, fisher_inverse)
    both_blocks = lax.all_gather(precond, "query", axis=1, tiled=True)
    partial_scores = score_rows(stored_grads, both_blocks)
    totals = lax.psum(partial_scores, "layer")
    factor = 1.0 / math.sqrt(
        fisher_inverse.shape[0] * lax.axis_size("layer") * stored_grads.shape[2]
    )
    return totals * factor


def solution(mesh):
    placed = (P(("dp", "query"), "layer", None), P("query", "layer", "dp"), P("layer", "dp", None))
    return jax.shard_map(
        shards, mesh=mesh, in_specs=placed, out_specs=P(("dp", "query"), None), check_vma=False
    )
```

profile of v0, /device:TPU:6, one launch (start us, length us, event | category | flops | bytes accessed | tf_op | source)
XLA Modules:
  0.0 319.8 jit_solution(7104415453092312354)
XLA Ops:
  6.5 0.0 copy-start
  6.5 0.0 all-gather.5.cloned.1.call-start
  6.5 0.7 all-gather.5.cloned.1.call-update
  7.3 0.0 all-gather.7.cloned.1.call-start
  7.3 98.3 %all-gather.5.cloned.1.call-done = bf16[512,1,4096]{2,0,1:T(8,128)(2,1)} async-done(((bf16[512,1,128]{2,0,1:T(8,128)(2,1)}), bf16[512,1,4096]{2,0,1:T(8,128)(2,1)}) %all-gather.5.cloned.1.call-update) | async-done | bytes 4194320 | tf_op jit(solution)/shard_map/all_gather | solution.py:11
  105.6 3.7 %fusion.2 = bf16[512,128]{1,0:T(8,128)(2,1)S(1)} fusion(bf16[512,1,4096]{2,0,1:T(8,128)(2,1)} %all-gather.5.cloned.1.call-done, bf16[1,128,4096]{2,1,0:T(8,128)(2,1)} %param.5), kind=kOutput, calls=%fused_computation.3 | convolution fusion | flops 536936448 | bytes 5373952 | tf_op jit(solution)/shard_map/dot_general | solution.py:10
  109.3 6.4 %all-gather = bf16[1024,128]{1,0:T(8,128)(2,1)} all-gather(bf16[512,128]{1,0:T(8,128)(2,1)S(1)} %fusion.2), channel_id=2, replica_groups=mesh['dp'=32,'layer'=8,'query'=2] {'query'}, dimensions={0}, use_global_device_ids=true | all-gather | bytes 393216 | tf_op jit(solution)/shard_map/all_gather | solution.py:30
  115.8 0.0 all-gather.7.cloned.1.call-update
  115.8 0.0 all-reduce.2.cloned.1.call-start
  115.9 110.8 %all-gather.7.cloned.1.call-done = bf16[1024,4096]{1,0:T(8,128)(2,1)} async-done(((bf16[1024,128]{1,0:T(8,128)(2,1)}), bf16[1024,4096]{1,0:T(8,128)(2,1)}) %all-gather.7.cloned.1.call-update) | async-done | bytes 8388624 | tf_op jit(solution)/shard_map/all_gather | solution.py:22
  226.6 0.0 copy-done
  226.6 6.5 %convolution_bitcast_fusion = f32[128,1024]{0,1:T(8,128)} fusion(bf16[1024,4096]{1,0:T(8,128)(2,1)} %all-gather.7.cloned.1.call-done, bf16[128,1,4096]{2,0,1:T(8,128)(2,1)S(1)} %copy-done), kind=kOutput, calls=%fused_computation.2 | convolution fusion | flops 1073741824 | bytes 9961472 | tf_op jit(solution)/shard_map/dot_general | solution.py:20
  233.1 0.0 all-reduce.2.cloned.1.call-update
  233.2 78.0 %all-reduce.2.cloned.1.call-done = f32[128,1024]{0,1:T(8,128)} async-done(((f32[128,1024]{0,1:T(8,128)}), f32[128,1024]{0,1:T(8,128)}) %all-reduce.2.cloned.1.call-update) | async-done | bytes 524304 | tf_op jit(solution)/shard_map/psum | solution.py:32
  311.2 1.1 broadcast_multiply_fusion
  312.3 1.0 copy.4
Async XLA Ops:
  6.5 220.1 %copy-start = (bf16[128,1,4096]{2,0,1:T(8,128)(2,1)S(1)}, bf16[128,1,4096]{2,0,1:T(8,128)(2,1)}, u32[]{:S(2)}) copy-start(bf16[128,1,4096]{2,0,1:T(8,128)(2,1)} %param.3) | copy-start | bytes 3145732
  6.5 99.1 %all-gather.5.cloned.1.call-start = ((), (), s32[]{:S(2)}) async-start(), calls=%async_computation | async-start | bytes 4325376 | tf_op jit(solution)/shard_map/all_gather | solution.py:11
  7.3 219.4 %all-gather.7.cloned.1.call-start = ((), (), s32[]{:S(2)}) async-start(), calls=%async_computation.2 | async-start | bytes 8650752 | tf_op jit(solution)/shard_map/all_gather | solution.py:22
  115.8 195.4 %all-reduce.2.cloned.1.call-start = ((), (), s32[]{:S(2)}) async-start(), calls=%async_computation.1 | async-start | bytes 1048576 | tf_op jit(solution)/shard_map/psum | solution.py:32
Sparse Core Ops, SparseCore 0:
  10.5 95.0 all-gather.4
  115.9 110.6 all-gather.6
  233.3 77.8 all-reduce.1
where the time goes:
time: 320 us
  waiting for transfers between devices  288 us (90%)
  between operations  13.1 us (4%)
  matrix products  10.3 us (3%)
  blocking collectives  6.44 us (2%)
    all_gather x1, waiting for transfers between devices, score_rows(): lax.all_gather(precond, 'dp', axis=2, tiled=True)  111 us
    all_gather x1, waiting for transfers between devices, precondition(): lax.all_gather(query_grads, 'dp', axis=2, tiled=True)  98.3 us
    psum x1, waiting for transfers between devices, shards(): totals = lax.psum(partial_scores, 'layer')  78 us
    dot_general x1, matrix products, score_rows(): lax.dot_general(stored_rows, lax.all_gather(precond, 'dp', axis=2, tiled=...  6.51 us
    all_gather x1, blocking collectives, shards(): both_blocks = lax.all_gather(precond, 'query', axis=1, tiled=True)  6.44 us
  transfers between devices with their start and end apart: 3, of which 3 were waited for; matrix products, arithmetic and copies ran while one was open for 0% of the time, Pallas kernels for 0%

commit v1 on v0

v1 whole, which is shorter than its diff:
```python
import functools
import math

import jax
import jax.numpy as jnp
from jax import lax
from jax.experimental import pallas as pl
from jax.experimental.pallas import tpu as pltpu
from jax.sharding import Mesh, PartitionSpec as P

F32 = jnp.float32
BF16 = jnp.bfloat16
PARTS = 1
NT = (((1,), (1,)), ((), ()))
PARAMS = pltpu.CompilerParams(vmem_limit_bytes=40 * 1024 * 1024)
WHOLE = pl.BlockSpec(memory_space=pltpu.VMEM)
SCALARS = pl.BlockSpec(memory_space=pltpu.SMEM)


def call(body, out_shape, inputs, scratch=(), flops=0):
    size = sum(math.prod(x.shape) * x.dtype.itemsize for x in (*inputs, *out_shape))
    return pl.pallas_call(
        body,
        out_shape=[jax.ShapeDtypeStruct(s.shape, s.dtype) for s in out_shape],
        in_specs=[SCALARS if x.dtype == jnp.int32 else WHOLE for x in inputs],
        out_specs=[WHOLE] * len(out_shape),
        scratch_shapes=scratch,
        compiler_params=PARAMS,
        cost_estimate=pl.CostEstimate(flops=flops, bytes_accessed=size, transcendentals=0),
    )(*inputs)


def like(*shape, dtype=BF16):
    return jax.ShapeDtypeStruct(shape, dtype)


def pack_body(ny, w, me, x, own, other):
    for dc, out in enumerate((own, other)):
        for dx in range(2):
            for y in range(ny):
                first = (((me[0] ^ dx) * ny + y) * 2 + (me[1] ^ dc)) * w
                out[dx, :, y * w : (y + 1) * w] = x[:, pl.ds(pl.multiple_of(first, w), w)]


def pack(me, x, ny, w):
    n = x.shape[0]
    return call(functools.partial(pack_body, ny, w), [like(2, n, ny * w)] * 2, [me, x])


def fold_body(feats, f00, f01, f10, f11, own, other, held):
    ny, _, w = feats.shape
    for y in range(ny):
        held[:, y * w : (y + 1) * w] = feats[y]
    for out, blocks in ((own, (f00, f10)), (other, (f01, f11))):
        for dx in range(2):
            out[dx] = lax.dot_general(held[...], blocks[dx][...], NT, preferred_element_type=F32)


def fold(feats, blocks):
    ny, q, w = feats.shape
    return call(
        fold_body,
        [like(2, q, w, dtype=F32)] * 2,
        [feats, *blocks],
        [pltpu.VMEM((q, ny * w), BF16)],
        flops=2 * q * ny * w * 4 * w,
    )


def score_body(precond, *refs):
    blocks, (own, other, held) = refs[:-3], refs[-3:]
    ny, _, w = precond.shape
    for y in range(ny):
        held[:, y * w : (y + 1) * w] = precond[y]
    for i in range(4):
        for dc, out in enumerate((own, other)):
            out[i] = lax.dot_general(blocks[i][dc], held[...], NT, preferred_element_type=F32)


def score(precond, blocks):
    ny, q, w = precond.shape
    n = blocks[0].shape[1]
    return call(
        score_body,
        [like(4, n, q, dtype=F32)] * 2,
        [precond, *blocks],
        [pltpu.VMEM((q, ny * w), BF16)],
        flops=2 * q * ny * w * 8 * n,
    )


def meet_body(me, own, came, out):
    for x in range(2):
        for l in range(2):
            i = (x ^ me[0]) * 2 + (l ^ me[2])
            out[x * 2 + l] = (own[i] + came[i]).astype(BF16)


def meet(me, own, came):
    return call(meet_body, [like(*own.shape)], [me, own, came])[0]


def swap(x, *axes):
    sizes = [lax.axis_size(a) for a in axes]
    n = math.prod(sizes)
    return lax.ppermute(x, axes, [(i, n - 1 - i) for i in range(n)])


def spread(x, axis):
    n = lax.axis_size(axis)
    return lax.all_to_all(jnp.broadcast_to(x[None], (n,) + x.shape), axis, 0, 0, tiled=True)


def shards(stored, query, fisher):
    ny, nz, nl = lax.axis_size("y"), lax.axis_size("z"), lax.axis_size("xl")
    me = jnp.stack([lax.axis_index(a) for a in ("xh", "core", "xl")]).astype(jnp.int32)
    stored, query, fisher = stored[:, 0], query[:, 0], fisher[0]
    n, f = stored.shape
    q, w = query.shape
    qs = q // PARTS

    feats = [spread(query[h * qs : (h + 1) * qs], "y") for h in range(PARTS)]

    near, far = pack(me, fisher, ny, w)
    fish = [near[0], swap(far[0], "core"), swap(near[1], "xh"), swap(far[1], "xh", "core")]

    near, far = pack(me, stored, ny, w)
    came = swap(far, "core")
    same, cross = (jnp.stack([near[dx], came[dx]]) for dx in range(2))
    rows = [same, swap(same, "xl"), swap(cross, "xh"), swap(cross, "xh", "xl")]

    precond = []
    for h in range(PARTS):
        own, other = fold(feats[h], fish)
        both = own + swap(other, "core")
        precond.append(spread((both[0] + swap(both[1], "xh")).astype(BF16), "y"))
    scores = []
    for h in range(PARTS):
        own, other = score(precond[h], rows)
        scores.append(meet(me, own, swap(other, "core")))
    scores = scores[0] if PARTS == 1 else jnp.concatenate(scores, axis=2)
    scores = scores.reshape(2 * nl * nz, n // nz, q)
    scores = lax.all_to_all(scores, ("xh", "xl", "z"), 0, 0, tiled=True)
    scores = jnp.sum(scores.reshape(2, nl, nz, n // nz, q).astype(F32), axis=(0, 2))
    factor = 1.0 / math.sqrt(nz * f)
    total = (scores.transpose(1, 0, 2).reshape(n // nz, nl * q) * factor).astype(BF16)
    return spread(total, "z").reshape(n, nl * q).astype(F32)


def solution(mesh):
    dp, layers, queries = mesh.devices.shape
    fine = Mesh(mesh.devices.reshape(2, dp // 4, 2, layers, queries), ("xh", "y", "core", "z", "xl"))
    dp = ("xh", "y", "core")
    placed = (P((*dp, "xl"), "z", None), P("xl", "z", dp), P("z", dp, None))
    return jax.shard_map(
        shards, mesh=fine, in_specs=placed, out_specs=P((*dp, "xl"), None), check_vma=False
    )
```

time: 320 us -> 151 us (0.47)
  waiting for transfers between devices: 288 us -> 54 us
  starting transfers between devices: 0.08 us -> 39.2 us
  blocking collectives: 6.44 us -> 43.8 us
  between operations: 13.1 us -> 0.22 us
  matrix products: 10.3 us -> 0 us
  Pallas kernels: 0 us -> 6.55 us
    all_gather x2 -> x0, waiting for transfers between devices: 209 us -> none  [the longest x1 111 us: score_rows(): lax.all_gather(precond, 'dp', axis=2, tiled=True)]
    psum x1 -> x0, waiting for transfers between devices: 78 us -> none  [shards(): totals = lax.psum(partial_scores, 'layer')]
    all_to_all x0 -> x2, blocking collectives: none -> 43.8 us  [the longest x1 28.5 us: shards(): scores = lax.all_to_all(scores, ('xh', 'xl', 'z'), 0, 0, tiled=True)]
    ppermute x0 -> x10, waiting for transfers between devices: none -> 41.7 us  [swap(): return lax.ppermute(x, axes, [(i, n - 1 - i) for i in range(n)])]
    ppermute x0 -> x10, starting transfers between devices: none -> 28.3 us  [swap(): return lax.ppermute(x, axes, [(i, n - 1 - i) for i in range(n)])]
    all_to_all x0 -> x2, waiting for transfers between devices: none -> 12.3 us  [spread(): lax.all_to_all(jnp.broadcast_to(x[None], (n,) + x.shape), axis, 0, 0, til...]
    all_to_all x0 -> x2, starting transfers between devices: none -> 10.9 us  [spread(): lax.all_to_all(jnp.broadcast_to(x[None], (n,) + x.shape), axis, 0, 0, til...]
    dot_general x2 -> x0, matrix products: 10.3 us -> none  [the longest x1 6.51 us: score_rows(): lax.dot_general(stored_rows, lax.all_gather(precond, 'dp', axis=2, tiled=...]
  transfers between devices with their start and end apart: 3 -> 12, of which waited for: 3 -> 9; matrix products, arithmetic and copies ran while one was open for 0% -> 0% of each run, Pallas kernels for 0% -> 1%
where the time goes in v1:
time: 151 us; the launch traced here: 148 us
  waiting for transfers between devices  54 us (36%)
  blocking collectives  43.8 us (29%)
  starting transfers between devices  39.2 us (26%)
  Pallas kernels  6.55 us (4%)
  local copies, waits for them, and re-layouts  3.34 us (2%)
    ppermute x10, waiting for transfers between devices, swap(): return lax.ppermute(x, axes, [(i, n - 1 - i) for i in range(n)])  41.7 us
    all_to_all x1, blocking collectives, shards(): scores = lax.all_to_all(scores, ('xh', 'xl', 'z'), 0, 0, tiled=True)  28.5 us
    ppermute x10, starting transfers between devices, swap(): return lax.ppermute(x, axes, [(i, n - 1 - i) for i in range(n)])  28.3 us
    all_to_all x1, blocking collectives, spread(): lax.all_to_all(jnp.broadcast_to(x[None], (n,) + x.shape), axis, 0, 0, til...  15.3 us
    all_to_all x2, waiting for transfers between devices, spread(): lax.all_to_all(jnp.broadcast_to(x[None], (n,) + x.shape), axis, 0, 0, til...  12.3 us
    all_to_all x2, starting transfers between devices, spread(): lax.all_to_all(jnp.broadcast_to(x[None], (n,) + x.shape), axis, 0, 0, til...  10.9 us
    pallas_call x5, Pallas kernels, call(): pl.pallas_call(body, out_shape=[jax.ShapeDtypeStruct(s.shape, s.dtype) fo...  6.55 us
    broadcast_in_dim x3, local copies, waits for them, and re-layouts, spread(): jnp.broadcast_to(x[None], (n,) + x.shape)  3.17 us
  transfers between devices with their start and end apart: 12, of which 9 were waited for; matrix products, arithmetic and copies ran while one was open for 0% of the time, Pallas kernels for 1%

profile of v1, /device:TPU:6, one launch (start us, length us, event | category | flops | bytes accessed | tf_op | source)
XLA Modules:
  0.0 148.3 jit_solution(6487467213108039580)
XLA Ops:
  0.0 2.0 %broadcast_in_dim.9 = bf16[8,512,128]{2,1,0:T(8,128)(2,1)} broadcast(bf16[512,128]{1,0:T(8,128)(2,1)} %bitcast.36), dimensions={1,2} | broadcast | bytes 1179648 | tf_op jit(solution)/shard_map/broadcast_in_dim | solution.py:111
  2.0 0.0 copy-start
  2.0 7.2 %all-to-all-start = ((bf16[8,512,128]{2,1,0:T(8,128)(2,1)}), bf16[8,512,128]{2,1,0:T(8,128)(2,1)S(1)}, u32[]{:S(2)}, u32[]{:S(2)}) async-start(bf16[8,512,128]{2,1,0:T(8,128)(2,1)} %broadcast_in_dim.9), calls=%async_computation | async-start | bytes 2097152 | tf_op jit(solution)/shard_map/all_to_all | solution.py:111
  9.3 0.1 pad_add_fusion.me
  9.3 0.0 copy-done
  9.3 0.8 shard_map.37
  10.2 3.3 %collective-permute-start.1 = (bf16[128,1024]{1,0:T(8,128)(2,1)S(1)}, bf16[128,1024]{1,0:T(8,128)(2,1)S(1)}, u32[]{:S(2)}, u32[]{:S(2)}) collective-permute-start(bf16[128,1024]{1,0:T(8,128)(2,1)S(1)} %get-tuple-element.27), channel_id=1, source_target_pairs={{0,256},{256,0},{1,257},{257,1},{2,258},{258,2},{3,259},{259,3},{4... | collective-permute-start | bytes 786440 | tf_op jit(solution)/shard_map/ppermute | solution.py:106
  13.6 2.9 %collective-permute-start.2 = (bf16[128,1024]{1,0:T(8,128)(2,1)S(1)}, bf16[128,1024]{1,0:T(8,128)(2,1)S(1)}, u32[]{:S(2)}, u32[]{:S(2)}) collective-permute-start(bf16[128,1024]{1,0:T(8,128)(2,1)S(1)} %get-tuple-element.25), channel_id=1, source_target_pairs={{0,272},{16,256},{256,16},{272,0},{1,273},{17,257},{257,17},{273,1... | collective-permute-start | bytes 786440 | tf_op jit(solution)/shard_map/ppermute | solution.py:106
  16.5 3.1 %collective-permute-start = (bf16[128,1024]{1,0:T(8,128)(2,1)S(1)}, bf16[128,1024]{1,0:T(8,128)(2,1)S(1)}, u32[]{:S(2)}, u32[]{:S(2)}) collective-permute-start(bf16[128,1024]{1,0:T(8,128)(2,1)S(1)} %get-tuple-element.26), channel_id=1, source_target_pairs={{0,16},{16,0},{1,17},{17,1},{2,18},{18,2},{3,19},{19,3},{4,20},{20... | collective-permute-start | bytes 786440 | tf_op jit(solution)/shard_map/ppermute | solution.py:106
  19.7 3.1 %collective-permute-done.1.f10 = bf16[128,1024]{1,0:T(8,128)(2,1)S(1)} collective-permute-done((bf16[128,1024]{1,0:T(8,128)(2,1)S(1)}, bf16[128,1024]{1,0:T(8,128)(2,1)S(1)}, u32[]{:S(2)}, u32[]{:S(2)}) %collective-permute-start.1) | collective-permute-done | bytes 262176 | tf_op jit(solution)/shard_map/ppermute | solution.py:106
  22.7 2.9 %collective-permute-done.2.f11 = bf16[128,1024]{1,0:T(8,128)(2,1)S(1)} collective-permute-done((bf16[128,1024]{1,0:T(8,128)(2,1)S(1)}, bf16[128,1024]{1,0:T(8,128)(2,1)S(1)}, u32[]{:S(2)}, u32[]{:S(2)}) %collective-permute-start.2) | collective-permute-done | bytes 262176 | tf_op jit(solution)/shard_map/ppermute | solution.py:106
  25.6 0.0 collective-permute-done.f01
  25.6 12.3 %all-to-all-done.feats = bf16[8,512,128]{2,1,0:T(8,128)(2,1)S(1)} async-done(((bf16[8,512,128]{2,1,0:T(8,128)(2,1)}), bf16[8,512,128]{2,1,0:T(8,128)(2,1)S(1)}, u32[]{:S(2)}, u32[]{:S(2)}) %all-to-all-start) | async-done | bytes 1048608 | tf_op jit(solution)/shard_map/all_to_all | solution.py:111
  38.0 1.3 shard_map.38
  39.3 1.9 %collective-permute-start.3 = (f32[2,512,128]{2,1,0:T(8,128)S(1)}, f32[2,512,128]{2,1,0:T(8,128)S(1)}, u32[]{:S(2)}, u32[]{:S(2)}) collective-permute-start(f32[2,512,128]{2,1,0:T(8,128)S(1)} %get-tuple-element.16), channel_id=1, source_target_pairs={{0,16},{16,0},{1,17},{17,1},{2,18},{18,2},{3,19},{19,3},{4,20},{20... | collective-permute-start | bytes 1572872 | tf_op jit(solution)/shard_map/ppermute | solution.py:106
  41.2 1.9 %collective-permute-done.3 = f32[2,512,128]{2,1,0:T(8,128)S(1)} collective-permute-done((f32[2,512,128]{2,1,0:T(8,128)S(1)}, f32[2,512,128]{2,1,0:T(8,128)S(1)}, u32[]{:S(2)}, u32[]{:S(2)}) %collective-permute-start.3) | collective-permute-done | bytes 524320 | tf_op jit(solution)/shard_map/ppermute | solution.py:106
  43.1 0.1 add.6
  43.2 3.3 %collective-permute-start.4 = (f32[512,128]{1,0:T(8,128)S(1)}, f32[512,128]{1,0:T(8,128)S(1)}, u32[]{:S(2)}, u32[]{:S(2)}) collective-permute-start(f32[512,128]{1,0:T(8,128)S(1)} %slice_bitcast_fusion), channel_id=1, source_target_pairs={{0,256},{256,0},{1,257},{257,1},{2,258},{258,2},{3,259},{259,3},{4... | collective-permute-start | bytes 786440 | tf_op jit(solution)/shard_map/ppermute | solution.py:106
  46.5 8.4 %collective-permute-done.4 = f32[512,128]{1,0:T(8,128)S(1)} collective-permute-done((f32[512,128]{1,0:T(8,128)S(1)}, f32[512,128]{1,0:T(8,128)S(1)}, u32[]{:S(2)}, u32[]{:S(2)}) %collective-permute-start.4) | collective-permute-done | bytes 262176 | tf_op jit(solution)/shard_map/ppermute | solution.py:106
  54.9 1.1 broadcast_in_dim.10
  56.1 0.0 copy-start.1
  56.1 3.7 %all-to-all-start.1 = ((bf16[8,512,128]{2,1,0:T(8,128)(2,1)}), bf16[8,512,128]{2,1,0:T(8,128)(2,1)S(1)}, u32[]{:S(2)}, u32[]{:S(2)}) async-start(bf16[8,512,128]{2,1,0:T(8,128)(2,1)} %broadcast_in_dim.10), calls=%async_computation.1 | async-start | bytes 2097152 | tf_op jit(solution)/shard_map/all_to_all | solution.py:111
  59.8 0.0 copy-done.1
  59.8 0.8 shard_map.39
  60.6 1.9 %collective-permute-start.5 = (bf16[2,128,1024]{2,1,0:T(8,128)(2,1)S(1)}, bf16[2,128,1024]{2,1,0:T(8,128)(2,1)S(1)}, u32[]{:S(2)}, u32[]{:S(2)}) collective-permute-start(bf16[2,128,1024]{2,1,0:T(8,128)(2,1)S(1)} %get-tuple-element.18), channel_id=1, source_target_pairs={{0,16},{16,0},{1,17},{17,1},{2,18},{18,2},{3,19},{19,3},{4,20},{20... | collective-permute-start | bytes 1572872 | tf_op jit(solution)/shard_map/ppermute | solution.py:106
  62.6 1.8 %collective-permute-done.5 = bf16[2,128,1024]{2,1,0:T(8,128)(2,1)S(1)} collective-permute-done((bf16[2,128,1024]{2,1,0:T(8,128)(2,1)S(1)}, bf16[2,128,1024]{2,1,0:T(8,128)(2,1)S(1)}, u32[]{:S(2)}, u32[]{:S(2)}) %collective-permute-start.5) | collective-permute-done | bytes 524320 | tf_op jit(solution)/shard_map/ppermute | solution.py:106
  64.4 0.1 pad_maximum_fusion.refs_0_
  64.5 2.7 %collective-permute-start.6 = (bf16[2,128,1024]{2,1,0:T(8,128)(2,1)S(1)}, bf16[2,128,1024]{2,1,0:T(8,128)(2,1)S(1)}, u32[]{:S(2)}, u32[]{:S(2)}) collective-permute-start(bf16[2,128,1024]{2,1,0:T(8,128)(2,1)S(1)} %pad_maximum_fusion.refs_0_), channel_id=1, source_target_pairs={{0,1},{1,0},{2,3},{3,2},{4,5},{5,4},{6,7},{7,6},{8,9},{9,8},{10,11... | collective-permute-start | bytes 1572872 | tf_op jit(solution)/shard_map/ppermute | solution.py:106
  67.2 0.1 pad_maximum_fusion.1
  67.3 3.0 %collective-permute-start.8 = (bf16[2,128,1024]{2,1,0:T(8,128)(2,1)S(1)}, bf16[2,128,1024]{2,1,0:T(8,128)(2,1)S(1)}, u32[]{:S(2)}, u32[]{:S(2)}) collective-permute-start(bf16[2,128,1024]{2,1,0:T(8,128)(2,1)S(1)} %pad_maximum_fusion.1), channel_id=1, source_target_pairs={{0,257},{1,256},{256,1},{257,0},{2,259},{3,258},{258,3},{259,2},{4... | collective-permute-start | bytes 1572872 | tf_op jit(solution)/shard_map/ppermute | solution.py:106
  70.4 4.0 %collective-permute-start.7 = (bf16[2,128,1024]{2,1,0:T(8,128)(2,1)S(1)}, bf16[2,128,1024]{2,1,0:T(8,128)(2,1)S(1)}, u32[]{:S(2)}, u32[]{:S(2)}) collective-permute-start(bf16[2,128,1024]{2,1,0:T(8,128)(2,1)S(1)} %pad_maximum_fusion.1), channel_id=1, source_target_pairs={{0,256},{256,0},{1,257},{257,1},{2,258},{258,2},{3,259},{259,3},{4... | collective-permute-start | bytes 1572872 | tf_op jit(solution)/shard_map/ppermute | solution.py:106
  74.4 6.8 %collective-permute-done.6.refs_1_ = bf16[2,128,1024]{2,1,0:T(8,128)(2,1)S(1)} collective-permute-done((bf16[2,128,1024]{2,1,0:T(8,128)(2,1)S(1)}, bf16[2,128,1024]{2,1,0:T(8,128)(2,1)S(1)}, u32[]{:S(2)}, u32[]{:S(2)}) %collective-permute-start.6) | collective-permute-done | bytes 524320 | tf_op jit(solution)/shard_map/ppermute | solution.py:106
  81.2 14.2 %collective-permute-done.8.refs_3_ = bf16[2,128,1024]{2,1,0:T(8,128)(2,1)S(1)} collective-permute-done((bf16[2,128,1024]{2,1,0:T(8,128)(2,1)S(1)}, bf16[2,128,1024]{2,1,0:T(8,128)(2,1)S(1)}, u32[]{:S(2)}, u32[]{:S(2)}) %collective-permute-start.8) | collective-permute-done | bytes 524320 | tf_op jit(solution)/shard_map/ppermute | solution.py:106
  95.3 0.0 collective-permute-done.7.refs_2_
  95.3 0.0 all-to-all-done.1.precond
  95.3 2.9 %shard_map.40 = (f32[4,128,512]{2,1,0:T(8,128)S(1)}, f32[4,128,512]{2,1,0:T(8,128)S(1)}) custom-call(bf16[8,512,128]{2,1,0:T(8,128)(2,1)S(1)} %all-to-all-done.1.precond, bf16[2,128,1024]{2,1,0:T(8,128)(2,1)S(1)} %pad_maximum_fusion.refs_0_, bf16[2,128,1024]{2,1,0:T(8,128)(2,1)S(1)} %collective-permute-done.6.refs_1_, ...), custom_call_target="tpu_custom_call" | custom-call | flops 1073741824 | bytes 5242880 | tf_op jit(solution)/shard_map/pallas_call | solution.py:22
  98.2 1.9 %collective-permute-start.9 = (f32[4,128,512]{2,1,0:T(8,128)S(1)}, f32[4,128,512]{2,1,0:T(8,128)S(1)}, u32[]{:S(2)}, u32[]{:S(2)}) collective-permute-start(f32[4,128,512]{2,1,0:T(8,128)S(1)} %get-tuple-element.20), channel_id=1, source_target_pairs={{0,16},{16,0},{1,17},{17,1},{2,18},{18,2},{3,19},{19,3},{4,20},{20... | collective-permute-start | bytes 3145736 | tf_op jit(solution)/shard_map/ppermute | solution.py:106
  100.2 2.6 %collective-permute-done.9.came = f32[4,128,512]{2,1,0:T(8,128)S(1)} collective-permute-done((f32[4,128,512]{2,1,0:T(8,128)S(1)}, f32[4,128,512]{2,1,0:T(8,128)S(1)}, u32[]{:S(2)}, u32[]{:S(2)}) %collective-permute-start.9) | collective-permute-done | bytes 1048608 | tf_op jit(solution)/shard_map/ppermute | solution.py:106
  102.8 0.7 shard_map.41
  103.5 28.5 %all_to_all.20 = bf16[32,16,512]{2,1,0:T(8,128)(2,1)S(1)} all-to-all(bf16[32,16,512]{2,1,0:T(8,128)(2,1)S(1)} %bitcast.32), channel_id=1, replica_groups=mesh['xh'=2,'y'=8,'core'=2,'z'=8,'xl'=2] {'xh','xl','z'}, dimensions={0} | all-to-all | bytes 1048576 | tf_op jit(solution)/shard_map/all_to_all | solution.py:143
  132.0 0.1 convert_reduce_fusion
  132.1 15.3 %all_to_all.21 = bf16[8,16,1024]{2,1,0:T(8,128)(2,1)S(1)} all-to-all(bf16[8,16,1024]{2,1,0:T(8,128)(2,1)S(1)} %broadcast_in_dim.22), channel_id=1, replica_groups=mesh['xh'=2,'y'=8,'core'=2,'z'=8,'xl'=2] {'z'}, dimensions={0} | all-to-all | bytes 524288 | tf_op jit(solution)/shard_map/all_to_all | solution.py:111
  147.5 0.9 bitcast_convert_fusion
  (9 shorter events, 0.2 us)
Async XLA Ops:
  2.0 7.3 %copy-start = (bf16[1,128,4096]{2,1,0:T(8,128)(2,1)S(1)}, bf16[1,128,4096]{2,1,0:T(8,128)(2,1)}, u32[]{:S(2)}) copy-start(bf16[1,128,4096]{2,1,0:T(8,128)(2,1)} %param.5) | copy-start | bytes 3145732
  2.0 36.0 %all-to-all-start = ((bf16[8,512,128]{2,1,0:T(8,128)(2,1)}), bf16[8,512,128]{2,1,0:T(8,128)(2,1)S(1)}, u32[]{:S(2)}, u32[]{:S(2)}) async-start(bf16[8,512,128]{2,1,0:T(8,128)(2,1)} %broadcast_in_dim.9), calls=%async_computation | async-start | bytes 2097152 | tf_op jit(solution)/shard_map/all_to_all | solution.py:111
  10.2 12.5 %collective-permute-start.1 = (bf16[128,1024]{1,0:T(8,128)(2,1)S(1)}, bf16[128,1024]{1,0:T(8,128)(2,1)S(1)}, u32[]{:S(2)}, u32[]{:S(2)}) collective-permute-start(bf16[128,1024]{1,0:T(8,128)(2,1)S(1)} %get-tuple-element.27), channel_id=1, source_target_pairs={{0,256},{256,0},{1,257},{257,1},{2,258},{258,2},{3,259},{259,3},{4... | collective-permute-start | bytes 786440 | tf_op jit(solution)/shard_map/ppermute | solution.py:106
  13.6 12.1 %collective-permute-start.2 = (bf16[128,1024]{1,0:T(8,128)(2,1)S(1)}, bf16[128,1024]{1,0:T(8,128)(2,1)S(1)}, u32[]{:S(2)}, u32[]{:S(2)}) collective-permute-start(bf16[128,1024]{1,0:T(8,128)(2,1)S(1)} %get-tuple-element.25), channel_id=1, source_target_pairs={{0,272},{16,256},{256,16},{272,0},{1,273},{17,257},{257,17},{273,1... | collective-permute-start | bytes 786440 | tf_op jit(solution)/shard_map/ppermute | solution.py:106
  16.5 9.1 %collective-permute-start = (bf16[128,1024]{1,0:T(8,128)(2,1)S(1)}, bf16[128,1024]{1,0:T(8,128)(2,1)S(1)}, u32[]{:S(2)}, u32[]{:S(2)}) collective-permute-start(bf16[128,1024]{1,0:T(8,128)(2,1)S(1)} %get-tuple-element.26), channel_id=1, source_target_pairs={{0,16},{16,0},{1,17},{17,1},{2,18},{18,2},{3,19},{19,3},{4,20},{20... | collective-permute-start | bytes 786440 | tf_op jit(solution)/shard_map/ppermute | solution.py:106
  39.3 3.8 %collective-permute-start.3 = (f32[2,512,128]{2,1,0:T(8,128)S(1)}, f32[2,512,128]{2,1,0:T(8,128)S(1)}, u32[]{:S(2)}, u32[]{:S(2)}) collective-permute-start(f32[2,512,128]{2,1,0:T(8,128)S(1)} %get-tuple-element.16), channel_id=1, source_target_pairs={{0,16},{16,0},{1,17},{17,1},{2,18},{18,2},{3,19},{19,3},{4,20},{20... | collective-permute-start | bytes 1572872 | tf_op jit(solution)/shard_map/ppermute | solution.py:106
  43.2 11.7 %collective-permute-start.4 = (f32[512,128]{1,0:T(8,128)S(1)}, f32[512,128]{1,0:T(8,128)S(1)}, u32[]{:S(2)}, u32[]{:S(2)}) collective-permute-start(f32[512,128]{1,0:T(8,128)S(1)} %slice_bitcast_fusion), channel_id=1, source_target_pairs={{0,256},{256,0},{1,257},{257,1},{2,258},{258,2},{3,259},{259,3},{4... | collective-permute-start | bytes 786440 | tf_op jit(solution)/shard_map/ppermute | solution.py:106
  56.1 3.7 %copy-start.1 = (bf16[128,1,4096]{2,0,1:T(8,128)(2,1)S(1)}, bf16[128,1,4096]{2,0,1:T(8,128)(2,1)}, u32[]{:S(2)}) copy-start(bf16[128,1,4096]{2,0,1:T(8,128)(2,1)} %param.3) | copy-start | bytes 3145732
  56.1 39.3 %all-to-all-start.1 = ((bf16[8,512,128]{2,1,0:T(8,128)(2,1)}), bf16[8,512,128]{2,1,0:T(8,128)(2,1)S(1)}, u32[]{:S(2)}, u32[]{:S(2)}) async-start(bf16[8,512,128]{2,1,0:T(8,128)(2,1)} %broadcast_in_dim.10), calls=%async_computation.1 | async-start | bytes 2097152 | tf_op jit(solution)/shard_map/all_to_all | solution.py:111
  60.6 3.8 %collective-permute-start.5 = (bf16[2,128,1024]{2,1,0:T(8,128)(2,1)S(1)}, bf16[2,128,1024]{2,1,0:T(8,128)(2,1)S(1)}, u32[]{:S(2)}, u32[]{:S(2)}) collective-permute-start(bf16[2,128,1024]{2,1,0:T(8,128)(2,1)S(1)} %get-tuple-element.18), channel_id=1, source_target_pairs={{0,16},{16,0},{1,17},{17,1},{2,18},{18,2},{3,19},{19,3},{4,20},{20... | collective-permute-start | bytes 1572872 | tf_op jit(solution)/shard_map/ppermute | solution.py:106
  64.5 16.7 %collective-permute-start.6 = (bf16[2,128,1024]{2,1,0:T(8,128)(2,1)S(1)}, bf16[2,128,1024]{2,1,0:T(8,128)(2,1)S(1)}, u32[]{:S(2)}, u32[]{:S(2)}) collective-permute-start(bf16[2,128,1024]{2,1,0:T(8,128)(2,1)S(1)} %pad_maximum_fusion.refs_0_), channel_id=1, source_target_pairs={{0,1},{1,0},{2,3},{3,2},{4,5},{5,4},{6,7},{7,6},{8,9},{9,8},{10,11... | collective-permute-start | bytes 1572872 | tf_op jit(solution)/shard_map/ppermute | solution.py:106
  67.3 28.0 %collective-permute-start.8 = (bf16[2,128,1024]{2,1,0:T(8,128)(2,1)S(1)}, bf16[2,128,1024]{2,1,0:T(8,128)(2,1)S(1)}, u32[]{:S(2)}, u32[]{:S(2)}) collective-permute-start(bf16[2,128,1024]{2,1,0:T(8,128)(2,1)S(1)} %pad_maximum_fusion.1), channel_id=1, source_target_pairs={{0,257},{1,256},{256,1},{257,0},{2,259},{3,258},{258,3},{259,2},{4... | collective-permute-start | bytes 1572872 | tf_op jit(solution)/shard_map/ppermute | solution.py:106
  70.4 25.0 %collective-permute-start.7 = (bf16[2,128,1024]{2,1,0:T(8,128)(2,1)S(1)}, bf16[2,128,1024]{2,1,0:T(8,128)(2,1)S(1)}, u32[]{:S(2)}, u32[]{:S(2)}) collective-permute-start(bf16[2,128,1024]{2,1,0:T(8,128)(2,1)S(1)} %pad_maximum_fusion.1), channel_id=1, source_target_pairs={{0,256},{256,0},{1,257},{257,1},{2,258},{258,2},{3,259},{259,3},{4... | collective-permute-start | bytes 1572872 | tf_op jit(solution)/shard_map/ppermute | solution.py:106
  98.2 4.6 %collective-permute-start.9 = (f32[4,128,512]{2,1,0:T(8,128)S(1)}, f32[4,128,512]{2,1,0:T(8,128)S(1)}, u32[]{:S(2)}, u32[]{:S(2)}) collective-permute-start(f32[4,128,512]{2,1,0:T(8,128)S(1)} %get-tuple-element.20), channel_id=1, source_target_pairs={{0,16},{16,0},{1,17},{17,1},{2,18},{18,2},{3,19},{19,3},{4,20},{20... | collective-permute-start | bytes 3145736 | tf_op jit(solution)/shard_map/ppermute | solution.py:106

commit v2 on v1

v2 whole, which is shorter than its diff:
```python
import functools
import math

import jax
import jax.numpy as jnp
from jax import lax
from jax.experimental import pallas as pl
from jax.experimental.pallas import tpu as pltpu
from jax.sharding import Mesh, PartitionSpec as P

F32 = jnp.float32
BF16 = jnp.bfloat16
PARTS = 2
NT = (((1,), (1,)), ((), ()))
PARAMS = pltpu.CompilerParams(vmem_limit_bytes=16 * 1024 * 1024)
WHOLE = pl.BlockSpec(memory_space=pltpu.VMEM)
ANYWHERE = pl.BlockSpec(memory_space=pl.ANY)
SCALARS = pl.BlockSpec(memory_space=pltpu.SMEM)


def call(body, out_shape, inputs, scratch=(), flops=0, after=()):
    if after:
        inner, k = body, len(after)
        body = lambda *refs: inner(*refs[k:])
    size = sum(math.prod(x.shape) * x.dtype.itemsize for x in (*inputs, *out_shape))
    return pl.pallas_call(
        body,
        out_shape=[jax.ShapeDtypeStruct(s.shape, s.dtype) for s in out_shape],
        in_specs=[ANYWHERE] * len(after) + [SCALARS if x.dtype == jnp.int32 else WHOLE for x in inputs],
        out_specs=[WHOLE] * len(out_shape),
        scratch_shapes=scratch,
        compiler_params=PARAMS,
        cost_estimate=pl.CostEstimate(flops=flops, bytes_accessed=size, transcendentals=0),
    )(*after, *inputs)


def like(*shape, dtype=BF16):
    return jax.ShapeDtypeStruct(shape, dtype)


def pack_body(ny, w, me, fisher, stored, f00, f01, f10, f11, own, other):
    for x, outs in ((fisher, ((f00, f10), (f01, f11))), (stored, ([own.at[0], own.at[1]], [other.at[0], other.at[1]]))):
        for dc in range(2):
            for dx in range(2):
                for y in range(ny):
                    first = (((me[0] ^ dx) * ny + y) * 2 + (me[1] ^ dc)) * w
                    outs[dc][dx][:, y * w : (y + 1) * w] = x[:, pl.ds(pl.multiple_of(first, w), w)]


def pack(me, fisher, stored, ny, w):
    n, g = stored.shape[0], fisher.shape[0]
    shapes = [like(g, ny * w)] * 4 + [like(2, n, ny * w)] * 2
    return call(functools.partial(pack_body, ny, w), shapes, [me, fisher, stored])


def pair_body(near, came, same, cross):
    for dx, out in enumerate((same, cross)):
        out[0], out[1] = near[dx], came[dx]


def pair(near, came):
    return call(pair_body, [like(*near.shape)] * 2, [near, came])


def copies_body(x, out):
    for i in range(out.shape[0]):
        out[i] = x[...]


def copies(x, n, after=()):
    return call(copies_body, [like(n, *x.shape)], [x], after=after)[0]


def settle_body(own, came, last, out):
    done = (own[...] + came[0] + last[...]).astype(BF16)
    for i in range(out.shape[0]):
        out[i] = done


def settle(own, came, last, n, after=()):
    return call(settle_body, [like(n, *own.shape)], [own, came, last], after=after)[0]


def fold_body(feats, f00, f01, f10, f11, own, own_x, other, held):
    ny, _, w = feats.shape
    for y in range(ny):
        held[:, y * w : (y + 1) * w] = feats[y]

    def dot(block):
        return lax.dot_general(held[...], block[...], NT, preferred_element_type=F32)

    other[0], other[1] = dot(f01), dot(f11)
    own[...], own_x[...] = dot(f00), dot(f10)


def fold(feats, blocks, after=()):
    ny, q, w = feats.shape
    return call(
        fold_body,
        [like(q, w, dtype=F32), like(q, w, dtype=F32), like(2, q, w, dtype=F32)],
        [feats, *blocks],
        [pltpu.VMEM((q, ny * w), BF16)],
        flops=2 * q * ny * w * 4 * w,
        after=after,
    )


def score_body(precond, *refs):
    blocks, (own, other, held) = refs[:-3], refs[-3:]
    ny, _, w = precond.shape
    for y in range(ny):
        held[:, y * w : (y + 1) * w] = precond[y]
    for i in range(4):
        for dc, out in enumerate((own, other)):
            out[i] = lax.dot_general(blocks[i][dc], held[...], NT, preferred_element_type=F32)


def score(precond, blocks):
    ny, q, w = precond.shape
    n = blocks[0].shape[1]
    return call(
        score_body,
        [like(4, n, q, dtype=F32)] * 2,
        [precond, *blocks],
        [pltpu.VMEM((q, ny * w), BF16)],
        flops=2 * q * ny * w * 8 * n,
    )


def meet_body(me, *refs):
    terms, out = refs[:-1], refs[-1]
    for h in range(len(terms) // 2):
        own, came = terms[2 * h : 2 * h + 2]
        q = own.shape[2]
        for x in range(2):
            for l in range(2):
                i = (x ^ me[0]) * 2 + (l ^ me[2])
                out[x * 2 + l, :, h * q : (h + 1) * q] = (own[i] + came[i]).astype(BF16)


def meet(me, terms):
    k, n, q = terms[0].shape
    return call(meet_body, [like(k, n, q * (len(terms) // 2))], [me, *terms])[0]


def finish_body(factor, scores, out):
    nx, nl, nz, rows, q = scores.shape
    for l in range(nl):
        total = jnp.zeros((rows, q), F32)
        for x in range(nx):
            for z in range(nz):
                total += scores[x, l, z].astype(F32)
        total = (total * factor).astype(BF16)
        for z in range(nz):
            out[z, :, l * q : (l + 1) * q] = total


def finish(scores, factor):
    _, nl, nz, rows, q = scores.shape
    return call(functools.partial(finish_body, factor), [like(nz, rows, nl * q)], [scores])[0]


def swap(x, *axes):
    sizes = [lax.axis_size(a) for a in axes]
    n = math.prod(sizes)
    return lax.ppermute(x, axes, [(i, n - 1 - i) for i in range(n)])


def trade(x, *axes):
    return lax.all_to_all(x, axes, 0, 0, tiled=True)


def shards(stored, query, fisher):
    ny, nz, nl = lax.axis_size("y"), lax.axis_size("z"), lax.axis_size("xl")
    me = jnp.stack([lax.axis_index(a) for a in ("xh", "core", "xl")]).astype(jnp.int32)
    stored, query, fisher = stored[:, 0], query[:, 0], fisher[0]
    n, f = stored.shape
    q, w = query.shape

    f00, f01, f10, f11, near, far = pack(me, fisher, stored, ny, w)
    fish = [f00, swap(f01, "core"), swap(f10, "xh"), swap(f11, "xh", "core")]
    same, cross = pair(near, swap(far, "core"))
    rows = [same, swap(same, "xl"), swap(cross, "xh"), swap(cross, "xh", "xl")]

    before_gather = ((), fish[1:])
    before_fold = ((same,), (rows[1],))
    before_settle = ((), (rows[2], rows[3]))
    half = q // PARTS
    feats = [
        trade(copies(query[h * half : (h + 1) * half], ny, before_gather[h]), "y") for h in range(PARTS)
    ]
    precond = []
    for h in range(PARTS):
        own, own_x, other = fold(feats[h], fish, before_fold[h])
        came = swap(other, "core")
        full = settle(own, came, swap(own_x + came[1], "xh"), ny, before_settle[h])
        precond.append(trade(full, "y"))
    terms = []
    for h in range(PARTS):
        own, other = score(precond[h], rows)
        terms += [own, swap(other, "core")]
    scores = trade(meet(me, terms).reshape(2 * nl * nz, n // nz, q), "xh", "xl", "z")
    total = finish(scores.reshape(2, nl, nz, n // nz, q), 1.0 / math.sqrt(nz * f))
    return trade(total, "z").reshape(n, nl * q).astype(F32)


def solution(mesh):
    dp, layers, queries = mesh.devices.shape
    fine = Mesh(mesh.devices.reshape(2, dp // 4, 2, layers, queries), ("xh", "y", "core", "z", "xl"))
    dp = ("xh", "y", "core")
    placed = (P((*dp, "xl"), "z", None), P("xl", "z", dp), P("z", dp, None))
    return jax.shard_map(
        shards, mesh=fine, in_specs=placed, out_specs=P((*dp, "xl"), None), check_vma=False
    )
```

time: 151 us -> 184 us (1.22)
  starting transfers between devices: 39.2 us -> 65.6 us
  Pallas kernels: 6.55 us -> 12 us
  waiting for transfers between devices: 54 us -> 56.4 us
  local copies, waits for them, and re-layouts: 3.34 us -> 5.36 us
    all_to_all x2 -> x4, starting transfers between devices: 10.9 us -> 28.8 us  [trade(): return lax.all_to_all(x, axes, 0, 0, tiled=True)]
    ppermute x10 -> x13, starting transfers between devices: 28.3 us -> 36.7 us  [swap(): return lax.ppermute(x, axes, [(i, n - 1 - i) for i in range(n)])]
    pallas_call x5 -> x12, Pallas kernels: 6.55 us -> 12 us  [call(): pl.pallas_call(body, out_shape=[jax.ShapeDtypeStruct(s.shape, s.dtype) fo...]
    unnamed x4 -> x18, local copies, waits for them, and re-layouts: 0.01 us -> 4.39 us
    broadcast_in_dim x3 -> x0, local copies, waits for them, and re-layouts: 3.17 us -> none  [spread(): jnp.broadcast_to(x[None], (n,) + x.shape)]
    ppermute x10 -> x13, waiting for transfers between devices: 41.7 us -> 44 us  [swap(): return lax.ppermute(x, axes, [(i, n - 1 - i) for i in range(n)])]
    all_to_all x2 -> x4, waiting for transfers between devices: 12.3 us -> 12.4 us  [trade(): return lax.all_to_all(x, axes, 0, 0, tiled=True)]
  transfers between devices with their start and end apart: 12 -> 17, of which waited for: 9 -> 6; matrix products, arithmetic and copies ran while one was open for 0% -> 0% of each run, Pallas kernels for 1% -> 5%
where the time goes in v2:
time: 184 us; the launch traced here: 183 us
  starting transfers between devices  65.6 us (36%)
  waiting for transfers between devices  56.4 us (31%)
  blocking collectives  42.2 us (23%)
  Pallas kernels  12 us (7%)
  local copies, waits for them, and re-layouts  5.36 us (3%)
    ppermute x13, waiting for transfers between devices, swap(): return lax.ppermute(x, axes, [(i, n - 1 - i) for i in range(n)])  44 us
    all_to_all x2, blocking collectives, trade(): return lax.all_to_all(x, axes, 0, 0, tiled=True)  42.2 us
    ppermute x13, starting transfers between devices, swap(): return lax.ppermute(x, axes, [(i, n - 1 - i) for i in range(n)])  36.7 us
    all_to_all x4, starting transfers between devices, trade(): return lax.all_to_all(x, axes, 0, 0, tiled=True)  28.8 us
    all_to_all x4, waiting for transfers between devices, trade(): return lax.all_to_all(x, axes, 0, 0, tiled=True)  12.4 us
    pallas_call x12, Pallas kernels, call(): pl.pallas_call(body, out_shape=[jax.ShapeDtypeStruct(s.shape, s.dtype) fo...  12 us
    unnamed x18, local copies, waits for them, and re-layouts  4.39 us
  transfers between devices with their start and end apart: 17, of which 6 were waited for; matrix products, arithmetic and copies ran while one was open for 0% of the time, Pallas kernels for 5%

profile of v2, /device:TPU:6, one launch (start us, length us, event | category | flops | bytes accessed | tf_op | source)
XLA Modules:
  0.0 182.8 jit_solution(4038414409328582144)
XLA Ops:
  0.0 1.0 slice_bitcast_fusion.2
  1.0 0.9 shard_map.39
  1.8 7.1 %all-to-all-start = ((bf16[8,256,128]{2,1,0:T(8,128)(2,1)}), bf16[8,256,128]{2,1,0:T(8,128)(2,1)S(1)}, u32[]{:S(2)}, u32[]{:S(2)}) async-start(bf16[8,256,128]{2,1,0:T(8,128)(2,1)} %shard_map.39), calls=%async_computation | async-start | bytes 1048576 | tf_op jit(solution)/shard_map/all_to_all | solution.py:170
  8.9 0.1 pad_add_fusion.me
  9.0 1.2 copy-done.2
  10.2 1.9 %shard_map.37 = (bf16[128,1024]{1,0:T(8,128)(2,1)S(1)}, bf16[128,1024]{1,0:T(8,128)(2,1)S(1)}, bf16[128,1024]{1,0:T(8,128)(2,1)S(1)}, bf16[128,1024]{1,0:T(8,128...) custom-call(s32[3]{0:T(128)S(1)} %pad_add_fusion.me, bf16[128,4096]{1,0:T(8,128)(2,1)S(1)} %bitcast.24, ...), custom_call_target="tpu_custom_call" | custom-call | bytes 4194316 | tf_op jit(solution)/shard_map/pallas_call | solution.py:26
  12.1 0.8 copy-done.3
  12.9 1.9 %collective-permute-start.1 = (bf16[128,1024]{1,0:T(8,128)(2,1)S(1)}, bf16[128,1024]{1,0:T(8,128)(2,1)S(1)}, u32[]{:S(2)}, u32[]{:S(2)}) collective-permute-start(bf16[128,1024]{1,0:T(8,128)(2,1)S(1)} %get-tuple-element.27), channel_id=1, source_target_pairs={{0,16},{16,0},{1,17},{17,1},{2,18},{18,2},{3,19},{19,3},{4,20},{20... | collective-permute-start | bytes 786440 | tf_op jit(solution)/shard_map/ppermute | solution.py:166
  14.8 3.3 %collective-permute-start.2 = (bf16[128,1024]{1,0:T(8,128)(2,1)S(1)}, bf16[128,1024]{1,0:T(8,128)(2,1)S(1)}, u32[]{:S(2)}, u32[]{:S(2)}) collective-permute-start(bf16[128,1024]{1,0:T(8,128)(2,1)S(1)} %get-tuple-element.28), channel_id=1, source_target_pairs={{0,256},{256,0},{1,257},{257,1},{2,258},{258,2},{3,259},{259,3},{4... | collective-permute-start | bytes 786440 | tf_op jit(solution)/shard_map/ppermute | solution.py:166
  18.2 3.9 %collective-permute-start.3 = (bf16[128,1024]{1,0:T(8,128)(2,1)S(1)}, bf16[128,1024]{1,0:T(8,128)(2,1)S(1)}, u32[]{:S(2)}, u32[]{:S(2)}) collective-permute-start(bf16[128,1024]{1,0:T(8,128)(2,1)S(1)} %get-tuple-element.29), channel_id=1, source_target_pairs={{0,272},{16,256},{256,16},{272,0},{1,273},{17,257},{257,17},{273,1... | collective-permute-start | bytes 786440 | tf_op jit(solution)/shard_map/ppermute | solution.py:166
  22.0 2.2 %collective-permute-start = (bf16[2,128,1024]{2,1,0:T(8,128)(2,1)}, bf16[2,128,1024]{2,1,0:T(8,128)(2,1)}, u32[]{:S(2)}, u32[]{:S(2)}) collective-permute-start(bf16[2,128,1024]{2,1,0:T(8,128)(2,1)} %get-tuple-element.24), channel_id=1, source_target_pairs={{0,16},{16,0},{1,17},{17,1},{2,18},{18,2},{3,19},{19,3},{4,20},{20... | collective-permute-start | bytes 1572872 | tf_op jit(solution)/shard_map/ppermute | solution.py:166
  24.2 3.1 %collective-permute-done.2.refs_4_.refs_1_ = bf16[128,1024]{1,0:T(8,128)(2,1)S(1)} collective-permute-done((bf16[128,1024]{1,0:T(8,128)(2,1)S(1)}, bf16[128,1024]{1,0:T(8,128)(2,1)S(1)}, u32[]{:S(2)}, u32[]{:S(2)}) %collective-permute-start.2) | collective-permute-done | bytes 262176 | tf_op jit(solution)/shard_map/ppermute | solution.py:166
  27.3 4.8 %collective-permute-done.3.refs_5_.refs_2_ = bf16[128,1024]{1,0:T(8,128)(2,1)S(1)} collective-permute-done((bf16[128,1024]{1,0:T(8,128)(2,1)S(1)}, bf16[128,1024]{1,0:T(8,128)(2,1)S(1)}, u32[]{:S(2)}, u32[]{:S(2)}) %collective-permute-start.3) | collective-permute-done | bytes 262176 | tf_op jit(solution)/shard_map/ppermute | solution.py:166
  32.2 0.9 shard_map.43
  33.1 7.3 %all-to-all-start.2 = ((bf16[8,256,128]{2,1,0:T(8,128)(2,1)}), bf16[8,256,128]{2,1,0:T(8,128)(2,1)S(1)}, u32[]{:S(2)}, u32[]{:S(2)}) async-start(bf16[8,256,128]{2,1,0:T(8,128)(2,1)} %shard_map.43), calls=%async_computation.2 | async-start | bytes 1048576 | tf_op jit(solution)/shard_map/all_to_all | solution.py:170
  40.4 0.0 collective-permute-done.came
  40.4 1.1 shard_map.38
  41.5 0.8 copy-done.7
  42.3 0.7 shard_map.40
  43.0 1.9 %collective-permute-start.4 = (f32[2,256,128]{2,1,0:T(8,128)S(1)}, f32[2,256,128]{2,1,0:T(8,128)S(1)}, u32[]{:S(2)}, u32[]{:S(2)}) collective-permute-start(f32[2,256,128]{2,1,0:T(8,128)S(1)} %get-tuple-element.31), channel_id=1, source_target_pairs={{0,16},{16,0},{1,17},{17,1},{2,18},{18,2},{3,19},{19,3},{4,20},{20... | collective-permute-start | bytes 786440 | tf_op jit(solution)/shard_map/ppermute | solution.py:166
  45.0 2.7 %collective-permute-start.6 = (bf16[2,128,1024]{2,1,0:T(8,128)(2,1)S(1)}, bf16[2,128,1024]{2,1,0:T(8,128)(2,1)S(1)}, u32[]{:S(2)}, u32[]{:S(2)}) collective-permute-start(bf16[2,128,1024]{2,1,0:T(8,128)(2,1)S(1)} %get-tuple-element.25.refs_0_), channel_id=1, source_target_pairs={{0,1},{1,0},{2,3},{3,2},{4,5},{5,4},{6,7},{7,6},{8,9},{9,8},{10,11... | collective-permute-start | bytes 1572872 | tf_op jit(solution)/shard_map/ppermute | solution.py:166
  47.7 0.0 collective-permute-done.4.came
  47.7 4.7 %collective-permute-start.5 = (f32[256,128]{1,0:T(8,128)S(1)}, f32[256,128]{1,0:T(8,128)S(1)}, u32[]{:S(2)}, u32[]{:S(2)}) collective-permute-start(f32[256,128]{1,0:T(8,128)S(1)} %fusion.1), channel_id=1, source_target_pairs={{0,256},{256,0},{1,257},{257,1},{2,258},{258,2},{3,259},{259,3},{4... | collective-permute-start | bytes 393224 | tf_op jit(solution)/shard_map/ppermute | solution.py:166
  52.5 13.1 %collective-permute-done.5.last = f32[256,128]{1,0:T(8,128)S(1)} collective-permute-done((f32[256,128]{1,0:T(8,128)S(1)}, f32[256,128]{1,0:T(8,128)S(1)}, u32[]{:S(2)}, u32[]{:S(2)}) %collective-permute-start.5) | collective-permute-done | bytes 131104 | tf_op jit(solution)/shard_map/ppermute | solution.py:166
  65.6 0.8 shard_map.41
  66.4 0.0 all-to-all-done.2.refs_1_
  66.4 7.2 %all-to-all-start.1 = ((bf16[8,256,128]{2,1,0:T(8,128)(2,1)}), bf16[8,256,128]{2,1,0:T(8,128)(2,1)S(1)}, u32[]{:S(2)}, u32[]{:S(2)}) async-start(bf16[8,256,128]{2,1,0:T(8,128)(2,1)} %shard_map.41), calls=%async_computation.1 | async-start | bytes 1048576 | tf_op jit(solution)/shard_map/all_to_all | solution.py:170
  73.6 0.0 collective-permute-done.6.refs_1_.refs_0_
  73.6 0.7 shard_map.44
  74.4 1.9 %collective-permute-start.10 = (f32[2,256,128]{2,1,0:T(8,128)S(1)}, f32[2,256,128]{2,1,0:T(8,128)S(1)}, u32[]{:S(2)}, u32[]{:S(2)}) collective-permute-start(f32[2,256,128]{2,1,0:T(8,128)S(1)} %get-tuple-element.37), channel_id=1, source_target_pairs={{0,16},{16,0},{1,17},{17,1},{2,18},{18,2},{3,19},{19,3},{4,20},{20... | collective-permute-start | bytes 786440 | tf_op jit(solution)/shard_map/ppermute | solution.py:166
  76.3 3.0 %collective-permute-start.8 = (bf16[2,128,1024]{2,1,0:T(8,128)(2,1)S(1)}, bf16[2,128,1024]{2,1,0:T(8,128)(2,1)S(1)}, u32[]{:S(2)}, u32[]{:S(2)}) collective-permute-start(bf16[2,128,1024]{2,1,0:T(8,128)(2,1)S(1)} %copy-done.8), channel_id=1, source_target_pairs={{0,257},{1,256},{256,1},{257,0},{2,259},{3,258},{258,3},{259,2},{4... | collective-permute-start | bytes 1572872 | tf_op jit(solution)/shard_map/ppermute | solution.py:166
  79.3 2.6 %collective-permute-start.7 = (bf16[2,128,1024]{2,1,0:T(8,128)(2,1)S(1)}, bf16[2,128,1024]{2,1,0:T(8,128)(2,1)S(1)}, u32[]{:S(2)}, u32[]{:S(2)}) collective-permute-start(bf16[2,128,1024]{2,1,0:T(8,128)(2,1)S(1)} %copy-done.8), channel_id=1, source_target_pairs={{0,256},{256,0},{1,257},{257,1},{2,258},{258,2},{3,259},{259,3},{4... | collective-permute-start | bytes 1572872 | tf_op jit(solution)/shard_map/ppermute | solution.py:166
  81.9 4.8 %collective-permute-start.11 = (f32[256,128]{1,0:T(8,128)S(1)}, f32[256,128]{1,0:T(8,128)S(1)}, u32[]{:S(2)}, u32[]{:S(2)}) collective-permute-start(f32[256,128]{1,0:T(8,128)S(1)} %fusion), channel_id=1, source_target_pairs={{0,256},{256,0},{1,257},{257,1},{2,258},{258,2},{3,259},{259,3},{4... | collective-permute-start | bytes 393224 | tf_op jit(solution)/shard_map/ppermute | solution.py:166
  86.7 21.1 %collective-permute-done.8.refs_3_.refs_1_ = bf16[2,128,1024]{2,1,0:T(8,128)(2,1)S(1)} collective-permute-done((bf16[2,128,1024]{2,1,0:T(8,128)(2,1)S(1)}, bf16[2,128,1024]{2,1,0:T(8,128)(2,1)S(1)}, u32[]{:S(2)}, u32[]{:S(2)}) %collective-permute-start.8) | collective-permute-done | bytes 524320 | tf_op jit(solution)/shard_map/ppermute | solution.py:166
  107.8 0.8 copy-done
  108.6 7.2 %all-to-all-start.3 = ((bf16[8,256,128]{2,1,0:T(8,128)(2,1)}), bf16[8,256,128]{2,1,0:T(8,128)(2,1)S(1)}, u32[]{:S(2)}, u32[]{:S(2)}) async-start(bf16[8,256,128]{2,1,0:T(8,128)(2,1)} %copy-done), calls=%async_computation.3 | async-start | bytes 1048576 | tf_op jit(solution)/shard_map/all_to_all | solution.py:170
  115.8 2.3 %shard_map.42 = (f32[4,128,256]{2,1,0:T(8,128)S(1)}, f32[4,128,256]{2,1,0:T(8,128)}) custom-call(bf16[8,256,128]{2,1,0:T(8,128)(2,1)S(1)} %all-to-all-done.1.precond, bf16[2,128,1024]{2,1,0:T(8,128)(2,1)S(1)} %get-tuple-element.25.refs_0_, bf16[2,128,1024]{2,1,0:T(8,128)(2,1)S(1)} %collective-permute-done.6.refs_1_.refs_0_, ...), custom_call_target="tpu_custom_call" | custom-call | flops 536870912 | bytes 3670016 | tf_op jit(solution)/shard_map/pallas_call | solution.py:26
  118.1 0.8 copy-done.5
  118.9 1.9 %collective-permute-start.9 = (f32[4,128,256]{2,1,0:T(8,128)}, f32[4,128,256]{2,1,0:T(8,128)}, u32[]{:S(2)}, u32[]{:S(2)}) collective-permute-start(f32[4,128,256]{2,1,0:T(8,128)} %get-tuple-element.35), channel_id=1, source_target_pairs={{0,16},{16,0},{1,17},{17,1},{2,18},{18,2},{3,19},{19,3},{4,20},{20... | collective-permute-start | bytes 1572872 | tf_op jit(solution)/shard_map/ppermute | solution.py:166
  120.8 12.4 %all-to-all-done.3.precond = bf16[8,256,128]{2,1,0:T(8,128)(2,1)S(1)} async-done(((bf16[8,256,128]{2,1,0:T(8,128)(2,1)}), bf16[8,256,128]{2,1,0:T(8,128)(2,1)S(1)}, u32[]{:S(2)}, u32[]{:S(2)}) %all-to-all-start.3) | async-done | bytes 524320 | tf_op jit(solution)/shard_map/all_to_all | solution.py:170
  133.2 1.5 shard_map.46
  134.7 1.9 %collective-permute-start.12 = (f32[4,128,256]{2,1,0:T(8,128)S(1)}, f32[4,128,256]{2,1,0:T(8,128)S(1)}, u32[]{:S(2)}, u32[]{:S(2)}) collective-permute-start(f32[4,128,256]{2,1,0:T(8,128)S(1)} %get-tuple-element.40), channel_id=1, source_target_pairs={{0,16},{16,0},{1,17},{17,1},{2,18},{18,2},{3,19},{19,3},{4,20},{20... | collective-permute-start | bytes 1572872 | tf_op jit(solution)/shard_map/ppermute | solution.py:166
  136.6 1.9 %collective-permute-done.12.refs_3_ = f32[4,128,256]{2,1,0:T(8,128)S(1)} collective-permute-done((f32[4,128,256]{2,1,0:T(8,128)S(1)}, f32[4,128,256]{2,1,0:T(8,128)S(1)}, u32[]{:S(2)}, u32[]{:S(2)}) %collective-permute-start.12) | collective-permute-done | bytes 524320 | tf_op jit(solution)/shard_map/ppermute | solution.py:166
  138.5 1.1 shard_map.47
  139.7 26.9 %all_to_all.30 = bf16[32,16,512]{2,1,0:T(8,128)(2,1)S(1)} all-to-all(bf16[32,16,512]{2,1,0:T(8,128)(2,1)S(1)} %bitcast.23), channel_id=1, replica_groups=mesh['xh'=2,'y'=8,'core'=2,'z'=8,'xl'=2] {'xh','xl','z'}, dimensions={0} | all-to-all | bytes 1048576 | tf_op jit(solution)/shard_map/all_to_all | solution.py:170
  166.5 0.1 shard_map.48
  166.6 15.3 %all_to_all.31 = bf16[8,16,1024]{2,1,0:T(8,128)(2,1)S(1)} all-to-all(bf16[8,16,1024]{2,1,0:T(8,128)(2,1)S(1)} %shard_map.48), channel_id=1, replica_groups=mesh['xh'=2,'y'=8,'core'=2,'z'=8,'xl'=2] {'z'}, dimensions={0} | all-to-all | bytes 524288 | tf_op jit(solution)/shard_map/all_to_all | solution.py:170
  181.9 0.9 bitcast_convert_fusion
  (23 shorter events, 0.1 us)
Async XLA Ops:
  0.0 9.0 %copy-start.1 = (bf16[1,128,4096]{2,1,0:T(8,128)(2,1)S(1)}, bf16[1,128,4096]{2,1,0:T(8,128)(2,1)}, u32[]{:S(2)}) copy-start(bf16[1,128,4096]{2,1,0:T(8,128)(2,1)} %param.5) | copy-start | bytes 3145732
  1.8 31.2 %all-to-all-start = ((bf16[8,256,128]{2,1,0:T(8,128)(2,1)}), bf16[8,256,128]{2,1,0:T(8,128)(2,1)S(1)}, u32[]{:S(2)}, u32[]{:S(2)}) async-start(bf16[8,256,128]{2,1,0:T(8,128)(2,1)} %shard_map.39), calls=%async_computation | async-start | bytes 1048576 | tf_op jit(solution)/shard_map/all_to_all | solution.py:170
  9.0 1.2 copy-start.2
  12.1 0.8 copy-start.3
  12.9 11.3 %collective-permute-start.1 = (bf16[128,1024]{1,0:T(8,128)(2,1)S(1)}, bf16[128,1024]{1,0:T(8,128)(2,1)S(1)}, u32[]{:S(2)}, u32[]{:S(2)}) collective-permute-start(bf16[128,1024]{1,0:T(8,128)(2,1)S(1)} %get-tuple-element.27), channel_id=1, source_target_pairs={{0,16},{16,0},{1,17},{17,1},{2,18},{18,2},{3,19},{19,3},{4,20},{20... | collective-permute-start | bytes 786440 | tf_op jit(solution)/shard_map/ppermute | solution.py:166
  14.8 12.5 %collective-permute-start.2 = (bf16[128,1024]{1,0:T(8,128)(2,1)S(1)}, bf16[128,1024]{1,0:T(8,128)(2,1)S(1)}, u32[]{:S(2)}, u32[]{:S(2)}) collective-permute-start(bf16[128,1024]{1,0:T(8,128)(2,1)S(1)} %get-tuple-element.28), channel_id=1, source_target_pairs={{0,256},{256,0},{1,257},{257,1},{2,258},{258,2},{3,259},{259,3},{4... | collective-permute-start | bytes 786440 | tf_op jit(solution)/shard_map/ppermute | solution.py:166
  18.2 14.0 %collective-permute-start.3 = (bf16[128,1024]{1,0:T(8,128)(2,1)S(1)}, bf16[128,1024]{1,0:T(8,128)(2,1)S(1)}, u32[]{:S(2)}, u32[]{:S(2)}) collective-permute-start(bf16[128,1024]{1,0:T(8,128)(2,1)S(1)} %get-tuple-element.29), channel_id=1, source_target_pairs={{0,272},{16,256},{256,16},{272,0},{1,273},{17,257},{257,17},{273,1... | collective-permute-start | bytes 786440 | tf_op jit(solution)/shard_map/ppermute | solution.py:166
  22.0 18.4 %collective-permute-start = (bf16[2,128,1024]{2,1,0:T(8,128)(2,1)}, bf16[2,128,1024]{2,1,0:T(8,128)(2,1)}, u32[]{:S(2)}, u32[]{:S(2)}) collective-permute-start(bf16[2,128,1024]{2,1,0:T(8,128)(2,1)} %get-tuple-element.24), channel_id=1, source_target_pairs={{0,16},{16,0},{1,17},{17,1},{2,18},{18,2},{3,19},{19,3},{4,20},{20... | collective-permute-start | bytes 1572872 | tf_op jit(solution)/shard_map/ppermute | solution.py:166
  33.0 7.4 %copy-start.4 = (bf16[2,128,1024]{2,1,0:T(8,128)(2,1)S(1)}, bf16[2,128,1024]{2,1,0:T(8,128)(2,1)}, u32[]{:S(2)}) copy-start(bf16[2,128,1024]{2,1,0:T(8,128)(2,1)} %copy-done.3) | copy-start | bytes 1572868
  33.1 33.4 %all-to-all-start.2 = ((bf16[8,256,128]{2,1,0:T(8,128)(2,1)}), bf16[8,256,128]{2,1,0:T(8,128)(2,1)S(1)}, u32[]{:S(2)}, u32[]{:S(2)}) async-start(bf16[8,256,128]{2,1,0:T(8,128)(2,1)} %shard_map.43), calls=%async_computation.2 | async-start | bytes 1048576 | tf_op jit(solution)/shard_map/all_to_all | solution.py:170
  41.5 0.8 copy-start.7
  43.0 4.7 %collective-permute-start.4 = (f32[2,256,128]{2,1,0:T(8,128)S(1)}, f32[2,256,128]{2,1,0:T(8,128)S(1)}, u32[]{:S(2)}, u32[]{:S(2)}) collective-permute-start(f32[2,256,128]{2,1,0:T(8,128)S(1)} %get-tuple-element.31), channel_id=1, source_target_pairs={{0,16},{16,0},{1,17},{17,1},{2,18},{18,2},{3,19},{19,3},{4,20},{20... | collective-permute-start | bytes 786440 | tf_op jit(solution)/shard_map/ppermute | solution.py:166
  45.0 28.7 %collective-permute-start.6 = (bf16[2,128,1024]{2,1,0:T(8,128)(2,1)S(1)}, bf16[2,128,1024]{2,1,0:T(8,128)(2,1)S(1)}, u32[]{:S(2)}, u32[]{:S(2)}) collective-permute-start(bf16[2,128,1024]{2,1,0:T(8,128)(2,1)S(1)} %get-tuple-element.25.refs_0_), channel_id=1, source_target_pairs={{0,1},{1,0},{2,3},{3,2},{4,5},{5,4},{6,7},{7,6},{8,9},{9,8},{10,11... | collective-permute-start | bytes 1572872 | tf_op jit(solution)/shard_map/ppermute | solution.py:166
  47.7 17.9 %collective-permute-start.5 = (f32[256,128]{1,0:T(8,128)S(1)}, f32[256,128]{1,0:T(8,128)S(1)}, u32[]{:S(2)}, u32[]{:S(2)}) collective-permute-start(f32[256,128]{1,0:T(8,128)S(1)} %fusion.1), channel_id=1, source_target_pairs={{0,256},{256,0},{1,257},{257,1},{2,258},{258,2},{3,259},{259,3},{4... | collective-permute-start | bytes 393224 | tf_op jit(solution)/shard_map/ppermute | solution.py:166
  66.4 42.2 %all-to-all-start.1 = ((bf16[8,256,128]{2,1,0:T(8,128)(2,1)}), bf16[8,256,128]{2,1,0:T(8,128)(2,1)S(1)}, u32[]{:S(2)}, u32[]{:S(2)}) async-start(bf16[8,256,128]{2,1,0:T(8,128)(2,1)} %shard_map.41), calls=%async_computation.1 | async-start | bytes 1048576 | tf_op jit(solution)/shard_map/all_to_all | solution.py:170
  73.6 2.7 %copy-start.8 = (bf16[2,128,1024]{2,1,0:T(8,128)(2,1)S(1)}, bf16[2,128,1024]{2,1,0:T(8,128)(2,1)}, u32[]{:S(2)}) copy-start(bf16[2,128,1024]{2,1,0:T(8,128)(2,1)} %copy-done.7) | copy-start | bytes 1572868
  74.4 7.5 %collective-permute-start.10 = (f32[2,256,128]{2,1,0:T(8,128)S(1)}, f32[2,256,128]{2,1,0:T(8,128)S(1)}, u32[]{:S(2)}, u32[]{:S(2)}) collective-permute-start(f32[2,256,128]{2,1,0:T(8,128)S(1)} %get-tuple-element.37), channel_id=1, source_target_pairs={{0,16},{16,0},{1,17},{17,1},{2,18},{18,2},{3,19},{19,3},{4,20},{20... | collective-permute-start | bytes 786440 | tf_op jit(solution)/shard_map/ppermute | solution.py:166
  76.3 31.5 %collective-permute-start.8 = (bf16[2,128,1024]{2,1,0:T(8,128)(2,1)S(1)}, bf16[2,128,1024]{2,1,0:T(8,128)(2,1)S(1)}, u32[]{:S(2)}, u32[]{:S(2)}) collective-permute-start(bf16[2,128,1024]{2,1,0:T(8,128)(2,1)S(1)} %copy-done.8), channel_id=1, source_target_pairs={{0,257},{1,256},{256,1},{257,0},{2,259},{3,258},{258,3},{259,2},{4... | collective-permute-start | bytes 1572872 | tf_op jit(solution)/shard_map/ppermute | solution.py:166
  79.3 28.5 %collective-permute-start.7 = (bf16[2,128,1024]{2,1,0:T(8,128)(2,1)S(1)}, bf16[2,128,1024]{2,1,0:T(8,128)(2,1)S(1)}, u32[]{:S(2)}, u32[]{:S(2)}) collective-permute-start(bf16[2,128,1024]{2,1,0:T(8,128)(2,1)S(1)} %copy-done.8), channel_id=1, source_target_pairs={{0,256},{256,0},{1,257},{257,1},{2,258},{258,2},{3,259},{259,3},{4... | collective-permute-start | bytes 1572872 | tf_op jit(solution)/shard_map/ppermute | solution.py:166
  81.9 25.9 %collective-permute-start.11 = (f32[256,128]{1,0:T(8,128)S(1)}, f32[256,128]{1,0:T(8,128)S(1)}, u32[]{:S(2)}, u32[]{:S(2)}) collective-permute-start(f32[256,128]{1,0:T(8,128)S(1)} %fusion), channel_id=1, source_target_pairs={{0,256},{256,0},{1,257},{257,1},{2,258},{258,2},{3,259},{259,3},{4... | collective-permute-start | bytes 393224 | tf_op jit(solution)/shard_map/ppermute | solution.py:166
  107.8 0.8 copy-start
  108.6 24.6 %all-to-all-start.3 = ((bf16[8,256,128]{2,1,0:T(8,128)(2,1)}), bf16[8,256,128]{2,1,0:T(8,128)(2,1)S(1)}, u32[]{:S(2)}, u32[]{:S(2)}) async-start(bf16[8,256,128]{2,1,0:T(8,128)(2,1)} %copy-done), calls=%async_computation.3 | async-start | bytes 1048576 | tf_op jit(solution)/shard_map/all_to_all | solution.py:170
  118.1 0.8 copy-start.5
  118.9 17.7 %collective-permute-start.9 = (f32[4,128,256]{2,1,0:T(8,128)}, f32[4,128,256]{2,1,0:T(8,128)}, u32[]{:S(2)}, u32[]{:S(2)}) collective-permute-start(f32[4,128,256]{2,1,0:T(8,128)} %get-tuple-element.35), channel_id=1, source_target_pairs={{0,16},{16,0},{1,17},{17,1},{2,18},{18,2},{3,19},{19,3},{4,20},{20... | collective-permute-start | bytes 1572872 | tf_op jit(solution)/shard_map/ppermute | solution.py:166
  133.2 5.3 %copy-start.6 = (f32[4,128,256]{2,1,0:T(8,128)S(1)}, f32[4,128,256]{2,1,0:T(8,128)}, u32[]{:S(2)}) copy-start(f32[4,128,256]{2,1,0:T(8,128)} %copy-done.5) | copy-start | bytes 1572868
  134.7 3.8 %collective-permute-start.12 = (f32[4,128,256]{2,1,0:T(8,128)S(1)}, f32[4,128,256]{2,1,0:T(8,128)S(1)}, u32[]{:S(2)}, u32[]{:S(2)}) collective-permute-start(f32[4,128,256]{2,1,0:T(8,128)S(1)} %get-tuple-element.40), channel_id=1, source_target_pairs={{0,16},{16,0},{1,17},{17,1},{2,18},{18,2},{3,19},{19,3},{4,20},{20... | collective-permute-start | bytes 1572872 | tf_op jit(solution)/shard_map/ppermute | solution.py:166

commit v3 on v2

--- a/solution.py
+++ b/solution.py
@@ -10,9 +10,8 @@
 
 F32 = jnp.float32
 BF16 = jnp.bfloat16
-PARTS = 2
 NT = (((1,), (1,)), ((), ()))
-PARAMS = pltpu.CompilerParams(vmem_limit_bytes=16 * 1024 * 1024)
+PARAMS = pltpu.CompilerParams(vmem_limit_bytes=40 * 1024 * 1024)
 WHOLE = pl.BlockSpec(memory_space=pltpu.VMEM)
 ANYWHERE = pl.BlockSpec(memory_space=pl.ANY)
 SCALARS = pl.BlockSpec(memory_space=pltpu.SMEM)
@@ -67,8 +66,8 @@
         out[i] = x[...]
 
 
-def copies(x, n, after=()):
-    return call(copies_body, [like(n, *x.shape)], [x], after=after)[0]
+def copies(x, n):
+    return call(copies_body, [like(n, *x.shape)], [x])[0]
 
 
 def settle_body(own, came, last, out):
@@ -77,54 +76,66 @@
         out[i] = done
 
 
-def settle(own, came, last, n, after=()):
-    return call(settle_body, [like(n, *own.shape)], [own, came, last], after=after)[0]
-
-
-def fold_body(feats, f00, f01, f10, f11, own, own_x, other, held):
-    ny, _, w = feats.shape
+def settle(own, came, last, n):
+    return call(settle_body, [like(n, *own.shape)], [own, came, last])[0]
+
+
+def join(held, parts):
+    ny, _, w = parts.shape
     for y in range(ny):
-        held[:, y * w : (y + 1) * w] = feats[y]
-
-    def dot(block):
-        return lax.dot_general(held[...], block[...], NT, preferred_element_type=F32)
-
-    other[0], other[1] = dot(f01), dot(f11)
-    own[...], own_x[...] = dot(f00), dot(f10)
+        held[:, y * w : (y + 1) * w] = parts[y]
+
+
+def fold_body(feats, f0, f1, out, out_x, held):
+    join(held, feats)
+    out_x[...] = lax.dot_general(held[...], f1[...], NT, preferred_element_type=F32)
+    out[...] = lax.dot_general(held[...], f0[...], NT, preferred_element_type=F32)
 
 
 def fold(feats, blocks, after=()):
     ny, q, w = feats.shape
     return call(
         fold_body,
-        [like(q, w, dtype=F32), like(q, w, dtype=F32), like(2, q, w, dtype=F32)],
+        [like(q, w, dtype=F32)] * 2,
         [feats, *blocks],
         [pltpu.VMEM((q, ny * w), BF16)],
-        flops=2 * q * ny * w * 4 * w,
+        flops=2 * q * ny * w * 2 * w,
         after=after,
     )
 
 
-def score_body(precond, *refs):
-    blocks, (own, other, held) = refs[:-3], refs[-3:]
-    ny, _, w = precond.shape
-    for y in range(ny):
-        held[:, y * w : (y + 1) * w] = precond[y]
-    for i in range(4):
-        for dc, out in enumerate((own, other)):
-            out[i] = lax.dot_general(blocks[i][dc], held[...], NT, preferred_element_type=F32)
-
-
-def score(precond, blocks):
+def fold_far_body(feats, f0, f1, out, held):
+    fold_body(feats, f0, f1, out.at[0], out.at[1], held)
+
+
+def fold_far(feats, blocks, after=()):
+    ny, q, w = feats.shape
+    return call(
+        fold_far_body,
+        [like(2, q, w, dtype=F32)],
+        [feats, *blocks],
+        [pltpu.VMEM((q, ny * w), BF16)],
+        flops=2 * q * ny * w * 2 * w,
+        after=after,
+    )[0]
+
+
+def score_body(dc, precond, b0, b1, b2, b3, out, held):
+    join(held, precond)
+    for i, block in enumerate((b0, b1, b2, b3)):
+        out[i] = lax.dot_general(block[dc], held[...], NT, preferred_element_type=F32)
+
+
+def score(dc, precond, blocks):
     ny, q, w = precond.shape
     n = blocks[0].shape[1]
     return call(
-        score_body,
-        [like(4, n, q, dtype=F32)] * 2,
+        functools.partial(score_body, dc),
+        [like(4, n, q, dtype=F32)],
         [precond, *blocks],
         [pltpu.VMEM((q, ny * w), BF16)],
-        flops=2 * q * ny * w * 8 * n,
-    )
+        flops=2 * q * ny * w * 4 * n,
+    )[0]
 
 
 def meet_body(me, *refs):
@@ -178,27 +189,16 @@
     q, w = query.shape
 
     f00, f01, f10, f11, near, far = pack(me, fisher, stored, ny, w)
-    fish = [f00, swap(f01, "core"), swap(f10, "xh"), swap(f11, "xh", "core")]
+    fish = (f00, swap(f10, "xh")), (swap(f01, "core"), swap(f11, "xh", "core"))
     same, cross = pair(near, swap(far, "core"))
     rows = [same, swap(same, "xl"), swap(cross, "xh"), swap(cross, "xh", "xl")]
 
-    before_gather = ((), fish[1:])
-    before_fold = ((same,), (rows[1],))
-    before_settle = ((), (rows[2], rows[3]))
-    half = q // PARTS
-    feats = [
-        trade(copies(query[h * half : (h + 1) * half], ny, before_gather[h]), "y") for h in range(PARTS)
-    ]
-    precond = []
-    for h in range(PARTS):
-        own, own_x, other = fold(feats[h], fish, before_fold[h])
-        came = swap(other, "core")
-        full = settle(own, came, swap(own_x + came[1], "xh"), ny, before_settle[h])
-        precond.append(trade(full, "y"))
-    terms = []
-    for h in range(PARTS):
-        own, other = score(precond[h], rows)
-        terms += [own, swap(other, "core")]
+    feats = trade(copies(query, ny), "y")
+    came = swap(fold_far(feats, fish[1], (same, fish[0][1])), "core")
+    own, own_x = fold(feats, fish[0])
+    precond = trade(settle(own, came, swap(own_x + came[1], "xh"), ny), "y")
+    came = swap(score(1, precond, rows), "core")
+    terms = [score(0, precond, rows), came]
     scores = trade(meet(me, terms).reshape(2 * nl * nz, n // nz, q), "xh", "xl", "z")
     total = finish(scores.reshape(2, nl, nz, n // nz, q), 1.0 / math.sqrt(nz * f))
     return trade(total, "z").reshape(n, nl * q).astype(F32)

time: 184 us -> 143 us (0.78)
  starting transfers between devices: 65.6 us -> 39.1 us
  waiting for transfers between devices: 56.4 us -> 46.4 us
  local copies, waits for them, and re-layouts: 5.36 us -> 0.91 us
  Pallas kernels: 12 us -> 9.34 us
  blocking collectives: 42.2 us -> 44.1 us
    all_to_all x4 -> x2, starting transfers between devices: 28.8 us -> 10.8 us  [trade(): return lax.all_to_all(x, axes, 0, 0, tiled=True)]
    ppermute x13 -> x10, starting transfers between devices: 36.7 us -> 28.3 us  [swap(): return lax.ppermute(x, axes, [(i, n - 1 - i) for i in range(n)])]
    ppermute x13 -> x10, waiting for transfers between devices: 44 us -> 38.3 us  [swap(): return lax.ppermute(x, axes, [(i, n - 1 - i) for i in range(n)])]
    all_to_all x4 -> x2, waiting for transfers between devices: 12.4 us -> 8.1 us  [trade(): return lax.all_to_all(x, axes, 0, 0, tiled=True)]
    unnamed x18 -> x6, local copies, waits for them, and re-layouts: 4.39 us -> 0.91 us
    pallas_call x12 -> x10, Pallas kernels: 12 us -> 9.34 us  [call(): pl.pallas_call(body, out_shape=[jax.ShapeDtypeStruct(s.shape, s.dtype) fo...]
    all_to_all x2, blocking collectives: 42.2 us -> 44.1 us  [trade(): return lax.all_to_all(x, axes, 0, 0, tiled=True)]
  transfers between devices with their start and end apart: 17 -> 12, of which waited for: 6 -> 8; matrix products, arithmetic and copies ran while one was open for 0% -> 0% of each run, Pallas kernels for 5% -> 3%
where the time goes in v3:
time: 143 us; the launch traced here: 141 us
  waiting for transfers between devices  46.4 us (32%)
  blocking collectives  44.1 us (31%)
  starting transfers between devices  39.1 us (27%)
  Pallas kernels  9.34 us (7%)
    all_to_all x2, blocking collectives, trade(): return lax.all_to_all(x, axes, 0, 0, tiled=True)  44.1 us
    ppermute x10, waiting for transfers between devices, swap(): return lax.ppermute(x, axes, [(i, n - 1 - i) for i in range(n)])  38.3 us
    ppermute x10, starting transfers between devices, swap(): return lax.ppermute(x, axes, [(i, n - 1 - i) for i in range(n)])  28.3 us
    all_to_all x2, starting transfers between devices, trade(): return lax.all_to_all(x, axes, 0, 0, tiled=True)  10.8 us
    pallas_call x10, Pallas kernels, call(): pl.pallas_call(body, out_shape=[jax.ShapeDtypeStruct(s.shape, s.dtype) fo...  9.34 us
    all_to_all x2, waiting for transfers between devices, trade(): return lax.all_to_all(x, axes, 0, 0, tiled=True)  8.1 us
  transfers between devices with their start and end apart: 12, of which 8 were waited for; matrix products, arithmetic and copies ran while one was open for 0% of the time, Pallas kernels for 3%

profile of v3, /device:TPU:6, one launch (start us, length us, event | category | flops | bytes accessed | tf_op | source)
XLA Modules:
  0.0 140.9 jit_solution(17506780903231794045)
XLA Ops:
  0.0 0.0 copy-start.2
  0.0 0.9 copy-done.2
  0.9 1.1 shard_map.37
  2.0 0.0 copy-start
  2.0 0.0 copy-start.1
  2.0 7.2 %all-to-all-start = ((bf16[8,512,128]{2,1,0:T(8,128)(2,1)}), bf16[8,512,128]{2,1,0:T(8,128)(2,1)S(1)}, u32[]{:S(2)}, u32[]{:S(2)}) async-start(bf16[8,512,128]{2,1,0:T(8,128)(2,1)} %shard_map.37), calls=%async_computation | async-start | bytes 2097152 | tf_op jit(solution)/shard_map/all_to_all | solution.py:181
  9.3 0.1 pad_add_fusion.me
  9.3 0.0 copy-done
  9.3 0.0 copy-done.1
  9.3 1.1 shard_map.38
  10.4 1.9 %collective-permute-start.1 = (bf16[2,128,1024]{2,1,0:T(8,128)(2,1)S(1)}, bf16[2,128,1024]{2,1,0:T(8,128)(2,1)S(1)}, u32[]{:S(2)}, u32[]{:S(2)}) collective-permute-start(bf16[2,128,1024]{2,1,0:T(8,128)(2,1)S(1)} %get-tuple-element.19), channel_id=1, source_target_pairs={{0,16},{16,0},{1,17},{17,1},{2,18},{18,2},{3,19},{19,3},{4,20},{20... | collective-permute-start | bytes 1572872 | tf_op jit(solution)/shard_map/ppermute | solution.py:177
  12.4 3.3 %collective-permute-start = (bf16[128,1024]{1,0:T(8,128)(2,1)S(1)}, bf16[128,1024]{1,0:T(8,128)(2,1)S(1)}, u32[]{:S(2)}, u32[]{:S(2)}) collective-permute-start(bf16[128,1024]{1,0:T(8,128)(2,1)S(1)} %get-tuple-element.16), channel_id=1, source_target_pairs={{0,256},{256,0},{1,257},{257,1},{2,258},{258,2},{3,259},{259,3},{4... | collective-permute-start | bytes 786440 | tf_op jit(solution)/shard_map/ppermute | solution.py:177
  15.7 2.1 %collective-permute-start.2 = (bf16[128,1024]{1,0:T(8,128)(2,1)S(1)}, bf16[128,1024]{1,0:T(8,128)(2,1)S(1)}, u32[]{:S(2)}, u32[]{:S(2)}) collective-permute-start(bf16[128,1024]{1,0:T(8,128)(2,1)S(1)} %get-tuple-element.21), channel_id=1, source_target_pairs={{0,16},{16,0},{1,17},{17,1},{2,18},{18,2},{3,19},{19,3},{4,20},{20... | collective-permute-start | bytes 786440 | tf_op jit(solution)/shard_map/ppermute | solution.py:177
  17.8 3.9 %collective-permute-start.3 = (bf16[128,1024]{1,0:T(8,128)(2,1)S(1)}, bf16[128,1024]{1,0:T(8,128)(2,1)S(1)}, u32[]{:S(2)}, u32[]{:S(2)}) collective-permute-start(bf16[128,1024]{1,0:T(8,128)(2,1)S(1)} %get-tuple-element.22), channel_id=1, source_target_pairs={{0,272},{16,256},{256,16},{272,0},{1,273},{17,257},{257,17},{273,1... | collective-permute-start | bytes 786440 | tf_op jit(solution)/shard_map/ppermute | solution.py:177
  21.8 0.0 collective-permute-done.1.came
  21.8 0.9 shard_map.40
  22.6 2.0 %collective-permute-done.f1.refs_1_ = bf16[128,1024]{1,0:T(8,128)(2,1)S(1)} collective-permute-done((bf16[128,1024]{1,0:T(8,128)(2,1)S(1)}, bf16[128,1024]{1,0:T(8,128)(2,1)S(1)}, u32[]{:S(2)}, u32[]{:S(2)}) %collective-permute-start) | collective-permute-done | bytes 262176 | tf_op jit(solution)/shard_map/ppermute | solution.py:177
  24.7 0.0 collective-permute-done.2.refs_3_
  24.7 5.2 %collective-permute-done.3.refs_4_ = bf16[128,1024]{1,0:T(8,128)(2,1)S(1)} collective-permute-done((bf16[128,1024]{1,0:T(8,128)(2,1)S(1)}, bf16[128,1024]{1,0:T(8,128)(2,1)S(1)}, u32[]{:S(2)}, u32[]{:S(2)}) %collective-permute-start.3) | collective-permute-done | bytes 262176 | tf_op jit(solution)/shard_map/ppermute | solution.py:177
  29.9 8.1 %all-to-all-done.feats.refs_2_ = bf16[8,512,128]{2,1,0:T(8,128)(2,1)S(1)} async-done(((bf16[8,512,128]{2,1,0:T(8,128)(2,1)}), bf16[8,512,128]{2,1,0:T(8,128)(2,1)S(1)}, u32[]{:S(2)}, u32[]{:S(2)}) %all-to-all-start) | async-done | bytes 1048608 | tf_op jit(solution)/shard_map/all_to_all | solution.py:181
  38.0 0.7 shard_map.41
  38.7 1.9 %collective-permute-start.4 = (f32[2,512,128]{2,1,0:T(8,128)S(1)}, f32[2,512,128]{2,1,0:T(8,128)S(1)}, u32[]{:S(2)}, u32[]{:S(2)}) collective-permute-start(f32[2,512,128]{2,1,0:T(8,128)S(1)} %shard_map.41), channel_id=1, source_target_pairs={{0,16},{16,0},{1,17},{17,1},{2,18},{18,2},{3,19},{19,3},{4,20},{20... | collective-permute-start | bytes 1572872 | tf_op jit(solution)/shard_map/ppermute | solution.py:177
  40.7 0.7 shard_map.39
  41.4 1.1 collective-permute-done.4.came
  42.6 3.3 %collective-permute-start.5 = (f32[512,128]{1,0:T(8,128)S(1)}, f32[512,128]{1,0:T(8,128)S(1)}, u32[]{:S(2)}, u32[]{:S(2)}) collective-permute-start(f32[512,128]{1,0:T(8,128)S(1)} %fusion), channel_id=1, source_target_pairs={{0,256},{256,0},{1,257},{257,1},{2,258},{258,2},{3,259},{259,3},{4... | collective-permute-start | bytes 786440 | tf_op jit(solution)/shard_map/ppermute | solution.py:177
  45.9 8.4 %collective-permute-done.5.last = f32[512,128]{1,0:T(8,128)S(1)} collective-permute-done((f32[512,128]{1,0:T(8,128)S(1)}, f32[512,128]{1,0:T(8,128)S(1)}, u32[]{:S(2)}, u32[]{:S(2)}) %collective-permute-start.5) | collective-permute-done | bytes 262176 | tf_op jit(solution)/shard_map/ppermute | solution.py:177
  54.3 1.1 shard_map.42
  55.4 3.6 %all-to-all-start.1 = ((bf16[8,512,128]{2,1,0:T(8,128)(2,1)}), bf16[8,512,128]{2,1,0:T(8,128)(2,1)S(1)}, u32[]{:S(2)}, u32[]{:S(2)}) async-start(bf16[8,512,128]{2,1,0:T(8,128)(2,1)} %shard_map.42), calls=%async_computation.1 | async-start | bytes 2097152 | tf_op jit(solution)/shard_map/all_to_all | solution.py:181
  58.9 2.4 %collective-permute-start.8 = (bf16[2,128,1024]{2,1,0:T(8,128)(2,1)}, bf16[2,128,1024]{2,1,0:T(8,128)(2,1)S(1)}, u32[]{:S(2)}, u32[]{:S(2)}) collective-permute-start(bf16[2,128,1024]{2,1,0:T(8,128)(2,1)} %get-tuple-element.24), channel_id=1, source_target_pairs={{0,257},{1,256},{256,1},{257,0},{2,259},{3,258},{258,3},{259,2},{4... | collective-permute-start | bytes 1572872 | tf_op jit(solution)/shard_map/ppermute | solution.py:177
  61.3 4.3 %collective-permute-start.7 = (bf16[2,128,1024]{2,1,0:T(8,128)(2,1)}, bf16[2,128,1024]{2,1,0:T(8,128)(2,1)S(1)}, u32[]{:S(2)}, u32[]{:S(2)}) collective-permute-start(bf16[2,128,1024]{2,1,0:T(8,128)(2,1)} %get-tuple-element.24), channel_id=1, source_target_pairs={{0,256},{256,0},{1,257},{257,1},{2,258},{258,2},{3,259},{259,3},{4... | collective-permute-start | bytes 1572872 | tf_op jit(solution)/shard_map/ppermute | solution.py:177
  65.6 3.1 %collective-permute-start.6 = (bf16[2,128,1024]{2,1,0:T(8,128)(2,1)S(1)}, bf16[2,128,1024]{2,1,0:T(8,128)(2,1)S(1)}, u32[]{:S(2)}, u32[]{:S(2)}) collective-permute-start(bf16[2,128,1024]{2,1,0:T(8,128)(2,1)S(1)} %get-tuple-element.20.refs_0_.b0), channel_id=1, source_target_pairs={{0,1},{1,0},{2,3},{3,2},{4,5},{5,4},{6,7},{7,6},{8,9},{9,8},{10,11... | collective-permute-start | bytes 1572872 | tf_op jit(solution)/shard_map/ppermute | solution.py:177
  68.8 17.8 %collective-permute-done.8.b3 = bf16[2,128,1024]{2,1,0:T(8,128)(2,1)S(1)} collective-permute-done((bf16[2,128,1024]{2,1,0:T(8,128)(2,1)}, bf16[2,128,1024]{2,1,0:T(8,128)(2,1)S(1)}, u32[]{:S(2)}, u32[]{:S(2)}) %collective-permute-start.8) | collective-permute-done | bytes 524320 | tf_op jit(solution)/shard_map/ppermute | solution.py:177
  86.6 0.0 collective-permute-done.7.b2
  86.6 2.5 %collective-permute-done.6.b1 = bf16[2,128,1024]{2,1,0:T(8,128)(2,1)S(1)} collective-permute-done((bf16[2,128,1024]{2,1,0:T(8,128)(2,1)S(1)}, bf16[2,128,1024]{2,1,0:T(8,128)(2,1)S(1)}, u32[]{:S(2)}, u32[]{:S(2)}) %collective-permute-start.6) | collective-permute-done | bytes 524320 | tf_op jit(solution)/shard_map/ppermute | solution.py:177
  89.1 0.0 all-to-all-done.1.precond
  89.1 1.5 %shard_map.44 = f32[4,128,512]{2,1,0:T(8,128)S(1)} custom-call(bf16[8,512,128]{2,1,0:T(8,128)(2,1)S(1)} %all-to-all-done.1.precond, bf16[2,128,1024]{2,1,0:T(8,128)(2,1)S(1)} %get-tuple-element.20.refs_0_.b0, bf16[2,128,1024]{2,1,0:T(8,128)(2,1)S(1)} %collective-permute-done.6.b1, bf16[2,128,1024]{2,1,0:T(8,128)(2,1)S(1)} %collective-permute-done.7.b2, ...), custom_call_target="tpu_custom_call" | custom-call | flops 536870912 | bytes 4194304 | tf_op jit(solution)/shard_map/pallas_call | solution.py:25
  90.7 1.9 %collective-permute-start.9 = (f32[4,128,512]{2,1,0:T(8,128)S(1)}, f32[4,128,512]{2,1,0:T(8,128)S(1)}, u32[]{:S(2)}, u32[]{:S(2)}) collective-permute-start(f32[4,128,512]{2,1,0:T(8,128)S(1)} %shard_map.44), channel_id=1, source_target_pairs={{0,16},{16,0},{1,17},{17,1},{2,18},{18,2},{3,19},{19,3},{4,20},{20... | collective-permute-start | bytes 3145736 | tf_op jit(solution)/shard_map/ppermute | solution.py:177
  92.6 1.5 %shard_map.43.refs_0_ = f32[4,128,512]{2,1,0:T(8,128)S(1)} custom-call(bf16[8,512,128]{2,1,0:T(8,128)(2,1)S(1)} %all-to-all-done.1.precond, bf16[2,128,1024]{2,1,0:T(8,128)(2,1)S(1)} %get-tuple-element.20.refs_0_.b0, bf16[2,128,1024]{2,1,0:T(8,128)(2,1)S(1)} %collective-permute-done.6.b1, bf16[2,128,1024]{2,1,0:T(8,128)(2,1)S(1)} %collective-permute-done.7.b2, ...), custom_call_target="tpu_custom_call" | custom-call | flops 536870912 | bytes 4194304 | tf_op jit(solution)/shard_map/pallas_call | solution.py:25
  94.1 1.1 collective-permute-done.9.refs_1_
  95.2 0.6 shard_map.45
  95.9 28.8 %all_to_all.20 = bf16[32,16,512]{2,1,0:T(8,128)(2,1)S(1)} all-to-all(bf16[32,16,512]{2,1,0:T(8,128)(2,1)S(1)} %bitcast.16), channel_id=1, replica_groups=mesh['xh'=2,'y'=8,'core'=2,'z'=8,'xl'=2] {'xh','xl','z'}, dimensions={0} | all-to-all | bytes 1048576 | tf_op jit(solution)/shard_map/all_to_all | solution.py:181
  124.6 0.1 shard_map.46
  124.7 15.3 %all_to_all.21 = bf16[8,16,1024]{2,1,0:T(8,128)(2,1)S(1)} all-to-all(bf16[8,16,1024]{2,1,0:T(8,128)(2,1)S(1)} %shard_map.46), channel_id=1, replica_groups=mesh['xh'=2,'y'=8,'core'=2,'z'=8,'xl'=2] {'z'}, dimensions={0} | all-to-all | bytes 524288 | tf_op jit(solution)/shard_map/all_to_all | solution.py:181
  140.0 0.9 bitcast_convert_fusion
  (1 shorter events, 0.0 us)
Async XLA Ops:
  0.0 0.9 copy-start.2
  2.0 7.3 %copy-start = (bf16[1,128,4096]{2,1,0:T(8,128)(2,1)S(1)}, bf16[1,128,4096]{2,1,0:T(8,128)(2,1)}, u32[]{:S(2)}) copy-start(bf16[1,128,4096]{2,1,0:T(8,128)(2,1)} %param.5) | copy-start | bytes 3145732
  2.0 7.3 %copy-start.1 = (bf16[128,1,4096]{2,0,1:T(8,128)(2,1)S(1)}, bf16[128,1,4096]{2,0,1:T(8,128)(2,1)}, u32[]{:S(2)}) copy-start(bf16[128,1,4096]{2,0,1:T(8,128)(2,1)} %param.3) | copy-start | bytes 3145732
  2.0 36.0 %all-to-all-start = ((bf16[8,512,128]{2,1,0:T(8,128)(2,1)}), bf16[8,512,128]{2,1,0:T(8,128)(2,1)S(1)}, u32[]{:S(2)}, u32[]{:S(2)}) async-start(bf16[8,512,128]{2,1,0:T(8,128)(2,1)} %shard_map.37), calls=%async_computation | async-start | bytes 2097152 | tf_op jit(solution)/shard_map/all_to_all | solution.py:181
  10.4 11.3 %collective-permute-start.1 = (bf16[2,128,1024]{2,1,0:T(8,128)(2,1)S(1)}, bf16[2,128,1024]{2,1,0:T(8,128)(2,1)S(1)}, u32[]{:S(2)}, u32[]{:S(2)}) collective-permute-start(bf16[2,128,1024]{2,1,0:T(8,128)(2,1)S(1)} %get-tuple-element.19), channel_id=1, source_target_pairs={{0,16},{16,0},{1,17},{17,1},{2,18},{18,2},{3,19},{19,3},{4,20},{20... | collective-permute-start | bytes 1572872 | tf_op jit(solution)/shard_map/ppermute | solution.py:177
  12.4 12.3 %collective-permute-start = (bf16[128,1024]{1,0:T(8,128)(2,1)S(1)}, bf16[128,1024]{1,0:T(8,128)(2,1)S(1)}, u32[]{:S(2)}, u32[]{:S(2)}) collective-permute-start(bf16[128,1024]{1,0:T(8,128)(2,1)S(1)} %get-tuple-element.16), channel_id=1, source_target_pairs={{0,256},{256,0},{1,257},{257,1},{2,258},{258,2},{3,259},{259,3},{4... | collective-permute-start | bytes 786440 | tf_op jit(solution)/shard_map/ppermute | solution.py:177
  15.7 9.0 %collective-permute-start.2 = (bf16[128,1024]{1,0:T(8,128)(2,1)S(1)}, bf16[128,1024]{1,0:T(8,128)(2,1)S(1)}, u32[]{:S(2)}, u32[]{:S(2)}) collective-permute-start(bf16[128,1024]{1,0:T(8,128)(2,1)S(1)} %get-tuple-element.21), channel_id=1, source_target_pairs={{0,16},{16,0},{1,17},{17,1},{2,18},{18,2},{3,19},{19,3},{4,20},{20... | collective-permute-start | bytes 786440 | tf_op jit(solution)/shard_map/ppermute | solution.py:177
  17.8 12.1 %collective-permute-start.3 = (bf16[128,1024]{1,0:T(8,128)(2,1)S(1)}, bf16[128,1024]{1,0:T(8,128)(2,1)S(1)}, u32[]{:S(2)}, u32[]{:S(2)}) collective-permute-start(bf16[128,1024]{1,0:T(8,128)(2,1)S(1)} %get-tuple-element.22), channel_id=1, source_target_pairs={{0,272},{16,256},{256,16},{272,0},{1,273},{17,257},{257,17},{273,1... | collective-permute-start | bytes 786440 | tf_op jit(solution)/shard_map/ppermute | solution.py:177
  38.7 3.8 %collective-permute-start.4 = (f32[2,512,128]{2,1,0:T(8,128)S(1)}, f32[2,512,128]{2,1,0:T(8,128)S(1)}, u32[]{:S(2)}, u32[]{:S(2)}) collective-permute-start(f32[2,512,128]{2,1,0:T(8,128)S(1)} %shard_map.41), channel_id=1, source_target_pairs={{0,16},{16,0},{1,17},{17,1},{2,18},{18,2},{3,19},{19,3},{4,20},{20... | collective-permute-start | bytes 1572872 | tf_op jit(solution)/shard_map/ppermute | solution.py:177
  42.6 11.7 %collective-permute-start.5 = (f32[512,128]{1,0:T(8,128)S(1)}, f32[512,128]{1,0:T(8,128)S(1)}, u32[]{:S(2)}, u32[]{:S(2)}) collective-permute-start(f32[512,128]{1,0:T(8,128)S(1)} %fusion), channel_id=1, source_target_pairs={{0,256},{256,0},{1,257},{257,1},{2,258},{258,2},{3,259},{259,3},{4... | collective-permute-start | bytes 786440 | tf_op jit(solution)/shard_map/ppermute | solution.py:177
  55.4 33.8 %all-to-all-start.1 = ((bf16[8,512,128]{2,1,0:T(8,128)(2,1)}), bf16[8,512,128]{2,1,0:T(8,128)(2,1)S(1)}, u32[]{:S(2)}, u32[]{:S(2)}) async-start(bf16[8,512,128]{2,1,0:T(8,128)(2,1)} %shard_map.42), calls=%async_computation.1 | async-start | bytes 2097152 | tf_op jit(solution)/shard_map/all_to_all | solution.py:181
  58.9 27.7 %collective-permute-start.8 = (bf16[2,128,1024]{2,1,0:T(8,128)(2,1)}, bf16[2,128,1024]{2,1,0:T(8,128)(2,1)S(1)}, u32[]{:S(2)}, u32[]{:S(2)}) collective-permute-start(bf16[2,128,1024]{2,1,0:T(8,128)(2,1)} %get-tuple-element.24), channel_id=1, source_target_pairs={{0,257},{1,256},{256,1},{257,0},{2,259},{3,258},{258,3},{259,2},{4... | collective-permute-start | bytes 1572872 | tf_op jit(solution)/shard_map/ppermute | solution.py:177
  61.3 25.3 %collective-permute-start.7 = (bf16[2,128,1024]{2,1,0:T(8,128)(2,1)}, bf16[2,128,1024]{2,1,0:T(8,128)(2,1)S(1)}, u32[]{:S(2)}, u32[]{:S(2)}) collective-permute-start(bf16[2,128,1024]{2,1,0:T(8,128)(2,1)} %get-tuple-element.24), channel_id=1, source_target_pairs={{0,256},{256,0},{1,257},{257,1},{2,258},{258,2},{3,259},{259,3},{4... | collective-permute-start | bytes 1572872 | tf_op jit(solution)/shard_map/ppermute | solution.py:177
  65.6 23.5 %collective-permute-start.6 = (bf16[2,128,1024]{2,1,0:T(8,128)(2,1)S(1)}, bf16[2,128,1024]{2,1,0:T(8,128)(2,1)S(1)}, u32[]{:S(2)}, u32[]{:S(2)}) collective-permute-start(bf16[2,128,1024]{2,1,0:T(8,128)(2,1)S(1)} %get-tuple-element.20.refs_0_.b0), channel_id=1, source_target_pairs={{0,1},{1,0},{2,3},{3,2},{4,5},{5,4},{6,7},{7,6},{8,9},{9,8},{10,11... | collective-permute-start | bytes 1572872 | tf_op jit(solution)/shard_map/ppermute | solution.py:177
  90.7 4.6 %collective-permute-start.9 = (f32[4,128,512]{2,1,0:T(8,128)S(1)}, f32[4,128,512]{2,1,0:T(8,128)S(1)}, u32[]{:S(2)}, u32[]{:S(2)}) collective-permute-start(f32[4,128,512]{2,1,0:T(8,128)S(1)} %shard_map.44), channel_id=1, source_target_pairs={{0,16},{16,0},{1,17},{17,1},{2,18},{18,2},{3,19},{19,3},{4,20},{20... | collective-permute-start | bytes 3145736 | tf_op jit(solution)/shard_map/ppermute | solution.py:177

commit v4 on v3

--- a/solution.py
+++ b/solution.py
@@ -37,28 +37,30 @@
     return jax.ShapeDtypeStruct(shape, dtype)
 
 
-def pack_body(ny, w, me, fisher, stored, f00, f01, f10, f11, own, other):
-    for x, outs in ((fisher, ((f00, f10), (f01, f11))), (stored, ([own.at[0], own.at[1]], [other.at[0], other.at[1]]))):
-        for dc in range(2):
-            for dx in range(2):
+def pack_body(ny, w, me, fisher, stored, f_near, f_far, f_cross, s_same, s_cross):
+    for x, outs in ((fisher, ((f_near, f_far), f_cross)), (stored, (s_same, s_cross))):
+        for dx in range(2):
+            for dc in range(2):
+                out = outs[dx][dc] if isinstance(outs[dx], tuple) else outs[dx].at[dc]
                 for y in range(ny):
                     first = (((me[0] ^ dx) * ny + y) * 2 + (me[1] ^ dc)) * w
-                    outs[dc][dx][:, y * w : (y + 1) * w] = x[:, pl.ds(pl.multiple_of(first, w), w)]
+                    out[:, y * w : (y + 1) * w] = x[:, pl.ds(pl.multiple_of(first, w), w)]
 
 
 def pack(me, fisher, stored, ny, w):
     n, g = stored.shape[0], fisher.shape[0]
-    shapes = [like(g, ny * w)] * 4 + [like(2, n, ny * w)] * 2
+    shapes = [like(g, ny * w)] * 2 + [like(2, g, ny * w)] + [like(2, n, ny * w)] * 2
     return call(functools.partial(pack_body, ny, w), shapes, [me, fisher, stored])
 
 
-def pair_body(near, came, same, cross):
-    for dx, out in enumerate((same, cross)):
-        out[0], out[1] = near[dx], came[dx]
-
-
-def pair(near, came):
-    return call(pair_body, [like(*near.shape)] * 2, [near, came])
+def gather_far_body(*refs):
+    blocks, out = refs[:-1], refs[-1]
+    for i, block in enumerate(blocks):
+        out[i] = block[...] if len(block.shape) == 2 else block[1]
+
+
+def gather_far(blocks):
+    return call(gather_far_body, [like(len(blocks), *blocks[0].shape[-2:])], blocks)[0]
 
 
 def copies_body(x, out):
@@ -86,26 +88,33 @@
         held[:, y * w : (y + 1) * w] = parts[y]
 
 
-def fold_body(feats, f0, f1, out, out_x, held):
+def join(held, parts):
+    ny, _, w = parts.shape
+    for y in range(ny):
+        held[:, y * w : (y + 1) * w] = parts[y]
+
+
+def fold_body(feats, near, cross, out, out_x, held):
     join(held, feats)
-    out_x[...] = lax.dot_general(held[...], f1[...], NT, preferred_element_type=F32)
-    out[...] = lax.dot_general(held[...], f0[...], NT, preferred_element_type=F32)
-
-
-def fold(feats, blocks, after=()):
+    out_x[...] = lax.dot_general(held[...], cross[0], NT, preferred_element_type=F32)
+    out[...] = lax.dot_general(held[...], near[...], NT, preferred_element_type=F32)
+
+
+def fold(feats, near, cross):
     ny, q, w = feats.shape
     return call(
         fold_body,
         [like(q, w, dtype=F32)] * 2,
-        [feats, *blocks],
+        [feats, near, cross],
         [pltpu.VMEM((q, ny * w), BF16)],
         flops=2 * q * ny * w * 2 * w,
-        after=after,
     )
 
 
-def fold_far_body(feats, f0, f1, out, held):
-    fold_body(feats, f0, f1, out.at[0], out.at[1], held)
+def fold_far_body(feats, blocks, out, held):
+    join(held, feats)
+    for dx in range(2):
+        out[dx] = lax.dot_general(held[...], blocks[dx], NT, preferred_element_type=F32)
 
 
 def fold_far(feats, blocks, after=()):
@@ -113,24 +122,28 @@
     return call(
         fold_far_body,
         [like(2, q, w, dtype=F32)],
-        [feats, *blocks],
+        [feats, blocks],
         [pltpu.VMEM((q, ny * w), BF16)],
         flops=2 * q * ny * w * 2 * w,
         after=after,
     )[0]
 
 
-def score_body(dc, precond, b0, b1, b2, b3, out, held):
+def score_body(precond, *refs):
+    blocks, (out, held) = refs[:-2], refs[-2:]
     join(held, precond)
-    for i, block in enumerate((b0, b1, b2, b3)):
-        out[i] = lax.dot_general(block[dc], held[...], NT, preferred_element_type=F32)
-
-
-def score(dc, precond, blocks):
+    i = 0
+    for block in blocks:
+        for k in range(block.shape[0] if len(blocks) == 2 else 1):
+            out[i] = lax.dot_general(block[k], held[...], NT, preferred_element_type=F32)
+            i += 1
+
+
+def score(precond, blocks):
     ny, q, w = precond.shape
     n = blocks[0].shape[1]
     return call(
-        functools.partial(score_body, dc),
+        score_body,
         [like(4, n, q, dtype=F32)],
         [precond, *blocks],
         [pltpu.VMEM((q, ny * w), BF16)],
@@ -145,7 +158,7 @@
         q = own.shape[2]
         for x in range(2):
             for l in range(2):
-                i = (x ^ me[0]) * 2 + (l ^ me[2])
+                i = (x ^ me[0]) * 2 + ((x ^ me[0]) ^ (l ^ me[2]))
                 out[x * 2 + l, :, h * q : (h + 1) * q] = (own[i] + came[i]).astype(BF16)
 
 
@@ -188,17 +201,20 @@
     n, f = stored.shape
     q, w = query.shape
 
-    f00, f01, f10, f11, near, far = pack(me, fisher, stored, ny, w)
-    fish = (f00, swap(f10, "xh")), (swap(f01, "core"), swap(f11, "xh", "core"))
-    same, cross = pair(near, swap(far, "core"))
-    rows = [same, swap(same, "xl"), swap(cross, "xh"), swap(cross, "xh", "xl")]
+    f_near, f_far, f_cross, s_same, s_cross = pack(me, fisher, stored, ny, w)
+    f_cross = swap(f_cross, "xh", "xl")
+    f_far = swap(gather_far([f_far, f_cross]), "core")
+    s_side = swap(s_same, "xl")
+    s_across = swap(s_cross, "xh", "xl")
+    s_passed = swap(s_across, "xl")
 
     feats = trade(copies(query, ny), "y")
-    came = swap(fold_far(feats, fish[1], (same, fish[0][1])), "core")
-    own, own_x = fold(feats, fish[0])
+    came = swap(fold_far(feats, f_far, (s_side, s_across)), "core")
+    own, own_x = fold(feats, f_near, f_cross)
     precond = trade(settle(own, came, swap(own_x + came[1], "xh"), ny), "y")
-    came = swap(score(1, precond, rows), "core")
-    terms = [score(0, precond, rows), came]
+    far = [swap(gather_far([s_same, s_side, s_across]), "core"), swap(gather_far([s_passed]), "core")]
+    came = swap(score(precond, far), "core")
+    terms = [score(precond, [s_same, s_side, s_across, s_passed]), came]
     scores = trade(meet(me, terms).reshape(2 * nl * nz, n // nz, q), "xh", "xl", "z")
     total = finish(scores.reshape(2, nl, nz, n // nz, q), 1.0 / math.sqrt(nz * f))
     return trade(total, "z").reshape(n, nl * q).astype(F32)

time: 143 us -> 148 us (1.035)
  local copies, waits for them, and re-layouts: 0.91 us -> 6.01 us
  waiting for transfers between devices: 46.4 us -> 50.1 us
  starting transfers between devices: 39.1 us -> 36.7 us
    ppermute x10, starting transfers between devices: 28.3 us -> 22.6 us  [swap(): return lax.ppermute(x, axes, [(i, n - 1 - i) for i in range(n)])]
    unnamed x6 -> x14, local copies, waits for them, and re-layouts: 0.91 us -> 6.01 us
    all_to_all x2, starting transfers between devices: 10.8 us -> 14.2 us  [trade(): return lax.all_to_all(x, axes, 0, 0, tiled=True)]
    ppermute x10, waiting for transfers between devices: 38.3 us -> 41 us  [swap(): return lax.ppermute(x, axes, [(i, n - 1 - i) for i in range(n)])]
    pallas_call x10 -> x12, Pallas kernels: 9.34 us -> 8.62 us  [call(): pl.pallas_call(body, out_shape=[jax.ShapeDtypeStruct(s.shape, s.dtype) fo...]
  transfers between devices with their start and end apart: 12 -> 12, of which waited for: 8 -> 8; matrix products, arithmetic and copies ran while one was open for 0% -> 0% of each run, Pallas kernels for 3% -> 2%
where the time goes in v4:
time: 148 us; the launch traced here: 146 us
  waiting for transfers between devices  50.1 us (34%)
  blocking collectives  43.8 us (30%)
  starting transfers between devices  36.7 us (25%)
  Pallas kernels  8.62 us (6%)
  local copies, waits for them, and re-layouts  6.01 us (4%)
    all_to_all x2, blocking collectives, trade(): return lax.all_to_all(x, axes, 0, 0, tiled=True)  43.8 us
    ppermute x10, waiting for transfers between devices, swap(): return lax.ppermute(x, axes, [(i, n - 1 - i) for i in range(n)])  41 us
    ppermute x10, starting transfers between devices, swap(): return lax.ppermute(x, axes, [(i, n - 1 - i) for i in range(n)])  22.6 us
    all_to_all x2, starting transfers between devices, trade(): return lax.all_to_all(x, axes, 0, 0, tiled=True)  14.2 us
    all_to_all x2, waiting for transfers between devices, trade(): return lax.all_to_all(x, axes, 0, 0, tiled=True)  9.1 us
    pallas_call x12, Pallas kernels, call(): pl.pallas_call(body, out_shape=[jax.ShapeDtypeStruct(s.shape, s.dtype) fo...  8.62 us
    unnamed x14, local copies, waits for them, and re-layouts  6.01 us
  transfers between devices with their start and end apart: 12, of which 8 were waited for; matrix products, arithmetic and copies ran while one was open for 0% of the time, Pallas kernels for 2%

profile of v4, /device:TPU:6, one launch (start us, length us, event | category | flops | bytes accessed | tf_op | source)
XLA Modules:
  0.0 146.4 jit_solution(16789069523022026932)
XLA Ops:
  0.0 0.0 copy-start.6
  0.0 0.9 copy-done.6
  0.9 1.1 shard_map.37
  2.0 0.0 copy-start
  2.0 7.2 %all-to-all-start = ((bf16[8,512,128]{2,1,0:T(8,128)(2,1)}), bf16[8,512,128]{2,1,0:T(8,128)(2,1)S(1)}, u32[]{:S(2)}, u32[]{:S(2)}) async-start(bf16[8,512,128]{2,1,0:T(8,128)(2,1)} %shard_map.37), calls=%async_computation | async-start | bytes 2097152 | tf_op jit(solution)/shard_map/all_to_all | solution.py:194
  9.3 0.1 pad_add_fusion.me
  9.4 0.0 copy-done
  9.4 0.0 copy-start.1
  9.4 1.2 copy-done.1
  10.6 1.1 shard_map.38
  11.7 4.2 %collective-permute-start = (bf16[2,128,1024]{2,1,0:T(8,128)(2,1)S(1)}, bf16[2,128,1024]{2,1,0:T(8,128)(2,1)S(1)}, u32[]{:S(2)}, u32[]{:S(2)}) collective-permute-start(bf16[2,128,1024]{2,1,0:T(8,128)(2,1)S(1)} %get-tuple-element.13), channel_id=1, source_target_pairs={{0,257},{1,256},{256,1},{257,0},{2,259},{3,258},{258,3},{259,2},{4... | collective-permute-start | bytes 1572872 | tf_op jit(solution)/shard_map/ppermute | solution.py:190
  15.9 2.8 %collective-permute-start.2 = (bf16[2,128,1024]{2,1,0:T(8,128)(2,1)S(1)}, bf16[2,128,1024]{2,1,0:T(8,128)(2,1)S(1)}, u32[]{:S(2)}, u32[]{:S(2)}) collective-permute-start(bf16[2,128,1024]{2,1,0:T(8,128)(2,1)S(1)} %get-tuple-element.16), channel_id=1, source_target_pairs={{0,257},{1,256},{256,1},{257,0},{2,259},{3,258},{258,3},{259,2},{4... | collective-permute-start | bytes 1572872 | tf_op jit(solution)/shard_map/ppermute | solution.py:190
  18.8 1.9 %collective-permute-start.1 = (bf16[2,128,1024]{2,1,0:T(8,128)(2,1)S(1)}, bf16[2,128,1024]{2,1,0:T(8,128)(2,1)S(1)}, u32[]{:S(2)}, u32[]{:S(2)}) collective-permute-start(bf16[2,128,1024]{2,1,0:T(8,128)(2,1)S(1)} %get-tuple-element.15.refs_0_), channel_id=1, source_target_pairs={{0,1},{1,0},{2,3},{3,2},{4,5},{5,4},{6,7},{7,6},{8,9},{9,8},{10,11... | collective-permute-start | bytes 1572872 | tf_op jit(solution)/shard_map/ppermute | solution.py:190
  20.7 9.0 %collective-permute-done.cross.refs_1_ = bf16[2,128,1024]{2,1,0:T(8,128)(2,1)S(1)} collective-permute-done((bf16[2,128,1024]{2,1,0:T(8,128)(2,1)S(1)}, bf16[2,128,1024]{2,1,0:T(8,128)(2,1)S(1)}, u32[]{:S(2)}, u32[]{:S(2)}) %collective-permute-start) | collective-permute-done | bytes 524320 | tf_op jit(solution)/shard_map/ppermute | solution.py:190
  29.7 1.9 %collective-permute-start.3 = (bf16[2,128,1024]{2,1,0:T(8,128)(2,1)S(1)}, bf16[2,128,1024]{2,1,0:T(8,128)(2,1)S(1)}, u32[]{:S(2)}, u32[]{:S(2)}) collective-permute-start(bf16[2,128,1024]{2,1,0:T(8,128)(2,1)S(1)} %shard_map.40), channel_id=1, source_target_pairs={{0,16},{16,0},{1,17},{17,1},{2,18},{18,2},{3,19},{19,3},{4,20},{20... | collective-permute-start | bytes 1572872 | tf_op jit(solution)/shard_map/ppermute | solution.py:190
  31.6 7.8 %collective-permute-done.2.refs_1_.refs_2_ = bf16[2,128,1024]{2,1,0:T(8,128)(2,1)S(1)} collective-permute-done((bf16[2,128,1024]{2,1,0:T(8,128)(2,1)S(1)}, bf16[2,128,1024]{2,1,0:T(8,128)(2,1)S(1)}, u32[]{:S(2)}, u32[]{:S(2)}) %collective-permute-start.2) | collective-permute-done | bytes 524320 | tf_op jit(solution)/shard_map/ppermute | solution.py:190
  39.4 0.0 collective-permute-done.1.refs_0_.refs_1_
  39.4 0.0 collective-permute-done.3.refs_3_
  39.4 0.8 copy-done.4
  40.2 0.0 all-to-all-done.feats.refs_2_
  40.2 1.0 copy-done.5
  41.3 0.7 shard_map.41
  42.0 1.9 %collective-permute-start.4 = (f32[2,512,128]{2,1,0:T(8,128)S(1)}, f32[2,512,128]{2,1,0:T(8,128)S(1)}, u32[]{:S(2)}, u32[]{:S(2)}) collective-permute-start(f32[2,512,128]{2,1,0:T(8,128)S(1)} %shard_map.41), channel_id=1, source_target_pairs={{0,16},{16,0},{1,17},{17,1},{2,18},{18,2},{3,19},{19,3},{4,20},{20... | collective-permute-start | bytes 1572872 | tf_op jit(solution)/shard_map/ppermute | solution.py:190
  43.9 0.7 shard_map.39
  44.7 1.1 collective-permute-done.4.came
  45.8 2.1 %collective-permute-start.5 = (f32[512,128]{1,0:T(8,128)S(1)}, f32[512,128]{1,0:T(8,128)S(1)}, u32[]{:S(2)}, u32[]{:S(2)}) collective-permute-start(f32[512,128]{1,0:T(8,128)S(1)} %fusion), channel_id=1, source_target_pairs={{0,256},{256,0},{1,257},{257,1},{2,258},{258,2},{3,259},{259,3},{4... | collective-permute-start | bytes 786440 | tf_op jit(solution)/shard_map/ppermute | solution.py:190
  47.9 9.6 %collective-permute-done.5.last = f32[512,128]{1,0:T(8,128)S(1)} collective-permute-done((f32[512,128]{1,0:T(8,128)S(1)}, f32[512,128]{1,0:T(8,128)S(1)}, u32[]{:S(2)}, u32[]{:S(2)}) %collective-permute-start.5) | collective-permute-done | bytes 262176 | tf_op jit(solution)/shard_map/ppermute | solution.py:190
  57.6 1.1 shard_map.42
  58.6 6.9 %all-to-all-start.1 = ((bf16[8,512,128]{2,1,0:T(8,128)(2,1)}), bf16[8,512,128]{2,1,0:T(8,128)(2,1)S(1)}, u32[]{:S(2)}, u32[]{:S(2)}) async-start(bf16[8,512,128]{2,1,0:T(8,128)(2,1)} %shard_map.42), calls=%async_computation.1 | async-start | bytes 2097152 | tf_op jit(solution)/shard_map/all_to_all | solution.py:194
  65.6 1.9 %collective-permute-start.6 = (bf16[2,128,1024]{2,1,0:T(8,128)(2,1)S(1)}, bf16[2,128,1024]{2,1,0:T(8,128)(2,1)S(1)}, u32[]{:S(2)}, u32[]{:S(2)}) collective-permute-start(bf16[2,128,1024]{2,1,0:T(8,128)(2,1)S(1)} %collective-permute-done.2.refs_1_.refs_2_), channel_id=1, source_target_pairs={{0,1},{1,0},{2,3},{3,2},{4,5},{5,4},{6,7},{7,6},{8,9},{9,8},{10,11... | collective-permute-start | bytes 1572872 | tf_op jit(solution)/shard_map/ppermute | solution.py:190
  67.5 0.1 shard_map.44
  67.6 1.9 %collective-permute-start.7 = (bf16[3,128,1024]{2,1,0:T(8,128)(2,1)S(1)}, bf16[3,128,1024]{2,1,0:T(8,128)(2,1)S(1)}, u32[]{:S(2)}, u32[]{:S(2)}) collective-permute-start(bf16[3,128,1024]{2,1,0:T(8,128)(2,1)S(1)} %shard_map.44), channel_id=1, source_target_pairs={{0,16},{16,0},{1,17},{17,1},{2,18},{18,2},{3,19},{19,3},{4,20},{20... | collective-permute-start | bytes 2359304 | tf_op jit(solution)/shard_map/ppermute | solution.py:190
  69.5 10.8 %collective-permute-done.6.refs_3_.refs_0_ = bf16[2,128,1024]{2,1,0:T(8,128)(2,1)S(1)} collective-permute-done((bf16[2,128,1024]{2,1,0:T(8,128)(2,1)S(1)}, bf16[2,128,1024]{2,1,0:T(8,128)(2,1)S(1)}, u32[]{:S(2)}, u32[]{:S(2)}) %collective-permute-start.6) | collective-permute-done | bytes 524320 | tf_op jit(solution)/shard_map/ppermute | solution.py:190
  80.3 1.9 %collective-permute-start.8 = (bf16[1,128,1024]{2,1,0:T(8,128)(2,1)S(1)}, bf16[1,128,1024]{2,1,0:T(8,128)(2,1)S(1)}, u32[]{:S(2)}, u32[]{:S(2)}) collective-permute-start(bf16[1,128,1024]{2,1,0:T(8,128)(2,1)S(1)} %shard_map.45), channel_id=1, source_target_pairs={{0,16},{16,0},{1,17},{17,1},{2,18},{18,2},{3,19},{19,3},{4,20},{20... | collective-permute-start | bytes 786440 | tf_op jit(solution)/shard_map/ppermute | solution.py:190
  82.3 1.5 %collective-permute-done.8.refs_1_ = bf16[1,128,1024]{2,1,0:T(8,128)(2,1)S(1)} collective-permute-done((bf16[1,128,1024]{2,1,0:T(8,128)(2,1)S(1)}, bf16[1,128,1024]{2,1,0:T(8,128)(2,1)S(1)}, u32[]{:S(2)}, u32[]{:S(2)}) %collective-permute-start.8) | collective-permute-done | bytes 262176 | tf_op jit(solution)/shard_map/ppermute | solution.py:190
  83.8 0.0 collective-permute-done.7.refs_0_
  83.8 0.9 copy-done.2
  84.7 9.1 %all-to-all-done.1.precond = bf16[8,512,128]{2,1,0:T(8,128)(2,1)S(1)} async-done(((bf16[8,512,128]{2,1,0:T(8,128)(2,1)}), bf16[8,512,128]{2,1,0:T(8,128)(2,1)S(1)}, u32[]{:S(2)}, u32[]{:S(2)}) %all-to-all-start.1) | async-done | bytes 1048608 | tf_op jit(solution)/shard_map/all_to_all | solution.py:194
  93.8 1.1 copy-done.3
  94.9 1.5 %shard_map.46 = f32[4,128,512]{2,1,0:T(8,128)S(1)} custom-call(bf16[8,512,128]{2,1,0:T(8,128)(2,1)S(1)} %all-to-all-done.1.precond, bf16[3,128,1024]{2,1,0:T(8,128)(2,1)S(1)} %copy-done.3, bf16[1,128,1024]{2,1,0:T(8,128)(2,1)S(1)} %collective-permute-done.8.refs_1_), custom_call_target="tpu_custom_call" | custom-call | flops 536870912 | bytes 3145728 | tf_op jit(solution)/shard_map/pallas_call | solution.py:25
  96.4 1.9 %collective-permute-start.9 = (f32[4,128,512]{2,1,0:T(8,128)S(1)}, f32[4,128,512]{2,1,0:T(8,128)S(1)}, u32[]{:S(2)}, u32[]{:S(2)}) collective-permute-start(f32[4,128,512]{2,1,0:T(8,128)S(1)} %shard_map.46), channel_id=1, source_target_pairs={{0,16},{16,0},{1,17},{17,1},{2,18},{18,2},{3,19},{19,3},{4,20},{20... | collective-permute-start | bytes 3145736 | tf_op jit(solution)/shard_map/ppermute | solution.py:190
  98.4 1.5 %shard_map.43.refs_0_ = f32[4,128,512]{2,1,0:T(8,128)S(1)} custom-call(bf16[8,512,128]{2,1,0:T(8,128)(2,1)S(1)} %all-to-all-done.1.precond, bf16[2,128,1024]{2,1,0:T(8,128)(2,1)S(1)} %get-tuple-element.15.refs_0_, bf16[2,128,1024]{2,1,0:T(8,128)(2,1)S(1)} %collective-permute-done.1.refs_0_.refs_1_, ...), custom_call_target="tpu_custom_call" | custom-call | flops 536870912 | bytes 4194304 | tf_op jit(solution)/shard_map/pallas_call | solution.py:25
  99.9 1.1 collective-permute-done.9.refs_1_
  101.0 0.6 shard_map.47
  101.6 28.5 %all_to_all.20 = bf16[32,16,512]{2,1,0:T(8,128)(2,1)S(1)} all-to-all(bf16[32,16,512]{2,1,0:T(8,128)(2,1)S(1)} %bitcast.16), channel_id=1, replica_groups=mesh['xh'=2,'y'=8,'core'=2,'z'=8,'xl'=2] {'xh','xl','z'}, dimensions={0} | all-to-all | bytes 1048576 | tf_op jit(solution)/shard_map/all_to_all | solution.py:194
  130.1 0.1 shard_map.48
  130.2 15.3 %all_to_all.21 = bf16[8,16,1024]{2,1,0:T(8,128)(2,1)S(1)} all-to-all(bf16[8,16,1024]{2,1,0:T(8,128)(2,1)S(1)} %shard_map.48), channel_id=1, replica_groups=mesh['xh'=2,'y'=8,'core'=2,'z'=8,'xl'=2] {'z'}, dimensions={0} | all-to-all | bytes 524288 | tf_op jit(solution)/shard_map/all_to_all | solution.py:194
  145.5 0.9 bitcast_convert_fusion
  (7 shorter events, 0.1 us)
Async XLA Ops:
  0.0 0.9 copy-start.6
  2.0 7.3 %copy-start = (bf16[1,128,4096]{2,1,0:T(8,128)(2,1)S(1)}, bf16[1,128,4096]{2,1,0:T(8,128)(2,1)}, u32[]{:S(2)}) copy-start(bf16[1,128,4096]{2,1,0:T(8,128)(2,1)} %param.5) | copy-start | bytes 3145732
  2.0 38.2 %all-to-all-start = ((bf16[8,512,128]{2,1,0:T(8,128)(2,1)}), bf16[8,512,128]{2,1,0:T(8,128)(2,1)S(1)}, u32[]{:S(2)}, u32[]{:S(2)}) async-start(bf16[8,512,128]{2,1,0:T(8,128)(2,1)} %shard_map.37), calls=%async_computation | async-start | bytes 2097152 | tf_op jit(solution)/shard_map/all_to_all | solution.py:194
  9.4 1.2 copy-start.1
  11.7 18.0 %collective-permute-start = (bf16[2,128,1024]{2,1,0:T(8,128)(2,1)S(1)}, bf16[2,128,1024]{2,1,0:T(8,128)(2,1)S(1)}, u32[]{:S(2)}, u32[]{:S(2)}) collective-permute-start(bf16[2,128,1024]{2,1,0:T(8,128)(2,1)S(1)} %get-tuple-element.13), channel_id=1, source_target_pairs={{0,257},{1,256},{256,1},{257,0},{2,259},{3,258},{258,3},{259,2},{4... | collective-permute-start | bytes 1572872 | tf_op jit(solution)/shard_map/ppermute | solution.py:190
  15.9 23.5 %collective-permute-start.2 = (bf16[2,128,1024]{2,1,0:T(8,128)(2,1)S(1)}, bf16[2,128,1024]{2,1,0:T(8,128)(2,1)S(1)}, u32[]{:S(2)}, u32[]{:S(2)}) collective-permute-start(bf16[2,128,1024]{2,1,0:T(8,128)(2,1)S(1)} %get-tuple-element.16), channel_id=1, source_target_pairs={{0,257},{1,256},{256,1},{257,0},{2,259},{3,258},{258,3},{259,2},{4... | collective-permute-start | bytes 1572872 | tf_op jit(solution)/shard_map/ppermute | solution.py:190
  18.8 20.7 %collective-permute-start.1 = (bf16[2,128,1024]{2,1,0:T(8,128)(2,1)S(1)}, bf16[2,128,1024]{2,1,0:T(8,128)(2,1)S(1)}, u32[]{:S(2)}, u32[]{:S(2)}) collective-permute-start(bf16[2,128,1024]{2,1,0:T(8,128)(2,1)S(1)} %get-tuple-element.15.refs_0_), channel_id=1, source_target_pairs={{0,1},{1,0},{2,3},{3,2},{4,5},{5,4},{6,7},{7,6},{8,9},{9,8},{10,11... | collective-permute-start | bytes 1572872 | tf_op jit(solution)/shard_map/ppermute | solution.py:190
  29.7 9.7 %collective-permute-start.3 = (bf16[2,128,1024]{2,1,0:T(8,128)(2,1)S(1)}, bf16[2,128,1024]{2,1,0:T(8,128)(2,1)S(1)}, u32[]{:S(2)}, u32[]{:S(2)}) collective-permute-start(bf16[2,128,1024]{2,1,0:T(8,128)(2,1)S(1)} %shard_map.40), channel_id=1, source_target_pairs={{0,16},{16,0},{1,17},{17,1},{2,18},{18,2},{3,19},{19,3},{4,20},{20... | collective-permute-start | bytes 1572872 | tf_op jit(solution)/shard_map/ppermute | solution.py:190
  39.4 0.8 copy-start.4
  40.2 1.0 copy-start.5
  42.0 3.8 %collective-permute-start.4 = (f32[2,512,128]{2,1,0:T(8,128)S(1)}, f32[2,512,128]{2,1,0:T(8,128)S(1)}, u32[]{:S(2)}, u32[]{:S(2)}) collective-permute-start(f32[2,512,128]{2,1,0:T(8,128)S(1)} %shard_map.41), channel_id=1, source_target_pairs={{0,16},{16,0},{1,17},{17,1},{2,18},{18,2},{3,19},{19,3},{4,20},{20... | collective-permute-start | bytes 1572872 | tf_op jit(solution)/shard_map/ppermute | solution.py:190
  45.8 11.7 %collective-permute-start.5 = (f32[512,128]{1,0:T(8,128)S(1)}, f32[512,128]{1,0:T(8,128)S(1)}, u32[]{:S(2)}, u32[]{:S(2)}) collective-permute-start(f32[512,128]{1,0:T(8,128)S(1)} %fusion), channel_id=1, source_target_pairs={{0,256},{256,0},{1,257},{257,1},{2,258},{258,2},{3,259},{259,3},{4... | collective-permute-start | bytes 786440 | tf_op jit(solution)/shard_map/ppermute | solution.py:190
  58.6 35.1 %all-to-all-start.1 = ((bf16[8,512,128]{2,1,0:T(8,128)(2,1)}), bf16[8,512,128]{2,1,0:T(8,128)(2,1)S(1)}, u32[]{:S(2)}, u32[]{:S(2)}) async-start(bf16[8,512,128]{2,1,0:T(8,128)(2,1)} %shard_map.42), calls=%async_computation.1 | async-start | bytes 2097152 | tf_op jit(solution)/shard_map/all_to_all | solution.py:194
  65.6 14.7 %collective-permute-start.6 = (bf16[2,128,1024]{2,1,0:T(8,128)(2,1)S(1)}, bf16[2,128,1024]{2,1,0:T(8,128)(2,1)S(1)}, u32[]{:S(2)}, u32[]{:S(2)}) collective-permute-start(bf16[2,128,1024]{2,1,0:T(8,128)(2,1)S(1)} %collective-permute-done.2.refs_1_.refs_2_), channel_id=1, source_target_pairs={{0,1},{1,0},{2,3},{3,2},{4,5},{5,4},{6,7},{7,6},{8,9},{9,8},{10,11... | collective-permute-start | bytes 1572872 | tf_op jit(solution)/shard_map/ppermute | solution.py:190
  67.6 16.2 %collective-permute-start.7 = (bf16[3,128,1024]{2,1,0:T(8,128)(2,1)S(1)}, bf16[3,128,1024]{2,1,0:T(8,128)(2,1)S(1)}, u32[]{:S(2)}, u32[]{:S(2)}) collective-permute-start(bf16[3,128,1024]{2,1,0:T(8,128)(2,1)S(1)} %shard_map.44), channel_id=1, source_target_pairs={{0,16},{16,0},{1,17},{17,1},{2,18},{18,2},{3,19},{19,3},{4,20},{20... | collective-permute-start | bytes 2359304 | tf_op jit(solution)/shard_map/ppermute | solution.py:190
  80.3 3.4 %collective-permute-start.8 = (bf16[1,128,1024]{2,1,0:T(8,128)(2,1)S(1)}, bf16[1,128,1024]{2,1,0:T(8,128)(2,1)S(1)}, u32[]{:S(2)}, u32[]{:S(2)}) collective-permute-start(bf16[1,128,1024]{2,1,0:T(8,128)(2,1)S(1)} %shard_map.45), channel_id=1, source_target_pairs={{0,16},{16,0},{1,17},{17,1},{2,18},{18,2},{3,19},{19,3},{4,20},{20... | collective-permute-start | bytes 786440 | tf_op jit(solution)/shard_map/ppermute | solution.py:190
  83.8 0.9 copy-start.2
  93.8 1.1 copy-start.3
  96.4 4.6 %collective-permute-start.9 = (f32[4,128,512]{2,1,0:T(8,128)S(1)}, f32[4,128,512]{2,1,0:T(8,128)S(1)}, u32[]{:S(2)}, u32[]{:S(2)}) collective-permute-start(f32[4,128,512]{2,1,0:T(8,128)S(1)} %shard_map.46), channel_id=1, source_target_pairs={{0,16},{16,0},{1,17},{17,1},{2,18},{18,2},{3,19},{19,3},{4,20},{20... | collective-permute-start | bytes 3145736 | tf_op jit(solution)/shard_map/ppermute | solution.py:190

commit v5 on v3

--- a/solution.py
+++ b/solution.py
@@ -37,8 +37,8 @@
     return jax.ShapeDtypeStruct(shape, dtype)
 
 
-def pack_body(ny, w, me, fisher, stored, f00, f01, f10, f11, own, other):
-    for x, outs in ((fisher, ((f00, f10), (f01, f11))), (stored, ([own.at[0], own.at[1]], [other.at[0], other.at[1]]))):
+def pack_body(ny, w, me, fisher, stored, f00, f01, f10, f11, near0, near1, far):
+    for x, outs in ((fisher, ((f00, f10), (f01, f11))), (stored, ((near0, near1), (far.at[0], far.at[1])))):
         for dc in range(2):
             for dx in range(2):
                 for y in range(ny):
@@ -48,26 +48,37 @@
 
 def pack(me, fisher, stored, ny, w):
     n, g = stored.shape[0], fisher.shape[0]
-    shapes = [like(g, ny * w)] * 4 + [like(2, n, ny * w)] * 2
+    shapes = [like(g, ny * w)] * 4 + [like(n, ny * w)] * 2 + [like(2, n, ny * w)]
     return call(functools.partial(pack_body, ny, w), shapes, [me, fisher, stored])
 
 
-def pair_body(near, came, same, cross):
-    for dx, out in enumerate((same, cross)):
-        out[0], out[1] = near[dx], came[dx]
-
-
-def pair(near, came):
-    return call(pair_body, [like(*near.shape)] * 2, [near, came])
-
-
-def copies_body(x, out):
-    for i in range(out.shape[0]):
-        out[i] = x[...]
+def part_body(near1, came, cross):
+    cross[0], cross[1] = near1[...], came[1]
+
+
+def part(near1, came):
+    return call(part_body, [like(*came.shape)], [near1, came])[0]
+
+
+def copies_body(x, out, block, came, sems):
+    load = pltpu.make_async_copy(x, block, came)
+    load.start()
+    load.wait()
+    moves = [pltpu.make_async_copy(block, out.at[i], sems.at[i]) for i in range(out.shape[0])]
+    for move in moves:
+        move.start()
+    for move in moves:
+        move.wait()
 
 
 def copies(x, n):
-    return call(copies_body, [like(n, *x.shape)], [x])[0]
+    return pl.pallas_call(
+        copies_body,
+        out_shape=like(n, *x.shape),
+        in_specs=[ANYWHERE],
+        out_specs=ANYWHERE,
+        scratch_shapes=[pltpu.VMEM(x.shape, BF16), pltpu.SemaphoreType.DMA, pltpu.SemaphoreType.DMA((n,))],
+    )(x)
 
 
 def settle_body(own, came, last, out):
@@ -120,54 +131,70 @@
     )[0]
 
 
-def score_body(dc, precond, b0, b1, b2, b3, out, held):
+def score_body(dc, same, side, precond, cross, twin, out, held, rows, sems):
+    loads = [
+        pltpu.make_async_copy(block if len(block.shape) == 2 else block.at[0], rows.at[i], sems.at[i])
+        for i, block in enumerate((same, side))
+    ]
+    for load in loads:
+        load.start()
     join(held, precond)
-    for i, block in enumerate((b0, b1, b2, b3)):
+    for i, block in ((2, cross), (3, twin)):
         out[i] = lax.dot_general(block[dc], held[...], NT, preferred_element_type=F32)
-
-
-def score(dc, precond, blocks):
+    for i, load in enumerate(loads):
+        load.wait()
+        out[i] = lax.dot_general(rows[i], held[...], NT, preferred_element_type=F32)
+
+
+def score(dc, precond, same, side, cross, twin):
     ny, q, w = precond.shape
-    n = blocks[0].shape[1]
-    return call(
+    n, k = side.shape
+    return pl.pallas_call(
         functools.partial(score_body, dc),
-        [like(4, n, q, dtype=F32)],
-        [precond, *blocks],
-        [pltpu.VMEM((q, ny * w), BF16)],
-        flops=2 * q * ny * w * 4 * n,
-    )[0]
-
-
-def meet_body(me, *refs):
-    terms, out = refs[:-1], refs[-1]
-    for h in range(len(terms) // 2):
-        own, came = terms[2 * h : 2 * h + 2]
-        q = own.shape[2]
-        for x in range(2):
-            for l in range(2):
-                i = (x ^ me[0]) * 2 + (l ^ me[2])
-                out[x * 2 + l, :, h * q : (h + 1) * q] = (own[i] + came[i]).astype(BF16)
-
-
-def meet(me, terms):
-    k, n, q = terms[0].shape
-    return call(meet_body, [like(k, n, q * (len(terms) // 2))], [me, *terms])[0]
+        out_shape=like(4, n, q, dtype=F32),
+        in_specs=[pl.BlockSpec(memory_space=pltpu.HBM)] * 2 + [WHOLE] * 3,
+        out_specs=WHOLE,
+        scratch_shapes=[pltpu.VMEM((q, k), BF16), pltpu.VMEM((2, n, k), BF16), pltpu.SemaphoreType.DMA((2,))],
+        compiler_params=PARAMS,
+        cost_estimate=pl.CostEstimate(flops=2 * q * k * 4 * n, bytes_accessed=4 * 1024 * 1024, transcendentals=0),
+    )(
+        pltpu.with_memory_space_constraint(same, pltpu.HBM),
+        pltpu.with_memory_space_constraint(side, pltpu.HBM),
+        precond,
+        cross,
+        twin,
+    )
+
+
+def meet_body(me, own, came, out):
+    nz, _, rows, _ = out.shape
+    for x in range(2):
+        for l in range(2):
+            i = (x ^ me[0]) * 2 + (l ^ me[2])
+            total = (own[i] + came[i]).astype(BF16)
+            for z in range(nz):
+                out[z, x * 2 + l] = total[z * rows : (z + 1) * rows]
+
+
+def meet(me, own, came, nz):
+    k, n, q = own.shape
+    return call(meet_body, [like(nz, k, n // nz, q)], [me, own, came])[0]
 
 
 def finish_body(factor, scores, out):
-    nx, nl, nz, rows, q = scores.shape
+    nz, nx, nl, rows, q = scores.shape
     for l in range(nl):
         total = jnp.zeros((rows, q), F32)
         for x in range(nx):
             for z in range(nz):
-                total += scores[x, l, z].astype(F32)
+                total += scores[z, x, l].astype(F32)
         total = (total * factor).astype(BF16)
         for z in range(nz):
             out[z, :, l * q : (l + 1) * q] = total
 
 
 def finish(scores, factor):
-    _, nl, nz, rows, q = scores.shape
+    nz, _, nl, rows, q = scores.shape
     return call(functools.partial(finish_body, factor), [like(nz, rows, nl * q)], [scores])[0]
 
 
@@ -188,19 +215,21 @@
     n, f = stored.shape
     q, w = query.shape
 
-    f00, f01, f10, f11, near, far = pack(me, fisher, stored, ny, w)
-    fish = (f00, swap(f10, "xh")), (swap(f01, "core"), swap(f11, "xh", "core"))
-    same, cross = pair(near, swap(far, "core"))
-    rows = [same, swap(same, "xl"), swap(cross, "xh"), swap(cross, "xh", "xl")]
+    f00, f01, f10, f11, near0, near1, far = pack(me, fisher, stored, ny, w)
+    fish = (f00, swap(f10, "xh", "xl")), (swap(f01, "core"), swap(f11, "xh", "core", "xl"))
+    came = swap(far, "core")
+    cross = part(near1, came)
+    side = swap(near0, "xl")
 
     feats = trade(copies(query, ny), "y")
-    came = swap(fold_far(feats, fish[1], (same, fish[0][1])), "core")
+    total = swap(fold_far(feats, fish[1], (cross, fish[0][1], side)), "core")
     own, own_x = fold(feats, fish[0])
-    precond = trade(settle(own, came, swap(own_x + came[1], "xh"), ny), "y")
-    came = swap(score(1, precond, rows), "core")
-    terms = [score(0, precond, rows), came]
-    scores = trade(meet(me, terms).reshape(2 * nl * nz, n // nz, q), "xh", "xl", "z")
-    total = finish(scores.reshape(2, nl, nz, n // nz, q), 1.0 / math.sqrt(nz * f))
+    precond = trade(settle(own, total, swap(own_x + total[1], "xh"), ny), "y")
+    twin, cross = swap(cross, "xh", "xl"), swap(cross, "xh")
+    far = swap(score(1, precond, came, swap(came[0], "xl"), cross, twin), "core")
+    terms = [score(0, precond, near0, side, cross, twin), far]
+    scores = trade(meet(me, *terms, nz).reshape(nz * 2 * nl, n // nz, q), "z", "xh", "xl")
+    total = finish(scores.reshape(nz, 2, nl, n // nz, q), 1.0 / math.sqrt(nz * f))
     return trade(total, "z").reshape(n, nl * q).astype(F32)
 
 

time: 143 us -> 141 us (0.986)
  waiting for transfers between devices: 46.4 us -> 43.1 us
  starting transfers between devices: 39.1 us -> 40.7 us
    pallas_call x0 -> x3, Pallas kernels: none -> 6.08 us  [the longest x2 4.11 us: score(): pl.pallas_call(functools.partial(score_body, dc), out_shape=like(4, n, q,...]
    pallas_call x10 -> x7, Pallas kernels: 9.34 us -> 4.38 us  [call(): pl.pallas_call(body, out_shape=[jax.ShapeDtypeStruct(s.shape, s.dtype) fo...]
    ppermute x10 -> x11, waiting for transfers between devices: 38.3 us -> 36 us  [swap(): return lax.ppermute(x, axes, [(i, n - 1 - i) for i in range(n)])]
    ppermute x10 -> x11, starting transfers between devices: 28.3 us -> 29.9 us  [swap(): return lax.ppermute(x, axes, [(i, n - 1 - i) for i in range(n)])]
  transfers between devices with their start and end apart: 12 -> 13, of which waited for: 8 -> 10; matrix products, arithmetic and copies ran while one was open for 0% -> 0% of each run, Pallas kernels for 3% -> 3%
where the time goes in v5:
time: 141 us; the launch traced here: 139 us
  blocking collectives  44 us (31%)
  waiting for transfers between devices  43.1 us (31%)
  starting transfers between devices  40.7 us (29%)
  Pallas kernels  10.5 us (7%)
    all_to_all x2, blocking collectives, trade(): return lax.all_to_all(x, axes, 0, 0, tiled=True)  44 us
    ppermute x11, waiting for transfers between devices, swap(): return lax.ppermute(x, axes, [(i, n - 1 - i) for i in range(n)])  36 us
    ppermute x11, starting transfers between devices, swap(): return lax.ppermute(x, axes, [(i, n - 1 - i) for i in range(n)])  29.9 us
    all_to_all x2, starting transfers between devices, trade(): return lax.all_to_all(x, axes, 0, 0, tiled=True)  10.8 us
    all_to_all x2, waiting for transfers between devices, trade(): return lax.all_to_all(x, axes, 0, 0, tiled=True)  7.08 us
    pallas_call x7, Pallas kernels, call(): pl.pallas_call(body, out_shape=[jax.ShapeDtypeStruct(s.shape, s.dtype) fo...  4.38 us
    pallas_call x2, Pallas kernels, score(): pl.pallas_call(functools.partial(score_body, dc), out_shape=like(4, n, q,...  4.11 us
  transfers between devices with their start and end apart: 13, of which 10 were waited for; matrix products, arithmetic and copies ran while one was open for 0% of the time, Pallas kernels for 3%

profile of v5, /device:TPU:6, one launch (start us, length us, event | category | flops | bytes accessed | tf_op | source)
XLA Modules:
  0.0 139.5 jit_solution(12040873935166940323)
XLA Ops:
  0.0 2.0 %shard_map.38 = bf16[8,512,128]{2,1,0:T(8,128)(2,1)} custom-call(bf16[512,128]{1,0:T(8,128)(2,1)} %bitcast.21), custom_call_target="tpu_custom_call" | custom-call | tf_op jit(solution)/shard_map/pallas_call | solution.py:75
  2.0 0.0 copy-start.2
  2.0 0.0 copy-start.3
  2.0 7.2 %all-to-all-start = ((bf16[8,512,128]{2,1,0:T(8,128)(2,1)}), bf16[8,512,128]{2,1,0:T(8,128)(2,1)S(1)}, u32[]{:S(2)}, u32[]{:S(2)}) async-start(bf16[8,512,128]{2,1,0:T(8,128)(2,1)} %shard_map.38), calls=%async_computation | async-start | bytes 2097152 | tf_op jit(solution)/shard_map/all_to_all | solution.py:208
  9.2 0.1 pad_add_fusion.me
  9.3 0.0 copy-done.2
  9.3 0.0 copy-done.3
  9.3 1.1 shard_map.37
  10.4 0.0 copy-start.4
  10.5 0.0 copy-start.5
  10.5 1.9 %collective-permute-start.2 = (bf16[2,128,1024]{2,1,0:T(8,128)(2,1)S(1)}, bf16[2,128,1024]{2,1,0:T(8,128)(2,1)S(1)}, u32[]{:S(2)}, u32[]{:S(2)}) collective-permute-start(bf16[2,128,1024]{2,1,0:T(8,128)(2,1)S(1)} %get-tuple-element.19), channel_id=1, source_target_pairs={{0,16},{16,0},{1,17},{17,1},{2,18},{18,2},{3,19},{19,3},{4,20},{20... | collective-permute-start | bytes 1572872 | tf_op jit(solution)/shard_map/ppermute | solution.py:204
  12.4 4.2 %collective-permute-start.1 = (bf16[128,1024]{1,0:T(8,128)(2,1)S(1)}, bf16[128,1024]{1,0:T(8,128)(2,1)S(1)}, u32[]{:S(2)}, u32[]{:S(2)}) collective-permute-start(bf16[128,1024]{1,0:T(8,128)(2,1)S(1)} %get-tuple-element.16), channel_id=1, source_target_pairs={{0,257},{1,256},{256,1},{257,0},{2,259},{3,258},{258,3},{259,2},{4... | collective-permute-start | bytes 786440 | tf_op jit(solution)/shard_map/ppermute | solution.py:204
  16.6 2.1 %collective-permute-start.3 = (bf16[128,1024]{1,0:T(8,128)(2,1)S(1)}, bf16[128,1024]{1,0:T(8,128)(2,1)S(1)}, u32[]{:S(2)}, u32[]{:S(2)}) collective-permute-start(bf16[128,1024]{1,0:T(8,128)(2,1)S(1)} %get-tuple-element.20), channel_id=1, source_target_pairs={{0,16},{16,0},{1,17},{17,1},{2,18},{18,2},{3,19},{19,3},{4,20},{20... | collective-permute-start | bytes 786440 | tf_op jit(solution)/shard_map/ppermute | solution.py:204
  18.8 2.7 %collective-permute-start.4 = (bf16[128,1024]{1,0:T(8,128)(2,1)S(1)}, bf16[128,1024]{1,0:T(8,128)(2,1)S(1)}, u32[]{:S(2)}, u32[]{:S(2)}) collective-permute-start(bf16[128,1024]{1,0:T(8,128)(2,1)S(1)} %get-tuple-element.21), channel_id=1, source_target_pairs={{0,273},{1,272},{16,257},{17,256},{256,17},{257,16},{272,1},{273,0... | collective-permute-start | bytes 786440 | tf_op jit(solution)/shard_map/ppermute | solution.py:204
  21.5 1.9 %collective-permute-start = (bf16[128,1024]{1,0:T(8,128)(2,1)S(1)}, bf16[128,1024]{1,0:T(8,128)(2,1)S(1)}, u32[]{:S(2)}, u32[]{:S(2)}) collective-permute-start(bf16[128,1024]{1,0:T(8,128)(2,1)S(1)} %get-tuple-element.14.same), channel_id=1, source_target_pairs={{0,1},{1,0},{2,3},{3,2},{4,5},{5,4},{6,7},{7,6},{8,9},{9,8},{10,11... | collective-permute-start | bytes 786440 | tf_op jit(solution)/shard_map/ppermute | solution.py:204
  23.4 0.0 collective-permute-done.2.came.same
  23.4 0.0 copy-start
  23.5 0.0 copy-done.4
  23.5 0.7 collective-permute-done.1.f1.refs_1_
  24.2 0.0 collective-permute-done.3.refs_4_
  24.2 5.9 %collective-permute-done.4.refs_5_ = bf16[128,1024]{1,0:T(8,128)(2,1)S(1)} collective-permute-done((bf16[128,1024]{1,0:T(8,128)(2,1)S(1)}, bf16[128,1024]{1,0:T(8,128)(2,1)S(1)}, u32[]{:S(2)}, u32[]{:S(2)}) %collective-permute-start.4) | collective-permute-done | bytes 262176 | tf_op jit(solution)/shard_map/ppermute | solution.py:204
  30.1 1.7 %collective-permute-done.refs_2_.side = bf16[128,1024]{1,0:T(8,128)(2,1)S(1)} collective-permute-done((bf16[128,1024]{1,0:T(8,128)(2,1)S(1)}, bf16[128,1024]{1,0:T(8,128)(2,1)S(1)}, u32[]{:S(2)}, u32[]{:S(2)}) %collective-permute-start) | collective-permute-done | bytes 262176 | tf_op jit(solution)/shard_map/ppermute | solution.py:204
  31.8 6.2 %all-to-all-done.feats.refs_3_ = bf16[8,512,128]{2,1,0:T(8,128)(2,1)S(1)} async-done(((bf16[8,512,128]{2,1,0:T(8,128)(2,1)}), bf16[8,512,128]{2,1,0:T(8,128)(2,1)S(1)}, u32[]{:S(2)}, u32[]{:S(2)}) %all-to-all-start) | async-done | bytes 1048608 | tf_op jit(solution)/shard_map/all_to_all | solution.py:208
  38.0 0.7 shard_map.41
  38.7 1.9 %collective-permute-start.5 = (f32[2,512,128]{2,1,0:T(8,128)S(1)}, f32[2,512,128]{2,1,0:T(8,128)S(1)}, u32[]{:S(2)}, u32[]{:S(2)}) collective-permute-start(f32[2,512,128]{2,1,0:T(8,128)S(1)} %shard_map.41), channel_id=1, source_target_pairs={{0,16},{16,0},{1,17},{17,1},{2,18},{18,2},{3,19},{19,3},{4,20},{20... | collective-permute-start | bytes 1572872 | tf_op jit(solution)/shard_map/ppermute | solution.py:204
  40.7 0.7 shard_map.39
  41.4 1.1 collective-permute-done.5.came
  42.6 3.3 %collective-permute-start.6 = (f32[512,128]{1,0:T(8,128)S(1)}, f32[512,128]{1,0:T(8,128)S(1)}, u32[]{:S(2)}, u32[]{:S(2)}) collective-permute-start(f32[512,128]{1,0:T(8,128)S(1)} %fusion), channel_id=1, source_target_pairs={{0,256},{256,0},{1,257},{257,1},{2,258},{258,2},{3,259},{259,3},{4... | collective-permute-start | bytes 786440 | tf_op jit(solution)/shard_map/ppermute | solution.py:204
  45.9 8.4 %collective-permute-done.6.last = f32[512,128]{1,0:T(8,128)S(1)} collective-permute-done((f32[512,128]{1,0:T(8,128)S(1)}, f32[512,128]{1,0:T(8,128)S(1)}, u32[]{:S(2)}, u32[]{:S(2)}) %collective-permute-start.6) | collective-permute-done | bytes 262176 | tf_op jit(solution)/shard_map/ppermute | solution.py:204
  54.3 1.1 shard_map.42
  55.4 3.6 %all-to-all-start.1 = ((bf16[8,512,128]{2,1,0:T(8,128)(2,1)}), bf16[8,512,128]{2,1,0:T(8,128)(2,1)S(1)}, u32[]{:S(2)}, u32[]{:S(2)}) async-start(bf16[8,512,128]{2,1,0:T(8,128)(2,1)} %shard_map.42), calls=%async_computation.1 | async-start | bytes 2097152 | tf_op jit(solution)/shard_map/all_to_all | solution.py:208
  58.9 2.4 %collective-permute-start.8 = (bf16[2,128,1024]{2,1,0:T(8,128)(2,1)S(1)}, bf16[2,128,1024]{2,1,0:T(8,128)(2,1)S(1)}, u32[]{:S(2)}, u32[]{:S(2)}) collective-permute-start(bf16[2,128,1024]{2,1,0:T(8,128)(2,1)S(1)} %shard_map.40.refs_0_), channel_id=1, source_target_pairs={{0,257},{1,256},{256,1},{257,0},{2,259},{3,258},{258,3},{259,2},{4... | collective-permute-start | bytes 1572872 | tf_op jit(solution)/shard_map/ppermute | solution.py:204
  61.3 4.3 %collective-permute-start.7 = (bf16[2,128,1024]{2,1,0:T(8,128)(2,1)S(1)}, bf16[2,128,1024]{2,1,0:T(8,128)(2,1)S(1)}, u32[]{:S(2)}, u32[]{:S(2)}) collective-permute-start(bf16[2,128,1024]{2,1,0:T(8,128)(2,1)S(1)} %shard_map.40.refs_0_), channel_id=1, source_target_pairs={{0,256},{256,0},{1,257},{257,1},{2,258},{258,2},{3,259},{259,3},{4... | collective-permute-start | bytes 1572872 | tf_op jit(solution)/shard_map/ppermute | solution.py:204
  65.7 3.1 %collective-permute-start.9 = (bf16[128,1024]{1,0:T(8,128)(2,1)S(1)}, bf16[128,1024]{1,0:T(8,128)(2,1)S(1)}, u32[]{:S(2)}, u32[]{:S(2)}) collective-permute-start(bf16[128,1024]{1,0:T(8,128)(2,1)S(1)} %slice_bitcast_fusion), channel_id=1, source_target_pairs={{0,1},{1,0},{2,3},{3,2},{4,5},{5,4},{6,7},{7,6},{8,9},{9,8},{10,11... | collective-permute-start | bytes 786440 | tf_op jit(solution)/shard_map/ppermute | solution.py:204
  68.8 14.5 %collective-permute-done.9.side = bf16[128,1024]{1,0:T(8,128)(2,1)S(1)} collective-permute-done((bf16[128,1024]{1,0:T(8,128)(2,1)S(1)}, bf16[128,1024]{1,0:T(8,128)(2,1)S(1)}, u32[]{:S(2)}, u32[]{:S(2)}) %collective-permute-start.9) | collective-permute-done | bytes 262176 | tf_op jit(solution)/shard_map/ppermute | solution.py:204
  83.3 3.1 %collective-permute-done.8.twin = bf16[2,128,1024]{2,1,0:T(8,128)(2,1)S(1)} collective-permute-done((bf16[2,128,1024]{2,1,0:T(8,128)(2,1)S(1)}, bf16[2,128,1024]{2,1,0:T(8,128)(2,1)S(1)}, u32[]{:S(2)}, u32[]{:S(2)}) %collective-permute-start.8) | collective-permute-done | bytes 524320 | tf_op jit(solution)/shard_map/ppermute | solution.py:204
  86.4 0.0 collective-permute-done.7.cross
  86.4 0.9 all-to-all-done.1.precond
  87.3 0.0 copy-done.7
  87.3 2.1 %shard_map.44 = f32[4,128,512]{2,1,0:T(8,128)S(1)} custom-call(bf16[2,128,1024]{2,1,0:T(8,128)(2,1)} %copy-done, bf16[128,1024]{1,0:T(8,128)(2,1)} %copy-done.7, bf16[8,512,128]{2,1,0:T(8,128)(2,1)S(1)} %all-to-all-done.1.precond, bf16[2,128,1024]{2,1,0:T(8,128)(2,1)S(1)} %collective-permute-done.7.cross, bf16[2,128,1024]{2,1,0:T(8,128)(2,1)S(1)} %collective-permute-done.8.twin), custom_call_target="tpu_custom_call" | custom-call | flops 536870912 | bytes 4194304 | tf_op jit(solution)/shard_map/pallas_call | solution.py:152
  89.4 1.9 %collective-permute-start.10 = (f32[4,128,512]{2,1,0:T(8,128)S(1)}, f32[4,128,512]{2,1,0:T(8,128)S(1)}, u32[]{:S(2)}, u32[]{:S(2)}) collective-permute-start(f32[4,128,512]{2,1,0:T(8,128)S(1)} %shard_map.44), channel_id=1, source_target_pairs={{0,16},{16,0},{1,17},{17,1},{2,18},{18,2},{3,19},{19,3},{4,20},{20... | collective-permute-start | bytes 3145736 | tf_op jit(solution)/shard_map/ppermute | solution.py:204
  91.3 2.1 %shard_map.43.own = f32[4,128,512]{2,1,0:T(8,128)S(1)} custom-call(bf16[128,1024]{1,0:T(8,128)(2,1)} %copy-done.4, bf16[128,1024]{1,0:T(8,128)(2,1)} %copy-done.1, bf16[8,512,128]{2,1,0:T(8,128)(2,1)S(1)} %all-to-all-done.1.precond, bf16[2,128,1024]{2,1,0:T(8,128)(2,1)S(1)} %collective-permute-done.7.cross, bf16[2,128,1024]{2,1,0:T(8,128)(2,1)S(1)} %collective-permute-done.8.twin), custom_call_target="tpu_custom_call" | custom-call | flops 536870912 | bytes 4194304 | tf_op jit(solution)/shard_map/pallas_call | solution.py:152
  93.4 0.6 collective-permute-done.10.came
  94.0 0.6 shard_map.45
  94.6 30.3 %all_to_all.20 = bf16[32,16,512]{2,1,0:T(8,128)(2,1)S(1)} all-to-all(bf16[32,16,512]{2,1,0:T(8,128)(2,1)S(1)} %bitcast.18), channel_id=1, replica_groups=mesh['xh'=2,'y'=8,'core'=2,'z'=8,'xl'=2] {'z','xh','xl'}, dimensions={0} | all-to-all | bytes 1048576 | tf_op jit(solution)/shard_map/all_to_all | solution.py:208
  124.9 0.1 shard_map.46
  125.0 13.6 %all_to_all.21 = bf16[8,16,1024]{2,1,0:T(8,128)(2,1)S(1)} all-to-all(bf16[8,16,1024]{2,1,0:T(8,128)(2,1)S(1)} %shard_map.46), channel_id=1, replica_groups=mesh['xh'=2,'y'=8,'core'=2,'z'=8,'xl'=2] {'z'}, dimensions={0} | all-to-all | bytes 524288 | tf_op jit(solution)/shard_map/all_to_all | solution.py:208
  138.6 0.9 bitcast_convert_fusion
  (10 shorter events, 0.1 us)
Async XLA Ops:
  2.0 7.3 %copy-start.2 = (bf16[1,128,4096]{2,1,0:T(8,128)(2,1)S(1)}, bf16[1,128,4096]{2,1,0:T(8,128)(2,1)}, u32[]{:S(2)}) copy-start(bf16[1,128,4096]{2,1,0:T(8,128)(2,1)} %param.5) | copy-start | bytes 3145732
  2.0 7.3 %copy-start.3 = (bf16[128,1,4096]{2,0,1:T(8,128)(2,1)S(1)}, bf16[128,1,4096]{2,0,1:T(8,128)(2,1)}, u32[]{:S(2)}) copy-start(bf16[128,1,4096]{2,0,1:T(8,128)(2,1)} %param.3) | copy-start | bytes 3145732
  2.0 36.0 %all-to-all-start = ((bf16[8,512,128]{2,1,0:T(8,128)(2,1)}), bf16[8,512,128]{2,1,0:T(8,128)(2,1)S(1)}, u32[]{:S(2)}, u32[]{:S(2)}) async-start(bf16[8,512,128]{2,1,0:T(8,128)(2,1)} %shard_map.38), calls=%async_computation | async-start | bytes 2097152 | tf_op jit(solution)/shard_map/all_to_all | solution.py:208
  10.4 13.0 %copy-start.4 = (bf16[128,1024]{1,0:T(8,128)(2,1)}, bf16[128,1024]{1,0:T(8,128)(2,1)S(1)}, u32[]{:S(2)}) copy-start(bf16[128,1024]{1,0:T(8,128)(2,1)S(1)} %get-tuple-element.14.same) | copy-start | bytes 786436
  10.5 13.0 %copy-start.5 = (bf16[128,1024]{1,0:T(8,128)(2,1)}, bf16[128,1024]{1,0:T(8,128)(2,1)S(1)}, u32[]{:S(2)}) copy-start(bf16[128,1024]{1,0:T(8,128)(2,1)S(1)} %get-tuple-element.15.f0) | copy-start | bytes 786436
  10.5 13.0 %collective-permute-start.2 = (bf16[2,128,1024]{2,1,0:T(8,128)(2,1)S(1)}, bf16[2,128,1024]{2,1,0:T(8,128)(2,1)S(1)}, u32[]{:S(2)}, u32[]{:S(2)}) collective-permute-start(bf16[2,128,1024]{2,1,0:T(8,128)(2,1)S(1)} %get-tuple-element.19), channel_id=1, source_target_pairs={{0,16},{16,0},{1,17},{17,1},{2,18},{18,2},{3,19},{19,3},{4,20},{20... | collective-permute-start | bytes 1572872 | tf_op jit(solution)/shard_map/ppermute | solution.py:204
  12.4 11.8 %collective-permute-start.1 = (bf16[128,1024]{1,0:T(8,128)(2,1)S(1)}, bf16[128,1024]{1,0:T(8,128)(2,1)S(1)}, u32[]{:S(2)}, u32[]{:S(2)}) collective-permute-start(bf16[128,1024]{1,0:T(8,128)(2,1)S(1)} %get-tuple-element.16), channel_id=1, source_target_pairs={{0,257},{1,256},{256,1},{257,0},{2,259},{3,258},{258,3},{259,2},{4... | collective-permute-start | bytes 786440 | tf_op jit(solution)/shard_map/ppermute | solution.py:204
  16.6 7.6 %collective-permute-start.3 = (bf16[128,1024]{1,0:T(8,128)(2,1)S(1)}, bf16[128,1024]{1,0:T(8,128)(2,1)S(1)}, u32[]{:S(2)}, u32[]{:S(2)}) collective-permute-start(bf16[128,1024]{1,0:T(8,128)(2,1)S(1)} %get-tuple-element.20), channel_id=1, source_target_pairs={{0,16},{16,0},{1,17},{17,1},{2,18},{18,2},{3,19},{19,3},{4,20},{20... | collective-permute-start | bytes 786440 | tf_op jit(solution)/shard_map/ppermute | solution.py:204
  18.8 11.3 %collective-permute-start.4 = (bf16[128,1024]{1,0:T(8,128)(2,1)S(1)}, bf16[128,1024]{1,0:T(8,128)(2,1)S(1)}, u32[]{:S(2)}, u32[]{:S(2)}) collective-permute-start(bf16[128,1024]{1,0:T(8,128)(2,1)S(1)} %get-tuple-element.21), channel_id=1, source_target_pairs={{0,273},{1,272},{16,257},{17,256},{256,17},{257,16},{272,1},{273,0... | collective-permute-start | bytes 786440 | tf_op jit(solution)/shard_map/ppermute | solution.py:204
  21.5 10.3 %collective-permute-start = (bf16[128,1024]{1,0:T(8,128)(2,1)S(1)}, bf16[128,1024]{1,0:T(8,128)(2,1)S(1)}, u32[]{:S(2)}, u32[]{:S(2)}) collective-permute-start(bf16[128,1024]{1,0:T(8,128)(2,1)S(1)} %get-tuple-element.14.same), channel_id=1, source_target_pairs={{0,1},{1,0},{2,3},{3,2},{4,5},{5,4},{6,7},{7,6},{8,9},{9,8},{10,11... | collective-permute-start | bytes 786440 | tf_op jit(solution)/shard_map/ppermute | solution.py:204
  23.4 42.2 %copy-start = (bf16[2,128,1024]{2,1,0:T(8,128)(2,1)}, bf16[2,128,1024]{2,1,0:T(8,128)(2,1)S(1)}, u32[]{:S(2)}) copy-start(bf16[2,128,1024]{2,1,0:T(8,128)(2,1)S(1)} %collective-permute-done.2.came.same) | copy-start | bytes 1572868
  31.8 6.9 %copy-start.1 = (bf16[128,1024]{1,0:T(8,128)(2,1)}, bf16[128,1024]{1,0:T(8,128)(2,1)S(1)}, u32[]{:S(2)}) copy-start(bf16[128,1024]{1,0:T(8,128)(2,1)S(1)} %collective-permute-done.refs_2_.side) | copy-start | bytes 786436
  38.0 2.7 %copy-start.6 = (bf16[128,1024]{1,0:T(8,128)(2,1)S(1)}, bf16[128,1024]{1,0:T(8,128)(2,1)}, u32[]{:S(2)}) copy-start(bf16[128,1024]{1,0:T(8,128)(2,1)} %copy-done.5) | copy-start | bytes 786436
  38.7 3.8 %collective-permute-start.5 = (f32[2,512,128]{2,1,0:T(8,128)S(1)}, f32[2,512,128]{2,1,0:T(8,128)S(1)}, u32[]{:S(2)}, u32[]{:S(2)}) collective-permute-start(f32[2,512,128]{2,1,0:T(8,128)S(1)} %shard_map.41), channel_id=1, source_target_pairs={{0,16},{16,0},{1,17},{17,1},{2,18},{18,2},{3,19},{19,3},{4,20},{20... | collective-permute-start | bytes 1572872 | tf_op jit(solution)/shard_map/ppermute | solution.py:204
  42.6 11.7 %collective-permute-start.6 = (f32[512,128]{1,0:T(8,128)S(1)}, f32[512,128]{1,0:T(8,128)S(1)}, u32[]{:S(2)}, u32[]{:S(2)}) collective-permute-start(f32[512,128]{1,0:T(8,128)S(1)} %fusion), channel_id=1, source_target_pairs={{0,256},{256,0},{1,257},{257,1},{2,258},{258,2},{3,259},{259,3},{4... | collective-permute-start | bytes 786440 | tf_op jit(solution)/shard_map/ppermute | solution.py:204
  55.4 32.0 %all-to-all-start.1 = ((bf16[8,512,128]{2,1,0:T(8,128)(2,1)}), bf16[8,512,128]{2,1,0:T(8,128)(2,1)S(1)}, u32[]{:S(2)}, u32[]{:S(2)}) async-start(bf16[8,512,128]{2,1,0:T(8,128)(2,1)} %shard_map.42), calls=%async_computation.1 | async-start | bytes 2097152 | tf_op jit(solution)/shard_map/all_to_all | solution.py:208
  58.9 27.5 %collective-permute-start.8 = (bf16[2,128,1024]{2,1,0:T(8,128)(2,1)S(1)}, bf16[2,128,1024]{2,1,0:T(8,128)(2,1)S(1)}, u32[]{:S(2)}, u32[]{:S(2)}) collective-permute-start(bf16[2,128,1024]{2,1,0:T(8,128)(2,1)S(1)} %shard_map.40.refs_0_), channel_id=1, source_target_pairs={{0,257},{1,256},{256,1},{257,0},{2,259},{3,258},{258,3},{259,2},{4... | collective-permute-start | bytes 1572872 | tf_op jit(solution)/shard_map/ppermute | solution.py:204
  61.3 25.1 %collective-permute-start.7 = (bf16[2,128,1024]{2,1,0:T(8,128)(2,1)S(1)}, bf16[2,128,1024]{2,1,0:T(8,128)(2,1)S(1)}, u32[]{:S(2)}, u32[]{:S(2)}) collective-permute-start(bf16[2,128,1024]{2,1,0:T(8,128)(2,1)S(1)} %shard_map.40.refs_0_), channel_id=1, source_target_pairs={{0,256},{256,0},{1,257},{257,1},{2,258},{258,2},{3,259},{259,3},{4... | collective-permute-start | bytes 1572872 | tf_op jit(solution)/shard_map/ppermute | solution.py:204
  65.7 17.6 %collective-permute-start.9 = (bf16[128,1024]{1,0:T(8,128)(2,1)S(1)}, bf16[128,1024]{1,0:T(8,128)(2,1)S(1)}, u32[]{:S(2)}, u32[]{:S(2)}) collective-permute-start(bf16[128,1024]{1,0:T(8,128)(2,1)S(1)} %slice_bitcast_fusion), channel_id=1, source_target_pairs={{0,1},{1,0},{2,3},{3,2},{4,5},{5,4},{6,7},{7,6},{8,9},{9,8},{10,11... | collective-permute-start | bytes 786440 | tf_op jit(solution)/shard_map/ppermute | solution.py:204
  83.3 4.0 %copy-start.7 = (bf16[128,1024]{1,0:T(8,128)(2,1)}, bf16[128,1024]{1,0:T(8,128)(2,1)S(1)}, u32[]{:S(2)}) copy-start(bf16[128,1024]{1,0:T(8,128)(2,1)S(1)} %collective-permute-done.9.side) | copy-start | bytes 786436
  89.4 4.6 %collective-permute-start.10 = (f32[4,128,512]{2,1,0:T(8,128)S(1)}, f32[4,128,512]{2,1,0:T(8,128)S(1)}, u32[]{:S(2)}, u32[]{:S(2)}) collective-permute-start(f32[4,128,512]{2,1,0:T(8,128)S(1)} %shard_map.44), channel_id=1, source_target_pairs={{0,16},{16,0},{1,17},{17,1},{2,18},{18,2},{3,19},{19,3},{4,20},{20... | collective-permute-start | bytes 3145736 | tf_op jit(solution)/shard_map/ppermute | solution.py:204

commit v6 on v5

--- a/solution.py
+++ b/solution.py
@@ -131,26 +131,41 @@
     )[0]
 
 
-def score_body(dc, same, side, precond, cross, twin, out, held, rows, sems):
-    loads = [
-        pltpu.make_async_copy(block if len(block.shape) == 2 else block.at[0], rows.at[i], sems.at[i])
-        for i, block in enumerate((same, side))
-    ]
+def score_far_body(precond, same, side, cross, twin, out, held):
+    join(held, precond)
+    for i, rows in enumerate((same, side, cross.at[1], twin.at[1])):
+        out[i] = lax.dot_general(rows[...], held[...], NT, preferred_element_type=F32)
+
+
+def score_far(precond, *blocks):
+    ny, q, w = precond.shape
+    n, k = blocks[0].shape
+    return call(
+        score_far_body,
+        [like(4, n, q, dtype=F32)],
+        [precond, *blocks],
+        [pltpu.VMEM((q, k), BF16)],
+        flops=2 * q * k * 4 * n,
+    )[0]
+
+
+def score_body(same, side, precond, cross, twin, out, held, rows, sems):
+    loads = [pltpu.make_async_copy(block, rows.at[i], sems.at[i]) for i, block in enumerate((same, side))]
     for load in loads:
         load.start()
     join(held, precond)
     for i, block in ((2, cross), (3, twin)):
-        out[i] = lax.dot_general(block[dc], held[...], NT, preferred_element_type=F32)
+        out[i] = lax.dot_general(block[0], held[...], NT, preferred_element_type=F32)
     for i, load in enumerate(loads):
         load.wait()
         out[i] = lax.dot_general(rows[i], held[...], NT, preferred_element_type=F32)
 
 
-def score(dc, precond, same, side, cross, twin):
+def score(precond, same, side, cross, twin):
     ny, q, w = precond.shape
     n, k = side.shape
     return pl.pallas_call(
-        functools.partial(score_body, dc),
+        score_body,
         out_shape=like(4, n, q, dtype=F32),
         in_specs=[pl.BlockSpec(memory_space=pltpu.HBM)] * 2 + [WHOLE] * 3,
         out_specs=WHOLE,
@@ -166,6 +181,23 @@
     )
 
 
+def fetch_body(came, out, sem):
+    load = pltpu.make_async_copy(came.at[0], out, sem)
+    load.start()
+    load.wait()
+
+
+def fetch(came, after):
+    return pl.pallas_call(
+        lambda _, *refs: fetch_body(*refs),
+        out_shape=like(*came.shape[1:]),
+        in_specs=[ANYWHERE, pl.BlockSpec(memory_space=pltpu.HBM)],
+        out_specs=WHOLE,
+        scratch_shapes=[pltpu.SemaphoreType.DMA],
+        compiler_params=PARAMS,
+    )(after, pltpu.with_memory_space_constraint(came, pltpu.HBM))
+
+
 def meet_body(me, own, came, out):
     nz, _, rows, _ = out.shape
     for x in range(2):
@@ -224,10 +256,11 @@
     feats = trade(copies(query, ny), "y")
     total = swap(fold_far(feats, fish[1], (cross, fish[0][1], side)), "core")
     own, own_x = fold(feats, fish[0])
-    precond = trade(settle(own, total, swap(own_x + total[1], "xh"), ny), "y")
+    full = settle(own, total, swap(own_x + total[1], "xh"), ny)
+    precond = trade(full, "y")
     twin, cross = swap(cross, "xh", "xl"), swap(cross, "xh")
-    far = swap(score(1, precond, came, swap(came[0], "xl"), cross, twin), "core")
-    terms = [score(0, precond, near0, side, cross, twin), far]
+    far = swap(score_far(precond, fetch(came, full), swap(came[0], "xl"), cross, twin), "core")
+    terms = [score(precond, near0, side, cross, twin), far]
     scores = trade(meet(me, *terms, nz).reshape(nz * 2 * nl, n // nz, q), "z", "xh", "xl")
     total = finish(scores.reshape(nz, 2, nl, n // nz, q), 1.0 / math.sqrt(nz * f))
     return trade(total, "z").reshape(n, nl * q).astype(F32)

time: 141 us -> 140 us (level)
    pallas_call x7 -> x8, Pallas kernels: 4.38 us -> 5.97 us  [call(): pl.pallas_call(body, out_shape=[jax.ShapeDtypeStruct(s.shape, s.dtype) fo...]
  transfers between devices with their start and end apart: 13 -> 13, of which waited for: 10 -> 10; matrix products, arithmetic and copies ran while one was open for 0% -> 0% of each run, Pallas kernels for 3% -> 4%
where the time goes in v6:
time: 140 us; the launch traced here: 139 us
  blocking collectives  44 us (31%)
  waiting for transfers between devices  42.1 us (30%)
  starting transfers between devices  40.7 us (29%)
  Pallas kernels  11 us (8%)
    all_to_all x2, blocking collectives, trade(): return lax.all_to_all(x, axes, 0, 0, tiled=True)  44 us
    ppermute x11, waiting for transfers between devices, swap(): return lax.ppermute(x, axes, [(i, n - 1 - i) for i in range(n)])  35.1 us
    ppermute x11, starting transfers between devices, swap(): return lax.ppermute(x, axes, [(i, n - 1 - i) for i in range(n)])  29.9 us
    all_to_all x2, starting transfers between devices, trade(): return lax.all_to_all(x, axes, 0, 0, tiled=True)  10.8 us
    all_to_all x2, waiting for transfers between devices, trade(): return lax.all_to_all(x, axes, 0, 0, tiled=True)  7.08 us
    pallas_call x8, Pallas kernels, call(): pl.pallas_call(body, out_shape=[jax.ShapeDtypeStruct(s.shape, s.dtype) fo...  5.97 us
  transfers between devices with their start and end apart: 13, of which 10 were waited for; matrix products, arithmetic and copies ran while one was open for 0% of the time, Pallas kernels for 4%

profile of v6, /device:TPU:6, one launch (start us, length us, event | category | flops | bytes accessed | tf_op | source)
XLA Modules:
  0.0 139.0 jit_solution(3392573762442103455)
XLA Ops:
  0.0 2.0 %shard_map.38 = bf16[8,512,128]{2,1,0:T(8,128)(2,1)} custom-call(bf16[512,128]{1,0:T(8,128)(2,1)} %bitcast.21), custom_call_target="tpu_custom_call" | custom-call | tf_op jit(solution)/shard_map/pallas_call | solution.py:75
  2.0 0.0 copy-start.2
  2.0 0.0 copy-start.3
  2.0 7.2 %all-to-all-start = ((bf16[8,512,128]{2,1,0:T(8,128)(2,1)}), bf16[8,512,128]{2,1,0:T(8,128)(2,1)S(1)}, u32[]{:S(2)}, u32[]{:S(2)}) async-start(bf16[8,512,128]{2,1,0:T(8,128)(2,1)} %shard_map.38), calls=%async_computation | async-start | bytes 2097152 | tf_op jit(solution)/shard_map/all_to_all | solution.py:240
  9.3 0.1 pad_add_fusion.me
  9.3 0.0 copy-done.2
  9.3 0.0 copy-done.3
  9.3 1.1 shard_map.37
  10.4 0.0 copy-start.4
  10.5 0.0 copy-start.5
  10.5 1.9 %collective-permute-start.2 = (bf16[2,128,1024]{2,1,0:T(8,128)(2,1)S(1)}, bf16[2,128,1024]{2,1,0:T(8,128)(2,1)S(1)}, u32[]{:S(2)}, u32[]{:S(2)}) collective-permute-start(bf16[2,128,1024]{2,1,0:T(8,128)(2,1)S(1)} %get-tuple-element.19), channel_id=1, source_target_pairs={{0,16},{16,0},{1,17},{17,1},{2,18},{18,2},{3,19},{19,3},{4,20},{20... | collective-permute-start | bytes 1572872 | tf_op jit(solution)/shard_map/ppermute | solution.py:236
  12.4 4.2 %collective-permute-start.1 = (bf16[128,1024]{1,0:T(8,128)(2,1)S(1)}, bf16[128,1024]{1,0:T(8,128)(2,1)S(1)}, u32[]{:S(2)}, u32[]{:S(2)}) collective-permute-start(bf16[128,1024]{1,0:T(8,128)(2,1)S(1)} %get-tuple-element.16), channel_id=1, source_target_pairs={{0,257},{1,256},{256,1},{257,0},{2,259},{3,258},{258,3},{259,2},{4... | collective-permute-start | bytes 786440 | tf_op jit(solution)/shard_map/ppermute | solution.py:236
  16.6 2.1 %collective-permute-start.3 = (bf16[128,1024]{1,0:T(8,128)(2,1)S(1)}, bf16[128,1024]{1,0:T(8,128)(2,1)S(1)}, u32[]{:S(2)}, u32[]{:S(2)}) collective-permute-start(bf16[128,1024]{1,0:T(8,128)(2,1)S(1)} %get-tuple-element.20), channel_id=1, source_target_pairs={{0,16},{16,0},{1,17},{17,1},{2,18},{18,2},{3,19},{19,3},{4,20},{20... | collective-permute-start | bytes 786440 | tf_op jit(solution)/shard_map/ppermute | solution.py:236
  18.8 2.7 %collective-permute-start.4 = (bf16[128,1024]{1,0:T(8,128)(2,1)S(1)}, bf16[128,1024]{1,0:T(8,128)(2,1)S(1)}, u32[]{:S(2)}, u32[]{:S(2)}) collective-permute-start(bf16[128,1024]{1,0:T(8,128)(2,1)S(1)} %get-tuple-element.21), channel_id=1, source_target_pairs={{0,273},{1,272},{16,257},{17,256},{256,17},{257,16},{272,1},{273,0... | collective-permute-start | bytes 786440 | tf_op jit(solution)/shard_map/ppermute | solution.py:236
  21.5 1.9 %collective-permute-start = (bf16[128,1024]{1,0:T(8,128)(2,1)S(1)}, bf16[128,1024]{1,0:T(8,128)(2,1)S(1)}, u32[]{:S(2)}, u32[]{:S(2)}) collective-permute-start(bf16[128,1024]{1,0:T(8,128)(2,1)S(1)} %get-tuple-element.14.same), channel_id=1, source_target_pairs={{0,1},{1,0},{2,3},{3,2},{4,5},{5,4},{6,7},{7,6},{8,9},{9,8},{10,11... | collective-permute-start | bytes 786440 | tf_op jit(solution)/shard_map/ppermute | solution.py:236
  23.4 0.0 collective-permute-done.2.came.refs_0_
  23.4 0.0 copy-start
  23.5 0.0 copy-done.4
  23.5 0.7 collective-permute-done.1.f1.refs_1_
  24.2 0.0 collective-permute-done.3.refs_4_
  24.2 5.9 %collective-permute-done.4.refs_5_ = bf16[128,1024]{1,0:T(8,128)(2,1)S(1)} collective-permute-done((bf16[128,1024]{1,0:T(8,128)(2,1)S(1)}, bf16[128,1024]{1,0:T(8,128)(2,1)S(1)}, u32[]{:S(2)}, u32[]{:S(2)}) %collective-permute-start.4) | collective-permute-done | bytes 262176 | tf_op jit(solution)/shard_map/ppermute | solution.py:236
  30.1 1.7 %collective-permute-done.refs_2_.side = bf16[128,1024]{1,0:T(8,128)(2,1)S(1)} collective-permute-done((bf16[128,1024]{1,0:T(8,128)(2,1)S(1)}, bf16[128,1024]{1,0:T(8,128)(2,1)S(1)}, u32[]{:S(2)}, u32[]{:S(2)}) %collective-permute-start) | collective-permute-done | bytes 262176 | tf_op jit(solution)/shard_map/ppermute | solution.py:236
  31.8 6.2 %all-to-all-done.feats.refs_3_ = bf16[8,512,128]{2,1,0:T(8,128)(2,1)S(1)} async-done(((bf16[8,512,128]{2,1,0:T(8,128)(2,1)}), bf16[8,512,128]{2,1,0:T(8,128)(2,1)S(1)}, u32[]{:S(2)}, u32[]{:S(2)}) %all-to-all-start) | async-done | bytes 1048608 | tf_op jit(solution)/shard_map/all_to_all | solution.py:240
  38.0 0.7 shard_map.41
  38.7 1.9 %collective-permute-start.5 = (f32[2,512,128]{2,1,0:T(8,128)S(1)}, f32[2,512,128]{2,1,0:T(8,128)S(1)}, u32[]{:S(2)}, u32[]{:S(2)}) collective-permute-start(f32[2,512,128]{2,1,0:T(8,128)S(1)} %shard_map.41), channel_id=1, source_target_pairs={{0,16},{16,0},{1,17},{17,1},{2,18},{18,2},{3,19},{19,3},{4,20},{20... | collective-permute-start | bytes 1572872 | tf_op jit(solution)/shard_map/ppermute | solution.py:236
  40.7 0.7 shard_map.39
  41.4 1.1 collective-permute-done.5.came
  42.6 3.3 %collective-permute-start.6 = (f32[512,128]{1,0:T(8,128)S(1)}, f32[512,128]{1,0:T(8,128)S(1)}, u32[]{:S(2)}, u32[]{:S(2)}) collective-permute-start(f32[512,128]{1,0:T(8,128)S(1)} %fusion), channel_id=1, source_target_pairs={{0,256},{256,0},{1,257},{257,1},{2,258},{258,2},{3,259},{259,3},{4... | collective-permute-start | bytes 786440 | tf_op jit(solution)/shard_map/ppermute | solution.py:236
  45.9 8.4 %collective-permute-done.6.last = f32[512,128]{1,0:T(8,128)S(1)} collective-permute-done((f32[512,128]{1,0:T(8,128)S(1)}, f32[512,128]{1,0:T(8,128)S(1)}, u32[]{:S(2)}, u32[]{:S(2)}) %collective-permute-start.6) | collective-permute-done | bytes 262176 | tf_op jit(solution)/shard_map/ppermute | solution.py:236
  54.3 1.1 shard_map.42._
  55.4 3.6 %all-to-all-start.1 = ((bf16[8,512,128]{2,1,0:T(8,128)(2,1)}), bf16[8,512,128]{2,1,0:T(8,128)(2,1)S(1)}, u32[]{:S(2)}, u32[]{:S(2)}) async-start(bf16[8,512,128]{2,1,0:T(8,128)(2,1)} %shard_map.42._), calls=%async_computation.1 | async-start | bytes 2097152 | tf_op jit(solution)/shard_map/all_to_all | solution.py:240
  58.9 2.4 %collective-permute-start.8 = (bf16[2,128,1024]{2,1,0:T(8,128)(2,1)S(1)}, bf16[2,128,1024]{2,1,0:T(8,128)(2,1)S(1)}, u32[]{:S(2)}, u32[]{:S(2)}) collective-permute-start(bf16[2,128,1024]{2,1,0:T(8,128)(2,1)S(1)} %shard_map.40.refs_0_), channel_id=1, source_target_pairs={{0,257},{1,256},{256,1},{257,0},{2,259},{3,258},{258,3},{259,2},{4... | collective-permute-start | bytes 1572872 | tf_op jit(solution)/shard_map/ppermute | solution.py:236
  61.3 4.3 %collective-permute-start.7 = (bf16[2,128,1024]{2,1,0:T(8,128)(2,1)S(1)}, bf16[2,128,1024]{2,1,0:T(8,128)(2,1)S(1)}, u32[]{:S(2)}, u32[]{:S(2)}) collective-permute-start(bf16[2,128,1024]{2,1,0:T(8,128)(2,1)S(1)} %shard_map.40.refs_0_), channel_id=1, source_target_pairs={{0,256},{256,0},{1,257},{257,1},{2,258},{258,2},{3,259},{259,3},{4... | collective-permute-start | bytes 1572872 | tf_op jit(solution)/shard_map/ppermute | solution.py:236
  65.7 3.1 %collective-permute-start.9 = (bf16[128,1024]{1,0:T(8,128)(2,1)S(1)}, bf16[128,1024]{1,0:T(8,128)(2,1)S(1)}, u32[]{:S(2)}, u32[]{:S(2)}) collective-permute-start(bf16[128,1024]{1,0:T(8,128)(2,1)S(1)} %slice_bitcast_fusion), channel_id=1, source_target_pairs={{0,1},{1,0},{2,3},{3,2},{4,5},{5,4},{6,7},{7,6},{8,9},{9,8},{10,11... | collective-permute-start | bytes 786440 | tf_op jit(solution)/shard_map/ppermute | solution.py:236
  68.8 1.0 shard_map.44.same
  69.8 13.5 %collective-permute-done.9.side = bf16[128,1024]{1,0:T(8,128)(2,1)S(1)} collective-permute-done((bf16[128,1024]{1,0:T(8,128)(2,1)S(1)}, bf16[128,1024]{1,0:T(8,128)(2,1)S(1)}, u32[]{:S(2)}, u32[]{:S(2)}) %collective-permute-start.9) | collective-permute-done | bytes 262176 | tf_op jit(solution)/shard_map/ppermute | solution.py:236
  83.3 3.1 %collective-permute-done.8.twin = bf16[2,128,1024]{2,1,0:T(8,128)(2,1)S(1)} collective-permute-done((bf16[2,128,1024]{2,1,0:T(8,128)(2,1)S(1)}, bf16[2,128,1024]{2,1,0:T(8,128)(2,1)S(1)}, u32[]{:S(2)}, u32[]{:S(2)}) %collective-permute-start.8) | collective-permute-done | bytes 524320 | tf_op jit(solution)/shard_map/ppermute | solution.py:236
  86.4 0.0 collective-permute-done.7.cross
  86.4 0.9 all-to-all-done.1.precond
  87.3 1.6 %shard_map.45 = f32[4,128,512]{2,1,0:T(8,128)S(1)} custom-call(bf16[8,512,128]{2,1,0:T(8,128)(2,1)S(1)} %all-to-all-done.1.precond, bf16[128,1024]{1,0:T(8,128)(2,1)S(1)} %shard_map.44.same, bf16[128,1024]{1,0:T(8,128)(2,1)S(1)} %collective-permute-done.9.side, bf16[2,128,1024]{2,1,0:T(8,128)(2,1)S(1)} %collective-permute-done.7.cross, ...), custom_call_target="tpu_custom_call" | custom-call | flops 536870912 | bytes 3670016 | tf_op jit(solution)/shard_map/pallas_call | solution.py:25
  88.9 1.9 %collective-permute-start.10 = (f32[4,128,512]{2,1,0:T(8,128)S(1)}, f32[4,128,512]{2,1,0:T(8,128)S(1)}, u32[]{:S(2)}, u32[]{:S(2)}) collective-permute-start(f32[4,128,512]{2,1,0:T(8,128)S(1)} %shard_map.45), channel_id=1, source_target_pairs={{0,16},{16,0},{1,17},{17,1},{2,18},{18,2},{3,19},{19,3},{4,20},{20... | collective-permute-start | bytes 3145736 | tf_op jit(solution)/shard_map/ppermute | solution.py:236
  90.9 2.1 %shard_map.43.own = f32[4,128,512]{2,1,0:T(8,128)S(1)} custom-call(bf16[128,1024]{1,0:T(8,128)(2,1)} %copy-done.4, bf16[128,1024]{1,0:T(8,128)(2,1)} %copy-done.1, bf16[8,512,128]{2,1,0:T(8,128)(2,1)S(1)} %all-to-all-done.1.precond, bf16[2,128,1024]{2,1,0:T(8,128)(2,1)S(1)} %collective-permute-done.7.cross, bf16[2,128,1024]{2,1,0:T(8,128)(2,1)S(1)} %collective-permute-done.8.twin), custom_call_target="tpu_custom_call" | custom-call | flops 536870912 | bytes 4194304 | tf_op jit(solution)/shard_map/pallas_call | solution.py:167
  92.9 0.6 collective-permute-done.10.came
  93.5 0.6 shard_map.46
  94.1 30.3 %all_to_all.20 = bf16[32,16,512]{2,1,0:T(8,128)(2,1)S(1)} all-to-all(bf16[32,16,512]{2,1,0:T(8,128)(2,1)S(1)} %bitcast.18), channel_id=1, replica_groups=mesh['xh'=2,'y'=8,'core'=2,'z'=8,'xl'=2] {'z','xh','xl'}, dimensions={0} | all-to-all | bytes 1048576 | tf_op jit(solution)/shard_map/all_to_all | solution.py:240
  124.5 0.1 shard_map.47
  124.6 13.6 %all_to_all.21 = bf16[8,16,1024]{2,1,0:T(8,128)(2,1)S(1)} all-to-all(bf16[8,16,1024]{2,1,0:T(8,128)(2,1)S(1)} %shard_map.47), channel_id=1, replica_groups=mesh['xh'=2,'y'=8,'core'=2,'z'=8,'xl'=2] {'z'}, dimensions={0} | all-to-all | bytes 524288 | tf_op jit(solution)/shard_map/all_to_all | solution.py:240
  138.2 0.9 bitcast_convert_fusion
  (9 shorter events, 0.1 us)
Async XLA Ops:
  2.0 7.3 %copy-start.2 = (bf16[1,128,4096]{2,1,0:T(8,128)(2,1)S(1)}, bf16[1,128,4096]{2,1,0:T(8,128)(2,1)}, u32[]{:S(2)}) copy-start(bf16[1,128,4096]{2,1,0:T(8,128)(2,1)} %param.5) | copy-start | bytes 3145732
  2.0 7.3 %copy-start.3 = (bf16[128,1,4096]{2,0,1:T(8,128)(2,1)S(1)}, bf16[128,1,4096]{2,0,1:T(8,128)(2,1)}, u32[]{:S(2)}) copy-start(bf16[128,1,4096]{2,0,1:T(8,128)(2,1)} %param.3) | copy-start | bytes 3145732
  2.0 36.0 %all-to-all-start = ((bf16[8,512,128]{2,1,0:T(8,128)(2,1)}), bf16[8,512,128]{2,1,0:T(8,128)(2,1)S(1)}, u32[]{:S(2)}, u32[]{:S(2)}) async-start(bf16[8,512,128]{2,1,0:T(8,128)(2,1)} %shard_map.38), calls=%async_computation | async-start | bytes 2097152 | tf_op jit(solution)/shard_map/all_to_all | solution.py:240
  10.4 13.0 %copy-start.4 = (bf16[128,1024]{1,0:T(8,128)(2,1)}, bf16[128,1024]{1,0:T(8,128)(2,1)S(1)}, u32[]{:S(2)}) copy-start(bf16[128,1024]{1,0:T(8,128)(2,1)S(1)} %get-tuple-element.14.same) | copy-start | bytes 786436
  10.5 13.0 %copy-start.5 = (bf16[128,1024]{1,0:T(8,128)(2,1)}, bf16[128,1024]{1,0:T(8,128)(2,1)S(1)}, u32[]{:S(2)}) copy-start(bf16[128,1024]{1,0:T(8,128)(2,1)S(1)} %get-tuple-element.15.f0) | copy-start | bytes 786436
  10.5 13.0 %collective-permute-start.2 = (bf16[2,128,1024]{2,1,0:T(8,128)(2,1)S(1)}, bf16[2,128,1024]{2,1,0:T(8,128)(2,1)S(1)}, u32[]{:S(2)}, u32[]{:S(2)}) collective-permute-start(bf16[2,128,1024]{2,1,0:T(8,128)(2,1)S(1)} %get-tuple-element.19), channel_id=1, source_target_pairs={{0,16},{16,0},{1,17},{17,1},{2,18},{18,2},{3,19},{19,3},{4,20},{20... | collective-permute-start | bytes 1572872 | tf_op jit(solution)/shard_map/ppermute | solution.py:236
  12.4 11.8 %collective-permute-start.1 = (bf16[128,1024]{1,0:T(8,128)(2,1)S(1)}, bf16[128,1024]{1,0:T(8,128)(2,1)S(1)}, u32[]{:S(2)}, u32[]{:S(2)}) collective-permute-start(bf16[128,1024]{1,0:T(8,128)(2,1)S(1)} %get-tuple-element.16), channel_id=1, source_target_pairs={{0,257},{1,256},{256,1},{257,0},{2,259},{3,258},{258,3},{259,2},{4... | collective-permute-start | bytes 786440 | tf_op jit(solution)/shard_map/ppermute | solution.py:236
  16.6 7.6 %collective-permute-start.3 = (bf16[128,1024]{1,0:T(8,128)(2,1)S(1)}, bf16[128,1024]{1,0:T(8,128)(2,1)S(1)}, u32[]{:S(2)}, u32[]{:S(2)}) collective-permute-start(bf16[128,1024]{1,0:T(8,128)(2,1)S(1)} %get-tuple-element.20), channel_id=1, source_target_pairs={{0,16},{16,0},{1,17},{17,1},{2,18},{18,2},{3,19},{19,3},{4,20},{20... | collective-permute-start | bytes 786440 | tf_op jit(solution)/shard_map/ppermute | solution.py:236
  18.8 11.3 %collective-permute-start.4 = (bf16[128,1024]{1,0:T(8,128)(2,1)S(1)}, bf16[128,1024]{1,0:T(8,128)(2,1)S(1)}, u32[]{:S(2)}, u32[]{:S(2)}) collective-permute-start(bf16[128,1024]{1,0:T(8,128)(2,1)S(1)} %get-tuple-element.21), channel_id=1, source_target_pairs={{0,273},{1,272},{16,257},{17,256},{256,17},{257,16},{272,1},{273,0... | collective-permute-start | bytes 786440 | tf_op jit(solution)/shard_map/ppermute | solution.py:236
  21.5 10.3 %collective-permute-start = (bf16[128,1024]{1,0:T(8,128)(2,1)S(1)}, bf16[128,1024]{1,0:T(8,128)(2,1)S(1)}, u32[]{:S(2)}, u32[]{:S(2)}) collective-permute-start(bf16[128,1024]{1,0:T(8,128)(2,1)S(1)} %get-tuple-element.14.same), channel_id=1, source_target_pairs={{0,1},{1,0},{2,3},{3,2},{4,5},{5,4},{6,7},{7,6},{8,9},{9,8},{10,11... | collective-permute-start | bytes 786440 | tf_op jit(solution)/shard_map/ppermute | solution.py:236
  23.4 42.2 %copy-start = (bf16[2,128,1024]{2,1,0:T(8,128)(2,1)}, bf16[2,128,1024]{2,1,0:T(8,128)(2,1)S(1)}, u32[]{:S(2)}) copy-start(bf16[2,128,1024]{2,1,0:T(8,128)(2,1)S(1)} %collective-permute-done.2.came.refs_0_) | copy-start | bytes 1572868
  31.8 6.9 %copy-start.1 = (bf16[128,1024]{1,0:T(8,128)(2,1)}, bf16[128,1024]{1,0:T(8,128)(2,1)S(1)}, u32[]{:S(2)}) copy-start(bf16[128,1024]{1,0:T(8,128)(2,1)S(1)} %collective-permute-done.refs_2_.side) | copy-start | bytes 786436
  38.0 2.7 %copy-start.6 = (bf16[128,1024]{1,0:T(8,128)(2,1)S(1)}, bf16[128,1024]{1,0:T(8,128)(2,1)}, u32[]{:S(2)}) copy-start(bf16[128,1024]{1,0:T(8,128)(2,1)} %copy-done.5) | copy-start | bytes 786436
  38.7 3.8 %collective-permute-start.5 = (f32[2,512,128]{2,1,0:T(8,128)S(1)}, f32[2,512,128]{2,1,0:T(8,128)S(1)}, u32[]{:S(2)}, u32[]{:S(2)}) collective-permute-start(f32[2,512,128]{2,1,0:T(8,128)S(1)} %shard_map.41), channel_id=1, source_target_pairs={{0,16},{16,0},{1,17},{17,1},{2,18},{18,2},{3,19},{19,3},{4,20},{20... | collective-permute-start | bytes 1572872 | tf_op jit(solution)/shard_map/ppermute | solution.py:236
  42.6 11.7 %collective-permute-start.6 = (f32[512,128]{1,0:T(8,128)S(1)}, f32[512,128]{1,0:T(8,128)S(1)}, u32[]{:S(2)}, u32[]{:S(2)}) collective-permute-start(f32[512,128]{1,0:T(8,128)S(1)} %fusion), channel_id=1, source_target_pairs={{0,256},{256,0},{1,257},{257,1},{2,258},{258,2},{3,259},{259,3},{4... | collective-permute-start | bytes 786440 | tf_op jit(solution)/shard_map/ppermute | solution.py:236
  55.4 32.0 %all-to-all-start.1 = ((bf16[8,512,128]{2,1,0:T(8,128)(2,1)}), bf16[8,512,128]{2,1,0:T(8,128)(2,1)S(1)}, u32[]{:S(2)}, u32[]{:S(2)}) async-start(bf16[8,512,128]{2,1,0:T(8,128)(2,1)} %shard_map.42._), calls=%async_computation.1 | async-start | bytes 2097152 | tf_op jit(solution)/shard_map/all_to_all | solution.py:240
  58.9 27.5 %collective-permute-start.8 = (bf16[2,128,1024]{2,1,0:T(8,128)(2,1)S(1)}, bf16[2,128,1024]{2,1,0:T(8,128)(2,1)S(1)}, u32[]{:S(2)}, u32[]{:S(2)}) collective-permute-start(bf16[2,128,1024]{2,1,0:T(8,128)(2,1)S(1)} %shard_map.40.refs_0_), channel_id=1, source_target_pairs={{0,257},{1,256},{256,1},{257,0},{2,259},{3,258},{258,3},{259,2},{4... | collective-permute-start | bytes 1572872 | tf_op jit(solution)/shard_map/ppermute | solution.py:236
  61.3 25.1 %collective-permute-start.7 = (bf16[2,128,1024]{2,1,0:T(8,128)(2,1)S(1)}, bf16[2,128,1024]{2,1,0:T(8,128)(2,1)S(1)}, u32[]{:S(2)}, u32[]{:S(2)}) collective-permute-start(bf16[2,128,1024]{2,1,0:T(8,128)(2,1)S(1)} %shard_map.40.refs_0_), channel_id=1, source_target_pairs={{0,256},{256,0},{1,257},{257,1},{2,258},{258,2},{3,259},{259,3},{4... | collective-permute-start | bytes 1572872 | tf_op jit(solution)/shard_map/ppermute | solution.py:236
  65.7 17.6 %collective-permute-start.9 = (bf16[128,1024]{1,0:T(8,128)(2,1)S(1)}, bf16[128,1024]{1,0:T(8,128)(2,1)S(1)}, u32[]{:S(2)}, u32[]{:S(2)}) collective-permute-start(bf16[128,1024]{1,0:T(8,128)(2,1)S(1)} %slice_bitcast_fusion), channel_id=1, source_target_pairs={{0,1},{1,0},{2,3},{3,2},{4,5},{5,4},{6,7},{7,6},{8,9},{9,8},{10,11... | collective-permute-start | bytes 786440 | tf_op jit(solution)/shard_map/ppermute | solution.py:236
  88.9 4.6 %collective-permute-start.10 = (f32[4,128,512]{2,1,0:T(8,128)S(1)}, f32[4,128,512]{2,1,0:T(8,128)S(1)}, u32[]{:S(2)}, u32[]{:S(2)}) collective-permute-start(f32[4,128,512]{2,1,0:T(8,128)S(1)} %shard_map.45), channel_id=1, source_target_pairs={{0,16},{16,0},{1,17},{17,1},{2,18},{18,2},{3,19},{19,3},{4,20},{20... | collective-permute-start | bytes 3145736 | tf_op jit(solution)/shard_map/ppermute | solution.py:236

commit v7 on v6

--- a/solution.py
+++ b/solution.py
@@ -236,8 +236,8 @@
     return lax.ppermute(x, axes, [(i, n - 1 - i) for i in range(n)])
 
 
-def trade(x, *axes):
-    return lax.all_to_all(x, axes, 0, 0, tiled=True)
+def trade(x, *axes, groups=None):
+    return lax.all_to_all(x, axes, 0, 0, axis_index_groups=groups, tiled=True)
 
 
 def shards(stored, query, fisher):
@@ -261,9 +261,10 @@
     twin, cross = swap(cross, "xh", "xl"), swap(cross, "xh")
     far = swap(score_far(precond, fetch(came, full), swap(came[0], "xl"), cross, twin), "core")
     terms = [score(precond, near0, side, cross, twin), far]
-    scores = trade(meet(me, *terms, nz).reshape(nz * 2 * nl, n // nz, q), "z", "xh", "xl")
+    last_first = [[z * 2 * nl + x for z in reversed(range(nz)) for x in range(2 * nl)]]
+    scores = trade(meet(me, *terms, nz).reshape(nz * 2 * nl, n // nz, q), "z", "xh", "xl", groups=last_first)
     total = finish(scores.reshape(nz, 2, nl, n // nz, q), 1.0 / math.sqrt(nz * f))
-    return trade(total, "z").reshape(n, nl * q).astype(F32)
+    return trade(total, "z", groups=[list(reversed(range(nz)))]).reshape(n, nl * q).astype(F32)
 
 
 def solution(mesh):

time: 140 us -> 137 us (0.979)
  blocking collectives: 44 us -> 41 us
    all_to_all x2, blocking collectives: 44 us -> 41 us  [trade(): return lax.all_to_all(x, axes, 0, 0, axis_index_groups=groups, tiled=True)]
where the time goes in v7:
time: 137 us; the launch traced here: 136 us
  waiting for transfers between devices  42.1 us (31%)
  blocking collectives  41 us (30%)
  starting transfers between devices  40.7 us (30%)
  Pallas kernels  11 us (8%)
    all_to_all x2, blocking collectives, trade(): return lax.all_to_all(x, axes, 0, 0, axis_index_groups=groups, tiled=True)  41 us
    ppermute x11, waiting for transfers between devices, swap(): return lax.ppermute(x, axes, [(i, n - 1 - i) for i in range(n)])  35.1 us
    ppermute x11, starting transfers between devices, swap(): return lax.ppermute(x, axes, [(i, n - 1 - i) for i in range(n)])  29.9 us
    all_to_all x2, starting transfers between devices, trade(): return lax.all_to_all(x, axes, 0, 0, axis_index_groups=groups, tiled=True)  10.8 us
    all_to_all x2, waiting for transfers between devices, trade(): return lax.all_to_all(x, axes, 0, 0, axis_index_groups=groups, tiled=True)  7.08 us
    pallas_call x8, Pallas kernels, call(): pl.pallas_call(body, out_shape=[jax.ShapeDtypeStruct(s.shape, s.dtype) fo...  5.97 us
  transfers between devices with their start and end apart: 13, of which 10 were waited for; matrix products, arithmetic and copies ran while one was open for 0% of the time, Pallas kernels for 4%

profile of v7, /device:TPU:6, one launch (start us, length us, event | category | flops | bytes accessed | tf_op | source)
XLA Modules:
  0.0 136.1 jit_solution(4303954003496292478)
XLA Ops:
  0.0 2.0 %shard_map.38 = bf16[8,512,128]{2,1,0:T(8,128)(2,1)} custom-call(bf16[512,128]{1,0:T(8,128)(2,1)} %bitcast.21), custom_call_target="tpu_custom_call" | custom-call | tf_op jit(solution)/shard_map/pallas_call | solution.py:75
  2.0 0.0 copy-start.2
  2.0 0.0 copy-start.3
  2.0 7.2 %all-to-all-start = ((bf16[8,512,128]{2,1,0:T(8,128)(2,1)}), bf16[8,512,128]{2,1,0:T(8,128)(2,1)S(1)}, u32[]{:S(2)}, u32[]{:S(2)}) async-start(bf16[8,512,128]{2,1,0:T(8,128)(2,1)} %shard_map.38), calls=%async_computation | async-start | bytes 2097152 | tf_op jit(solution)/shard_map/all_to_all | solution.py:240
  9.3 0.1 pad_add_fusion.me
  9.3 0.0 copy-done.2
  9.3 0.0 copy-done.3
  9.3 1.1 shard_map.37
  10.4 0.0 copy-start.4
  10.5 0.0 copy-start.5
  10.5 1.9 %collective-permute-start.2 = (bf16[2,128,1024]{2,1,0:T(8,128)(2,1)S(1)}, bf16[2,128,1024]{2,1,0:T(8,128)(2,1)S(1)}, u32[]{:S(2)}, u32[]{:S(2)}) collective-permute-start(bf16[2,128,1024]{2,1,0:T(8,128)(2,1)S(1)} %get-tuple-element.19), channel_id=1, source_target_pairs={{0,16},{16,0},{1,17},{17,1},{2,18},{18,2},{3,19},{19,3},{4,20},{20... | collective-permute-start | bytes 1572872 | tf_op jit(solution)/shard_map/ppermute | solution.py:236
  12.4 4.2 %collective-permute-start.1 = (bf16[128,1024]{1,0:T(8,128)(2,1)S(1)}, bf16[128,1024]{1,0:T(8,128)(2,1)S(1)}, u32[]{:S(2)}, u32[]{:S(2)}) collective-permute-start(bf16[128,1024]{1,0:T(8,128)(2,1)S(1)} %get-tuple-element.16), channel_id=1, source_target_pairs={{0,257},{1,256},{256,1},{257,0},{2,259},{3,258},{258,3},{259,2},{4... | collective-permute-start | bytes 786440 | tf_op jit(solution)/shard_map/ppermute | solution.py:236
  16.6 2.1 %collective-permute-start.3 = (bf16[128,1024]{1,0:T(8,128)(2,1)S(1)}, bf16[128,1024]{1,0:T(8,128)(2,1)S(1)}, u32[]{:S(2)}, u32[]{:S(2)}) collective-permute-start(bf16[128,1024]{1,0:T(8,128)(2,1)S(1)} %get-tuple-element.20), channel_id=1, source_target_pairs={{0,16},{16,0},{1,17},{17,1},{2,18},{18,2},{3,19},{19,3},{4,20},{20... | collective-permute-start | bytes 786440 | tf_op jit(solution)/shard_map/ppermute | solution.py:236
  18.8 2.7 %collective-permute-start.4 = (bf16[128,1024]{1,0:T(8,128)(2,1)S(1)}, bf16[128,1024]{1,0:T(8,128)(2,1)S(1)}, u32[]{:S(2)}, u32[]{:S(2)}) collective-permute-start(bf16[128,1024]{1,0:T(8,128)(2,1)S(1)} %get-tuple-element.21), channel_id=1, source_target_pairs={{0,273},{1,272},{16,257},{17,256},{256,17},{257,16},{272,1},{273,0... | collective-permute-start | bytes 786440 | tf_op jit(solution)/shard_map/ppermute | solution.py:236
  21.5 1.9 %collective-permute-start = (bf16[128,1024]{1,0:T(8,128)(2,1)S(1)}, bf16[128,1024]{1,0:T(8,128)(2,1)S(1)}, u32[]{:S(2)}, u32[]{:S(2)}) collective-permute-start(bf16[128,1024]{1,0:T(8,128)(2,1)S(1)} %get-tuple-element.14.same), channel_id=1, source_target_pairs={{0,1},{1,0},{2,3},{3,2},{4,5},{5,4},{6,7},{7,6},{8,9},{9,8},{10,11... | collective-permute-start | bytes 786440 | tf_op jit(solution)/shard_map/ppermute | solution.py:236
  23.4 0.0 collective-permute-done.2.came.refs_0_
  23.4 0.0 copy-start
  23.5 0.0 copy-done.4
  23.5 0.7 collective-permute-done.1.f1.refs_1_
  24.2 0.0 collective-permute-done.3.refs_4_
  24.2 5.9 %collective-permute-done.4.refs_5_ = bf16[128,1024]{1,0:T(8,128)(2,1)S(1)} collective-permute-done((bf16[128,1024]{1,0:T(8,128)(2,1)S(1)}, bf16[128,1024]{1,0:T(8,128)(2,1)S(1)}, u32[]{:S(2)}, u32[]{:S(2)}) %collective-permute-start.4) | collective-permute-done | bytes 262176 | tf_op jit(solution)/shard_map/ppermute | solution.py:236
  30.1 1.7 %collective-permute-done.refs_2_.side = bf16[128,1024]{1,0:T(8,128)(2,1)S(1)} collective-permute-done((bf16[128,1024]{1,0:T(8,128)(2,1)S(1)}, bf16[128,1024]{1,0:T(8,128)(2,1)S(1)}, u32[]{:S(2)}, u32[]{:S(2)}) %collective-permute-start) | collective-permute-done | bytes 262176 | tf_op jit(solution)/shard_map/ppermute | solution.py:236
  31.8 6.2 %all-to-all-done.feats.refs_3_ = bf16[8,512,128]{2,1,0:T(8,128)(2,1)S(1)} async-done(((bf16[8,512,128]{2,1,0:T(8,128)(2,1)}), bf16[8,512,128]{2,1,0:T(8,128)(2,1)S(1)}, u32[]{:S(2)}, u32[]{:S(2)}) %all-to-all-start) | async-done | bytes 1048608 | tf_op jit(solution)/shard_map/all_to_all | solution.py:240
  38.0 0.7 shard_map.41
  38.7 1.9 %collective-permute-start.5 = (f32[2,512,128]{2,1,0:T(8,128)S(1)}, f32[2,512,128]{2,1,0:T(8,128)S(1)}, u32[]{:S(2)}, u32[]{:S(2)}) collective-permute-start(f32[2,512,128]{2,1,0:T(8,128)S(1)} %shard_map.41), channel_id=1, source_target_pairs={{0,16},{16,0},{1,17},{17,1},{2,18},{18,2},{3,19},{19,3},{4,20},{20... | collective-permute-start | bytes 1572872 | tf_op jit(solution)/shard_map/ppermute | solution.py:236
  40.7 0.7 shard_map.39
  41.4 1.1 collective-permute-done.5.came
  42.6 3.3 %collective-permute-start.6 = (f32[512,128]{1,0:T(8,128)S(1)}, f32[512,128]{1,0:T(8,128)S(1)}, u32[]{:S(2)}, u32[]{:S(2)}) collective-permute-start(f32[512,128]{1,0:T(8,128)S(1)} %fusion), channel_id=1, source_target_pairs={{0,256},{256,0},{1,257},{257,1},{2,258},{258,2},{3,259},{259,3},{4... | collective-permute-start | bytes 786440 | tf_op jit(solution)/shard_map/ppermute | solution.py:236
  45.9 8.4 %collective-permute-done.6.last = f32[512,128]{1,0:T(8,128)S(1)} collective-permute-done((f32[512,128]{1,0:T(8,128)S(1)}, f32[512,128]{1,0:T(8,128)S(1)}, u32[]{:S(2)}, u32[]{:S(2)}) %collective-permute-start.6) | collective-permute-done | bytes 262176 | tf_op jit(solution)/shard_map/ppermute | solution.py:236
  54.3 1.1 shard_map.42._
  55.4 3.6 %all-to-all-start.1 = ((bf16[8,512,128]{2,1,0:T(8,128)(2,1)}), bf16[8,512,128]{2,1,0:T(8,128)(2,1)S(1)}, u32[]{:S(2)}, u32[]{:S(2)}) async-start(bf16[8,512,128]{2,1,0:T(8,128)(2,1)} %shard_map.42._), calls=%async_computation.1 | async-start | bytes 2097152 | tf_op jit(solution)/shard_map/all_to_all | solution.py:240
  58.9 2.4 %collective-permute-start.8 = (bf16[2,128,1024]{2,1,0:T(8,128)(2,1)S(1)}, bf16[2,128,1024]{2,1,0:T(8,128)(2,1)S(1)}, u32[]{:S(2)}, u32[]{:S(2)}) collective-permute-start(bf16[2,128,1024]{2,1,0:T(8,128)(2,1)S(1)} %shard_map.40.refs_0_), channel_id=1, source_target_pairs={{0,257},{1,256},{256,1},{257,0},{2,259},{3,258},{258,3},{259,2},{4... | collective-permute-start | bytes 1572872 | tf_op jit(solution)/shard_map/ppermute | solution.py:236
  61.3 4.3 %collective-permute-start.7 = (bf16[2,128,1024]{2,1,0:T(8,128)(2,1)S(1)}, bf16[2,128,1024]{2,1,0:T(8,128)(2,1)S(1)}, u32[]{:S(2)}, u32[]{:S(2)}) collective-permute-start(bf16[2,128,1024]{2,1,0:T(8,128)(2,1)S(1)} %shard_map.40.refs_0_), channel_id=1, source_target_pairs={{0,256},{256,0},{1,257},{257,1},{2,258},{258,2},{3,259},{259,3},{4... | collective-permute-start | bytes 1572872 | tf_op jit(solution)/shard_map/ppermute | solution.py:236
  65.7 3.1 %collective-permute-start.9 = (bf16[128,1024]{1,0:T(8,128)(2,1)S(1)}, bf16[128,1024]{1,0:T(8,128)(2,1)S(1)}, u32[]{:S(2)}, u32[]{:S(2)}) collective-permute-start(bf16[128,1024]{1,0:T(8,128)(2,1)S(1)} %slice_bitcast_fusion), channel_id=1, source_target_pairs={{0,1},{1,0},{2,3},{3,2},{4,5},{5,4},{6,7},{7,6},{8,9},{9,8},{10,11... | collective-permute-start | bytes 786440 | tf_op jit(solution)/shard_map/ppermute | solution.py:236
  68.8 1.0 shard_map.44.same
  69.8 13.5 %collective-permute-done.9.side = bf16[128,1024]{1,0:T(8,128)(2,1)S(1)} collective-permute-done((bf16[128,1024]{1,0:T(8,128)(2,1)S(1)}, bf16[128,1024]{1,0:T(8,128)(2,1)S(1)}, u32[]{:S(2)}, u32[]{:S(2)}) %collective-permute-start.9) | collective-permute-done | bytes 262176 | tf_op jit(solution)/shard_map/ppermute | solution.py:236
  83.3 3.1 %collective-permute-done.8.twin = bf16[2,128,1024]{2,1,0:T(8,128)(2,1)S(1)} collective-permute-done((bf16[2,128,1024]{2,1,0:T(8,128)(2,1)S(1)}, bf16[2,128,1024]{2,1,0:T(8,128)(2,1)S(1)}, u32[]{:S(2)}, u32[]{:S(2)}) %collective-permute-start.8) | collective-permute-done | bytes 524320 | tf_op jit(solution)/shard_map/ppermute | solution.py:236
  86.4 0.0 collective-permute-done.7.cross
  86.4 0.9 all-to-all-done.1.precond
  87.3 1.6 %shard_map.45 = f32[4,128,512]{2,1,0:T(8,128)S(1)} custom-call(bf16[8,512,128]{2,1,0:T(8,128)(2,1)S(1)} %all-to-all-done.1.precond, bf16[128,1024]{1,0:T(8,128)(2,1)S(1)} %shard_map.44.same, bf16[128,1024]{1,0:T(8,128)(2,1)S(1)} %collective-permute-done.9.side, bf16[2,128,1024]{2,1,0:T(8,128)(2,1)S(1)} %collective-permute-done.7.cross, ...), custom_call_target="tpu_custom_call" | custom-call | flops 536870912 | bytes 3670016 | tf_op jit(solution)/shard_map/pallas_call | solution.py:25
  88.9 1.9 %collective-permute-start.10 = (f32[4,128,512]{2,1,0:T(8,128)S(1)}, f32[4,128,512]{2,1,0:T(8,128)S(1)}, u32[]{:S(2)}, u32[]{:S(2)}) collective-permute-start(f32[4,128,512]{2,1,0:T(8,128)S(1)} %shard_map.45), channel_id=1, source_target_pairs={{0,16},{16,0},{1,17},{17,1},{2,18},{18,2},{3,19},{19,3},{4,20},{20... | collective-permute-start | bytes 3145736 | tf_op jit(solution)/shard_map/ppermute | solution.py:236
  90.9 2.1 %shard_map.43.own = f32[4,128,512]{2,1,0:T(8,128)S(1)} custom-call(bf16[128,1024]{1,0:T(8,128)(2,1)} %copy-done.4, bf16[128,1024]{1,0:T(8,128)(2,1)} %copy-done.1, bf16[8,512,128]{2,1,0:T(8,128)(2,1)S(1)} %all-to-all-done.1.precond, bf16[2,128,1024]{2,1,0:T(8,128)(2,1)S(1)} %collective-permute-done.7.cross, bf16[2,128,1024]{2,1,0:T(8,128)(2,1)S(1)} %collective-permute-done.8.twin), custom_call_target="tpu_custom_call" | custom-call | flops 536870912 | bytes 4194304 | tf_op jit(solution)/shard_map/pallas_call | solution.py:167
  92.9 0.6 collective-permute-done.10.came
  93.5 0.6 shard_map.46
  94.1 27.3 %all_to_all.20 = bf16[32,16,512]{2,1,0:T(8,128)(2,1)S(1)} all-to-all(bf16[32,16,512]{2,1,0:T(8,128)(2,1)S(1)} %bitcast.18), channel_id=1, replica_groups={{14,15,270,271,12,13,268,269,10,11,266,267,8,9,264,265,6,7,262,263,4,5,..., dimensions={0} | all-to-all | bytes 1048576 | tf_op jit(solution)/shard_map/all_to_all | solution.py:240
  121.4 0.1 shard_map.47
  121.5 13.8 %all_to_all.21 = bf16[8,16,1024]{2,1,0:T(8,128)(2,1)S(1)} all-to-all(bf16[8,16,1024]{2,1,0:T(8,128)(2,1)S(1)} %shard_map.47), channel_id=1, replica_groups={{14,12,10,8,6,4,2,0},{15,13,11,9,7,5,3,1},{30,28,26,24,22,20,18,16},{31..., dimensions={0} | all-to-all | bytes 524288 | tf_op jit(solution)/shard_map/all_to_all | solution.py:240
  135.2 0.9 bitcast_convert_fusion
  (9 shorter events, 0.1 us)
Async XLA Ops:
  2.0 7.3 %copy-start.2 = (bf16[1,128,4096]{2,1,0:T(8,128)(2,1)S(1)}, bf16[1,128,4096]{2,1,0:T(8,128)(2,1)}, u32[]{:S(2)}) copy-start(bf16[1,128,4096]{2,1,0:T(8,128)(2,1)} %param.5) | copy-start | bytes 3145732
  2.0 7.3 %copy-start.3 = (bf16[128,1,4096]{2,0,1:T(8,128)(2,1)S(1)}, bf16[128,1,4096]{2,0,1:T(8,128)(2,1)}, u32[]{:S(2)}) copy-start(bf16[128,1,4096]{2,0,1:T(8,128)(2,1)} %param.3) | copy-start | bytes 3145732
  2.0 36.0 %all-to-all-start = ((bf16[8,512,128]{2,1,0:T(8,128)(2,1)}), bf16[8,512,128]{2,1,0:T(8,128)(2,1)S(1)}, u32[]{:S(2)}, u32[]{:S(2)}) async-start(bf16[8,512,128]{2,1,0:T(8,128)(2,1)} %shard_map.38), calls=%async_computation | async-start | bytes 2097152 | tf_op jit(solution)/shard_map/all_to_all | solution.py:240
  10.4 13.0 %copy-start.4 = (bf16[128,1024]{1,0:T(8,128)(2,1)}, bf16[128,1024]{1,0:T(8,128)(2,1)S(1)}, u32[]{:S(2)}) copy-start(bf16[128,1024]{1,0:T(8,128)(2,1)S(1)} %get-tuple-element.14.same) | copy-start | bytes 786436
  10.5 13.0 %copy-start.5 = (bf16[128,1024]{1,0:T(8,128)(2,1)}, bf16[128,1024]{1,0:T(8,128)(2,1)S(1)}, u32[]{:S(2)}) copy-start(bf16[128,1024]{1,0:T(8,128)(2,1)S(1)} %get-tuple-element.15.f0) | copy-start | bytes 786436
  10.5 13.0 %collective-permute-start.2 = (bf16[2,128,1024]{2,1,0:T(8,128)(2,1)S(1)}, bf16[2,128,1024]{2,1,0:T(8,128)(2,1)S(1)}, u32[]{:S(2)}, u32[]{:S(2)}) collective-permute-start(bf16[2,128,1024]{2,1,0:T(8,128)(2,1)S(1)} %get-tuple-element.19), channel_id=1, source_target_pairs={{0,16},{16,0},{1,17},{17,1},{2,18},{18,2},{3,19},{19,3},{4,20},{20... | collective-permute-start | bytes 1572872 | tf_op jit(solution)/shard_map/ppermute | solution.py:236
  12.4 11.8 %collective-permute-start.1 = (bf16[128,1024]{1,0:T(8,128)(2,1)S(1)}, bf16[128,1024]{1,0:T(8,128)(2,1)S(1)}, u32[]{:S(2)}, u32[]{:S(2)}) collective-permute-start(bf16[128,1024]{1,0:T(8,128)(2,1)S(1)} %get-tuple-element.16), channel_id=1, source_target_pairs={{0,257},{1,256},{256,1},{257,0},{2,259},{3,258},{258,3},{259,2},{4... | collective-permute-start | bytes 786440 | tf_op jit(solution)/shard_map/ppermute | solution.py:236
  16.6 7.6 %collective-permute-start.3 = (bf16[128,1024]{1,0:T(8,128)(2,1)S(1)}, bf16[128,1024]{1,0:T(8,128)(2,1)S(1)}, u32[]{:S(2)}, u32[]{:S(2)}) collective-permute-start(bf16[128,1024]{1,0:T(8,128)(2,1)S(1)} %get-tuple-element.20), channel_id=1, source_target_pairs={{0,16},{16,0},{1,17},{17,1},{2,18},{18,2},{3,19},{19,3},{4,20},{20... | collective-permute-start | bytes 786440 | tf_op jit(solution)/shard_map/ppermute | solution.py:236
  18.8 11.3 %collective-permute-start.4 = (bf16[128,1024]{1,0:T(8,128)(2,1)S(1)}, bf16[128,1024]{1,0:T(8,128)(2,1)S(1)}, u32[]{:S(2)}, u32[]{:S(2)}) collective-permute-start(bf16[128,1024]{1,0:T(8,128)(2,1)S(1)} %get-tuple-element.21), channel_id=1, source_target_pairs={{0,273},{1,272},{16,257},{17,256},{256,17},{257,16},{272,1},{273,0... | collective-permute-start | bytes 786440 | tf_op jit(solution)/shard_map/ppermute | solution.py:236
  21.5 10.3 %collective-permute-start = (bf16[128,1024]{1,0:T(8,128)(2,1)S(1)}, bf16[128,1024]{1,0:T(8,128)(2,1)S(1)}, u32[]{:S(2)}, u32[]{:S(2)}) collective-permute-start(bf16[128,1024]{1,0:T(8,128)(2,1)S(1)} %get-tuple-element.14.same), channel_id=1, source_target_pairs={{0,1},{1,0},{2,3},{3,2},{4,5},{5,4},{6,7},{7,6},{8,9},{9,8},{10,11... | collective-permute-start | bytes 786440 | tf_op jit(solution)/shard_map/ppermute | solution.py:236
  23.4 42.2 %copy-start = (bf16[2,128,1024]{2,1,0:T(8,128)(2,1)}, bf16[2,128,1024]{2,1,0:T(8,128)(2,1)S(1)}, u32[]{:S(2)}) copy-start(bf16[2,128,1024]{2,1,0:T(8,128)(2,1)S(1)} %collective-permute-done.2.came.refs_0_) | copy-start | bytes 1572868
  31.8 6.9 %copy-start.1 = (bf16[128,1024]{1,0:T(8,128)(2,1)}, bf16[128,1024]{1,0:T(8,128)(2,1)S(1)}, u32[]{:S(2)}) copy-start(bf16[128,1024]{1,0:T(8,128)(2,1)S(1)} %collective-permute-done.refs_2_.side) | copy-start | bytes 786436
  38.0 2.7 %copy-start.6 = (bf16[128,1024]{1,0:T(8,128)(2,1)S(1)}, bf16[128,1024]{1,0:T(8,128)(2,1)}, u32[]{:S(2)}) copy-start(bf16[128,1024]{1,0:T(8,128)(2,1)} %copy-done.5) | copy-start | bytes 786436
  38.7 3.8 %collective-permute-start.5 = (f32[2,512,128]{2,1,0:T(8,128)S(1)}, f32[2,512,128]{2,1,0:T(8,128)S(1)}, u32[]{:S(2)}, u32[]{:S(2)}) collective-permute-start(f32[2,512,128]{2,1,0:T(8,128)S(1)} %shard_map.41), channel_id=1, source_target_pairs={{0,16},{16,0},{1,17},{17,1},{2,18},{18,2},{3,19},{19,3},{4,20},{20... | collective-permute-start | bytes 1572872 | tf_op jit(solution)/shard_map/ppermute | solution.py:236
  42.6 11.7 %collective-permute-start.6 = (f32[512,128]{1,0:T(8,128)S(1)}, f32[512,128]{1,0:T(8,128)S(1)}, u32[]{:S(2)}, u32[]{:S(2)}) collective-permute-start(f32[512,128]{1,0:T(8,128)S(1)} %fusion), channel_id=1, source_target_pairs={{0,256},{256,0},{1,257},{257,1},{2,258},{258,2},{3,259},{259,3},{4... | collective-permute-start | bytes 786440 | tf_op jit(solution)/shard_map/ppermute | solution.py:236
  55.4 32.0 %all-to-all-start.1 = ((bf16[8,512,128]{2,1,0:T(8,128)(2,1)}), bf16[8,512,128]{2,1,0:T(8,128)(2,1)S(1)}, u32[]{:S(2)}, u32[]{:S(2)}) async-start(bf16[8,512,128]{2,1,0:T(8,128)(2,1)} %shard_map.42._), calls=%async_computation.1 | async-start | bytes 2097152 | tf_op jit(solution)/shard_map/all_to_all | solution.py:240
  58.9 27.5 %collective-permute-start.8 = (bf16[2,128,1024]{2,1,0:T(8,128)(2,1)S(1)}, bf16[2,128,1024]{2,1,0:T(8,128)(2,1)S(1)}, u32[]{:S(2)}, u32[]{:S(2)}) collective-permute-start(bf16[2,128,1024]{2,1,0:T(8,128)(2,1)S(1)} %shard_map.40.refs_0_), channel_id=1, source_target_pairs={{0,257},{1,256},{256,1},{257,0},{2,259},{3,258},{258,3},{259,2},{4... | collective-permute-start | bytes 1572872 | tf_op jit(solution)/shard_map/ppermute | solution.py:236
  61.3 25.1 %collective-permute-start.7 = (bf16[2,128,1024]{2,1,0:T(8,128)(2,1)S(1)}, bf16[2,128,1024]{2,1,0:T(8,128)(2,1)S(1)}, u32[]{:S(2)}, u32[]{:S(2)}) collective-permute-start(bf16[2,128,1024]{2,1,0:T(8,128)(2,1)S(1)} %shard_map.40.refs_0_), channel_id=1, source_target_pairs={{0,256},{256,0},{1,257},{257,1},{2,258},{258,2},{3,259},{259,3},{4... | collective-permute-start | bytes 1572872 | tf_op jit(solution)/shard_map/ppermute | solution.py:236
  65.7 17.6 %collective-permute-start.9 = (bf16[128,1024]{1,0:T(8,128)(2,1)S(1)}, bf16[128,1024]{1,0:T(8,128)(2,1)S(1)}, u32[]{:S(2)}, u32[]{:S(2)}) collective-permute-start(bf16[128,1024]{1,0:T(8,128)(2,1)S(1)} %slice_bitcast_fusion), channel_id=1, source_target_pairs={{0,1},{1,0},{2,3},{3,2},{4,5},{5,4},{6,7},{7,6},{8,9},{9,8},{10,11... | collective-permute-start | bytes 786440 | tf_op jit(solution)/shard_map/ppermute | solution.py:236
  88.9 4.6 %collective-permute-start.10 = (f32[4,128,512]{2,1,0:T(8,128)S(1)}, f32[4,128,512]{2,1,0:T(8,128)S(1)}, u32[]{:S(2)}, u32[]{:S(2)}) collective-permute-start(f32[4,128,512]{2,1,0:T(8,128)S(1)} %shard_map.45), channel_id=1, source_target_pairs={{0,16},{16,0},{1,17},{17,1},{2,18},{18,2},{3,19},{19,3},{4,20},{20... | collective-permute-start | bytes 3145736 | tf_op jit(solution)/shard_map/ppermute | solution.py:236

commit v8 on v7

--- a/solution.py
+++ b/solution.py
@@ -37,13 +37,17 @@
     return jax.ShapeDtypeStruct(shape, dtype)
 
 
+def across(n):
+    return [i // 2 + (i % 2) * (n // 2) for i in range(n)]
+
+
 def pack_body(ny, w, me, fisher, stored, f00, f01, f10, f11, near0, near1, far):
     for x, outs in ((fisher, ((f00, f10), (f01, f11))), (stored, ((near0, near1), (far.at[0], far.at[1])))):
         for dc in range(2):
             for dx in range(2):
-                for y in range(ny):
+                for i, y in enumerate(across(ny)):
                     first = (((me[0] ^ dx) * ny + y) * 2 + (me[1] ^ dc)) * w
-                    outs[dc][dx][:, y * w : (y + 1) * w] = x[:, pl.ds(pl.multiple_of(first, w), w)]
+                    outs[dc][dx][:, i * w : (i + 1) * w] = x[:, pl.ds(pl.multiple_of(first, w), w)]
 
 
 def pack(me, fisher, stored, ny, w):
@@ -253,11 +257,11 @@
     cross = part(near1, came)
     side = swap(near0, "xl")
 
-    feats = trade(copies(query, ny), "y")
+    feats = trade(copies(query, ny), "y", groups=[across(ny)])
     total = swap(fold_far(feats, fish[1], (cross, fish[0][1], side)), "core")
     own, own_x = fold(feats, fish[0])
     full = settle(own, total, swap(own_x + total[1], "xh"), ny)
-    precond = trade(full, "y")
+    precond = trade(full, "y", groups=[across(ny)])
     twin, cross = swap(cross, "xh", "xl"), swap(cross, "xh")
     far = swap(score_far(precond, fetch(came, full), swap(came[0], "xl"), cross, twin), "core")
     terms = [score(precond, near0, side, cross, twin), far]

time: 137 us -> 135 us (0.985)
  waiting for transfers between devices: 42.1 us -> 38.2 us
    all_to_all x2, waiting for transfers between devices: 7.08 us -> 3.46 us  [trade(): return lax.all_to_all(x, axes, 0, 0, axis_index_groups=groups, tiled=True)]
  transfers between devices with their start and end apart: 13 -> 13, of which waited for: 10 -> 9; matrix products, arithmetic and copies ran while one was open for 0% -> 0% of each run, Pallas kernels for 4% -> 4%
where the time goes in v8:
time: 135 us; the launch traced here: 133 us
  starting transfers between devices  41.7 us (31%)
  blocking collectives  40.8 us (30%)
  waiting for transfers between devices  38.2 us (28%)
  Pallas kernels  11 us (8%)
    all_to_all x2, blocking collectives, trade(): return lax.all_to_all(x, axes, 0, 0, axis_index_groups=groups, tiled=True)  40.8 us
    ppermute x11, waiting for transfers between devices, swap(): return lax.ppermute(x, axes, [(i, n - 1 - i) for i in range(n)])  34.8 us
    ppermute x11, starting transfers between devices, swap(): return lax.ppermute(x, axes, [(i, n - 1 - i) for i in range(n)])  29.9 us
    all_to_all x2, starting transfers between devices, trade(): return lax.all_to_all(x, axes, 0, 0, axis_index_groups=groups, tiled=True)  11.8 us
    pallas_call x8, Pallas kernels, call(): pl.pallas_call(body, out_shape=[jax.ShapeDtypeStruct(s.shape, s.dtype) fo...  6.02 us
    all_to_all x2, waiting for transfers between devices, trade(): return lax.all_to_all(x, axes, 0, 0, axis_index_groups=groups, tiled=True)  3.46 us
  transfers between devices with their start and end apart: 13, of which 9 were waited for; matrix products, arithmetic and copies ran while one was open for 0% of the time, Pallas kernels for 4%

profile of v8, /device:TPU:6, one launch (start us, length us, event | category | flops | bytes accessed | tf_op | source)
XLA Modules:
  0.0 133.0 jit_solution(17585771571977046471)
XLA Ops:
  0.0 2.0 %shard_map.38 = bf16[8,512,128]{2,1,0:T(8,128)(2,1)} custom-call(bf16[512,128]{1,0:T(8,128)(2,1)} %bitcast.21), custom_call_target="tpu_custom_call" | custom-call | tf_op jit(solution)/shard_map/pallas_call | solution.py:79
  2.0 0.0 copy-start.2
  2.0 0.0 copy-start.3
  2.0 7.2 %all-to-all-start = ((bf16[8,512,128]{2,1,0:T(8,128)(2,1)}), bf16[8,512,128]{2,1,0:T(8,128)(2,1)S(1)}, u32[]{:S(2)}, u32[]{:S(2)}) async-start(bf16[8,512,128]{2,1,0:T(8,128)(2,1)} %shard_map.38), calls=%async_computation | async-start | bytes 2097152 | tf_op jit(solution)/shard_map/all_to_all | solution.py:244
  9.3 0.1 pad_add_fusion.me
  9.3 0.0 copy-done.2
  9.3 0.0 copy-done.3
  9.3 1.2 shard_map.37
  10.5 0.0 copy-start.4
  10.5 0.0 copy-start.5
  10.5 1.9 %collective-permute-start.2 = (bf16[2,128,1024]{2,1,0:T(8,128)(2,1)S(1)}, bf16[2,128,1024]{2,1,0:T(8,128)(2,1)S(1)}, u32[]{:S(2)}, u32[]{:S(2)}) collective-permute-start(bf16[2,128,1024]{2,1,0:T(8,128)(2,1)S(1)} %get-tuple-element.19), channel_id=1, source_target_pairs={{0,16},{16,0},{1,17},{17,1},{2,18},{18,2},{3,19},{19,3},{4,20},{20... | collective-permute-start | bytes 1572872 | tf_op jit(solution)/shard_map/ppermute | solution.py:240
  12.4 4.2 %collective-permute-start.1 = (bf16[128,1024]{1,0:T(8,128)(2,1)S(1)}, bf16[128,1024]{1,0:T(8,128)(2,1)S(1)}, u32[]{:S(2)}, u32[]{:S(2)}) collective-permute-start(bf16[128,1024]{1,0:T(8,128)(2,1)S(1)} %get-tuple-element.16), channel_id=1, source_target_pairs={{0,257},{1,256},{256,1},{257,0},{2,259},{3,258},{258,3},{259,2},{4... | collective-permute-start | bytes 786440 | tf_op jit(solution)/shard_map/ppermute | solution.py:240
  16.7 2.1 %collective-permute-start.3 = (bf16[128,1024]{1,0:T(8,128)(2,1)S(1)}, bf16[128,1024]{1,0:T(8,128)(2,1)S(1)}, u32[]{:S(2)}, u32[]{:S(2)}) collective-permute-start(bf16[128,1024]{1,0:T(8,128)(2,1)S(1)} %get-tuple-element.20), channel_id=1, source_target_pairs={{0,16},{16,0},{1,17},{17,1},{2,18},{18,2},{3,19},{19,3},{4,20},{20... | collective-permute-start | bytes 786440 | tf_op jit(solution)/shard_map/ppermute | solution.py:240
  18.8 2.7 %collective-permute-start.4 = (bf16[128,1024]{1,0:T(8,128)(2,1)S(1)}, bf16[128,1024]{1,0:T(8,128)(2,1)S(1)}, u32[]{:S(2)}, u32[]{:S(2)}) collective-permute-start(bf16[128,1024]{1,0:T(8,128)(2,1)S(1)} %get-tuple-element.21), channel_id=1, source_target_pairs={{0,273},{1,272},{16,257},{17,256},{256,17},{257,16},{272,1},{273,0... | collective-permute-start | bytes 786440 | tf_op jit(solution)/shard_map/ppermute | solution.py:240
  21.5 1.9 %collective-permute-start = (bf16[128,1024]{1,0:T(8,128)(2,1)S(1)}, bf16[128,1024]{1,0:T(8,128)(2,1)S(1)}, u32[]{:S(2)}, u32[]{:S(2)}) collective-permute-start(bf16[128,1024]{1,0:T(8,128)(2,1)S(1)} %get-tuple-element.14.same), channel_id=1, source_target_pairs={{0,1},{1,0},{2,3},{3,2},{4,5},{5,4},{6,7},{7,6},{8,9},{9,8},{10,11... | collective-permute-start | bytes 786440 | tf_op jit(solution)/shard_map/ppermute | solution.py:240
  23.5 0.0 collective-permute-done.2.came.refs_0_
  23.5 0.0 copy-start
  23.5 0.0 copy-done.4
  23.6 0.7 collective-permute-done.1.f1.refs_1_
  24.3 0.0 collective-permute-done.3.refs_4_
  24.3 5.9 %collective-permute-done.4.refs_5_ = bf16[128,1024]{1,0:T(8,128)(2,1)S(1)} collective-permute-done((bf16[128,1024]{1,0:T(8,128)(2,1)S(1)}, bf16[128,1024]{1,0:T(8,128)(2,1)S(1)}, u32[]{:S(2)}, u32[]{:S(2)}) %collective-permute-start.4) | collective-permute-done | bytes 262176 | tf_op jit(solution)/shard_map/ppermute | solution.py:240
  30.1 1.7 %collective-permute-done.refs_2_.side = bf16[128,1024]{1,0:T(8,128)(2,1)S(1)} collective-permute-done((bf16[128,1024]{1,0:T(8,128)(2,1)S(1)}, bf16[128,1024]{1,0:T(8,128)(2,1)S(1)}, u32[]{:S(2)}, u32[]{:S(2)}) %collective-permute-start) | collective-permute-done | bytes 262176 | tf_op jit(solution)/shard_map/ppermute | solution.py:240
  31.9 3.5 %all-to-all-done.feats.refs_3_ = bf16[8,512,128]{2,1,0:T(8,128)(2,1)S(1)} async-done(((bf16[8,512,128]{2,1,0:T(8,128)(2,1)}), bf16[8,512,128]{2,1,0:T(8,128)(2,1)S(1)}, u32[]{:S(2)}, u32[]{:S(2)}) %all-to-all-start) | async-done | bytes 1048608 | tf_op jit(solution)/shard_map/all_to_all | solution.py:244
  35.3 0.7 shard_map.41
  36.1 1.9 %collective-permute-start.5 = (f32[2,512,128]{2,1,0:T(8,128)S(1)}, f32[2,512,128]{2,1,0:T(8,128)S(1)}, u32[]{:S(2)}, u32[]{:S(2)}) collective-permute-start(f32[2,512,128]{2,1,0:T(8,128)S(1)} %shard_map.41), channel_id=1, source_target_pairs={{0,16},{16,0},{1,17},{17,1},{2,18},{18,2},{3,19},{19,3},{4,20},{20... | collective-permute-start | bytes 1572872 | tf_op jit(solution)/shard_map/ppermute | solution.py:240
  38.0 0.7 shard_map.39
  38.8 1.1 collective-permute-done.5.came
  39.9 3.3 %collective-permute-start.6 = (f32[512,128]{1,0:T(8,128)S(1)}, f32[512,128]{1,0:T(8,128)S(1)}, u32[]{:S(2)}, u32[]{:S(2)}) collective-permute-start(f32[512,128]{1,0:T(8,128)S(1)} %fusion), channel_id=1, source_target_pairs={{0,256},{256,0},{1,257},{257,1},{2,258},{258,2},{3,259},{259,3},{4... | collective-permute-start | bytes 786440 | tf_op jit(solution)/shard_map/ppermute | solution.py:240
  43.2 8.4 %collective-permute-done.6.last = f32[512,128]{1,0:T(8,128)S(1)} collective-permute-done((f32[512,128]{1,0:T(8,128)S(1)}, f32[512,128]{1,0:T(8,128)S(1)}, u32[]{:S(2)}, u32[]{:S(2)}) %collective-permute-start.6) | collective-permute-done | bytes 262176 | tf_op jit(solution)/shard_map/ppermute | solution.py:240
  51.7 1.1 shard_map.42._
  52.7 4.5 %all-to-all-start.1 = ((bf16[8,512,128]{2,1,0:T(8,128)(2,1)}), bf16[8,512,128]{2,1,0:T(8,128)(2,1)S(1)}, u32[]{:S(2)}, u32[]{:S(2)}) async-start(bf16[8,512,128]{2,1,0:T(8,128)(2,1)} %shard_map.42._), calls=%async_computation.1 | async-start | bytes 2097152 | tf_op jit(solution)/shard_map/all_to_all | solution.py:244
  57.3 3.3 %collective-permute-start.8 = (bf16[2,128,1024]{2,1,0:T(8,128)(2,1)S(1)}, bf16[2,128,1024]{2,1,0:T(8,128)(2,1)S(1)}, u32[]{:S(2)}, u32[]{:S(2)}) collective-permute-start(bf16[2,128,1024]{2,1,0:T(8,128)(2,1)S(1)} %shard_map.40.refs_0_), channel_id=1, source_target_pairs={{0,257},{1,256},{256,1},{257,0},{2,259},{3,258},{258,3},{259,2},{4... | collective-permute-start | bytes 1572872 | tf_op jit(solution)/shard_map/ppermute | solution.py:240
  60.6 3.4 %collective-permute-start.7 = (bf16[2,128,1024]{2,1,0:T(8,128)(2,1)S(1)}, bf16[2,128,1024]{2,1,0:T(8,128)(2,1)S(1)}, u32[]{:S(2)}, u32[]{:S(2)}) collective-permute-start(bf16[2,128,1024]{2,1,0:T(8,128)(2,1)S(1)} %shard_map.40.refs_0_), channel_id=1, source_target_pairs={{0,256},{256,0},{1,257},{257,1},{2,258},{258,2},{3,259},{259,3},{4... | collective-permute-start | bytes 1572872 | tf_op jit(solution)/shard_map/ppermute | solution.py:240
  64.0 3.1 %collective-permute-start.9 = (bf16[128,1024]{1,0:T(8,128)(2,1)S(1)}, bf16[128,1024]{1,0:T(8,128)(2,1)S(1)}, u32[]{:S(2)}, u32[]{:S(2)}) collective-permute-start(bf16[128,1024]{1,0:T(8,128)(2,1)S(1)} %slice_bitcast_fusion), channel_id=1, source_target_pairs={{0,1},{1,0},{2,3},{3,2},{4,5},{5,4},{6,7},{7,6},{8,9},{9,8},{10,11... | collective-permute-start | bytes 786440 | tf_op jit(solution)/shard_map/ppermute | solution.py:240
  67.1 1.0 shard_map.44.same
  68.1 13.3 %collective-permute-done.9.side = bf16[128,1024]{1,0:T(8,128)(2,1)S(1)} collective-permute-done((bf16[128,1024]{1,0:T(8,128)(2,1)S(1)}, bf16[128,1024]{1,0:T(8,128)(2,1)S(1)}, u32[]{:S(2)}, u32[]{:S(2)}) %collective-permute-start.9) | collective-permute-done | bytes 262176 | tf_op jit(solution)/shard_map/ppermute | solution.py:240
  81.4 3.1 %collective-permute-done.8.twin = bf16[2,128,1024]{2,1,0:T(8,128)(2,1)S(1)} collective-permute-done((bf16[2,128,1024]{2,1,0:T(8,128)(2,1)S(1)}, bf16[2,128,1024]{2,1,0:T(8,128)(2,1)S(1)}, u32[]{:S(2)}, u32[]{:S(2)}) %collective-permute-start.8) | collective-permute-done | bytes 524320 | tf_op jit(solution)/shard_map/ppermute | solution.py:240
  84.5 0.0 collective-permute-done.7.cross
  84.5 0.0 all-to-all-done.1.precond
  84.5 1.6 %shard_map.45 = f32[4,128,512]{2,1,0:T(8,128)S(1)} custom-call(bf16[8,512,128]{2,1,0:T(8,128)(2,1)S(1)} %all-to-all-done.1.precond, bf16[128,1024]{1,0:T(8,128)(2,1)S(1)} %shard_map.44.same, bf16[128,1024]{1,0:T(8,128)(2,1)S(1)} %collective-permute-done.9.side, bf16[2,128,1024]{2,1,0:T(8,128)(2,1)S(1)} %collective-permute-done.7.cross, ...), custom_call_target="tpu_custom_call" | custom-call | flops 536870912 | bytes 3670016 | tf_op jit(solution)/shard_map/pallas_call | solution.py:25
  86.0 1.9 %collective-permute-start.10 = (f32[4,128,512]{2,1,0:T(8,128)S(1)}, f32[4,128,512]{2,1,0:T(8,128)S(1)}, u32[]{:S(2)}, u32[]{:S(2)}) collective-permute-start(f32[4,128,512]{2,1,0:T(8,128)S(1)} %shard_map.45), channel_id=1, source_target_pairs={{0,16},{16,0},{1,17},{17,1},{2,18},{18,2},{3,19},{19,3},{4,20},{20... | collective-permute-start | bytes 3145736 | tf_op jit(solution)/shard_map/ppermute | solution.py:240
  88.0 2.1 %shard_map.43.own = f32[4,128,512]{2,1,0:T(8,128)S(1)} custom-call(bf16[128,1024]{1,0:T(8,128)(2,1)} %copy-done.4, bf16[128,1024]{1,0:T(8,128)(2,1)} %copy-done.1, bf16[8,512,128]{2,1,0:T(8,128)(2,1)S(1)} %all-to-all-done.1.precond, bf16[2,128,1024]{2,1,0:T(8,128)(2,1)S(1)} %collective-permute-done.7.cross, bf16[2,128,1024]{2,1,0:T(8,128)(2,1)S(1)} %collective-permute-done.8.twin), custom_call_target="tpu_custom_call" | custom-call | flops 536870912 | bytes 4194304 | tf_op jit(solution)/shard_map/pallas_call | solution.py:171
  90.0 0.6 collective-permute-done.10.came
  90.6 0.6 shard_map.46
  91.3 27.0 %all_to_all.20 = bf16[32,16,512]{2,1,0:T(8,128)(2,1)S(1)} all-to-all(bf16[32,16,512]{2,1,0:T(8,128)(2,1)S(1)} %bitcast.18), channel_id=1, replica_groups={{14,15,270,271,12,13,268,269,10,11,266,267,8,9,264,265,6,7,262,263,4,5,..., dimensions={0} | all-to-all | bytes 1048576 | tf_op jit(solution)/shard_map/all_to_all | solution.py:244
  118.3 0.1 shard_map.47
  118.3 13.8 %all_to_all.21 = bf16[8,16,1024]{2,1,0:T(8,128)(2,1)S(1)} all-to-all(bf16[8,16,1024]{2,1,0:T(8,128)(2,1)S(1)} %shard_map.47), channel_id=1, replica_groups={{14,12,10,8,6,4,2,0},{15,13,11,9,7,5,3,1},{30,28,26,24,22,20,18,16},{31..., dimensions={0} | all-to-all | bytes 524288 | tf_op jit(solution)/shard_map/all_to_all | solution.py:244
  132.1 0.9 bitcast_convert_fusion
  (9 shorter events, 0.1 us)
Async XLA Ops:
  2.0 7.3 %copy-start.2 = (bf16[1,128,4096]{2,1,0:T(8,128)(2,1)S(1)}, bf16[1,128,4096]{2,1,0:T(8,128)(2,1)}, u32[]{:S(2)}) copy-start(bf16[1,128,4096]{2,1,0:T(8,128)(2,1)} %param.5) | copy-start | bytes 3145732
  2.0 7.3 %copy-start.3 = (bf16[128,1,4096]{2,0,1:T(8,128)(2,1)S(1)}, bf16[128,1,4096]{2,0,1:T(8,128)(2,1)}, u32[]{:S(2)}) copy-start(bf16[128,1,4096]{2,0,1:T(8,128)(2,1)} %param.3) | copy-start | bytes 3145732
  2.0 33.3 %all-to-all-start = ((bf16[8,512,128]{2,1,0:T(8,128)(2,1)}), bf16[8,512,128]{2,1,0:T(8,128)(2,1)S(1)}, u32[]{:S(2)}, u32[]{:S(2)}) async-start(bf16[8,512,128]{2,1,0:T(8,128)(2,1)} %shard_map.38), calls=%async_computation | async-start | bytes 2097152 | tf_op jit(solution)/shard_map/all_to_all | solution.py:244
  10.5 13.0 %copy-start.4 = (bf16[128,1024]{1,0:T(8,128)(2,1)}, bf16[128,1024]{1,0:T(8,128)(2,1)S(1)}, u32[]{:S(2)}) copy-start(bf16[128,1024]{1,0:T(8,128)(2,1)S(1)} %get-tuple-element.14.same) | copy-start | bytes 786436
  10.5 13.0 %copy-start.5 = (bf16[128,1024]{1,0:T(8,128)(2,1)}, bf16[128,1024]{1,0:T(8,128)(2,1)S(1)}, u32[]{:S(2)}) copy-start(bf16[128,1024]{1,0:T(8,128)(2,1)S(1)} %get-tuple-element.15.f0) | copy-start | bytes 786436
  10.5 13.0 %collective-permute-start.2 = (bf16[2,128,1024]{2,1,0:T(8,128)(2,1)S(1)}, bf16[2,128,1024]{2,1,0:T(8,128)(2,1)S(1)}, u32[]{:S(2)}, u32[]{:S(2)}) collective-permute-start(bf16[2,128,1024]{2,1,0:T(8,128)(2,1)S(1)} %get-tuple-element.19), channel_id=1, source_target_pairs={{0,16},{16,0},{1,17},{17,1},{2,18},{18,2},{3,19},{19,3},{4,20},{20... | collective-permute-start | bytes 1572872 | tf_op jit(solution)/shard_map/ppermute | solution.py:240
  12.4 11.8 %collective-permute-start.1 = (bf16[128,1024]{1,0:T(8,128)(2,1)S(1)}, bf16[128,1024]{1,0:T(8,128)(2,1)S(1)}, u32[]{:S(2)}, u32[]{:S(2)}) collective-permute-start(bf16[128,1024]{1,0:T(8,128)(2,1)S(1)} %get-tuple-element.16), channel_id=1, source_target_pairs={{0,257},{1,256},{256,1},{257,0},{2,259},{3,258},{258,3},{259,2},{4... | collective-permute-start | bytes 786440 | tf_op jit(solution)/shard_map/ppermute | solution.py:240
  16.7 7.6 %collective-permute-start.3 = (bf16[128,1024]{1,0:T(8,128)(2,1)S(1)}, bf16[128,1024]{1,0:T(8,128)(2,1)S(1)}, u32[]{:S(2)}, u32[]{:S(2)}) collective-permute-start(bf16[128,1024]{1,0:T(8,128)(2,1)S(1)} %get-tuple-element.20), channel_id=1, source_target_pairs={{0,16},{16,0},{1,17},{17,1},{2,18},{18,2},{3,19},{19,3},{4,20},{20... | collective-permute-start | bytes 786440 | tf_op jit(solution)/shard_map/ppermute | solution.py:240
  18.8 11.3 %collective-permute-start.4 = (bf16[128,1024]{1,0:T(8,128)(2,1)S(1)}, bf16[128,1024]{1,0:T(8,128)(2,1)S(1)}, u32[]{:S(2)}, u32[]{:S(2)}) collective-permute-start(bf16[128,1024]{1,0:T(8,128)(2,1)S(1)} %get-tuple-element.21), channel_id=1, source_target_pairs={{0,273},{1,272},{16,257},{17,256},{256,17},{257,16},{272,1},{273,0... | collective-permute-start | bytes 786440 | tf_op jit(solution)/shard_map/ppermute | solution.py:240
  21.5 10.3 %collective-permute-start = (bf16[128,1024]{1,0:T(8,128)(2,1)S(1)}, bf16[128,1024]{1,0:T(8,128)(2,1)S(1)}, u32[]{:S(2)}, u32[]{:S(2)}) collective-permute-start(bf16[128,1024]{1,0:T(8,128)(2,1)S(1)} %get-tuple-element.14.same), channel_id=1, source_target_pairs={{0,1},{1,0},{2,3},{3,2},{4,5},{5,4},{6,7},{7,6},{8,9},{9,8},{10,11... | collective-permute-start | bytes 786440 | tf_op jit(solution)/shard_map/ppermute | solution.py:240
  23.5 40.5 %copy-start = (bf16[2,128,1024]{2,1,0:T(8,128)(2,1)}, bf16[2,128,1024]{2,1,0:T(8,128)(2,1)S(1)}, u32[]{:S(2)}) copy-start(bf16[2,128,1024]{2,1,0:T(8,128)(2,1)S(1)} %collective-permute-done.2.came.refs_0_) | copy-start | bytes 1572868
  31.9 4.2 %copy-start.1 = (bf16[128,1024]{1,0:T(8,128)(2,1)}, bf16[128,1024]{1,0:T(8,128)(2,1)S(1)}, u32[]{:S(2)}) copy-start(bf16[128,1024]{1,0:T(8,128)(2,1)S(1)} %collective-permute-done.refs_2_.side) | copy-start | bytes 786436
  35.3 2.7 %copy-start.6 = (bf16[128,1024]{1,0:T(8,128)(2,1)S(1)}, bf16[128,1024]{1,0:T(8,128)(2,1)}, u32[]{:S(2)}) copy-start(bf16[128,1024]{1,0:T(8,128)(2,1)} %copy-done.5) | copy-start | bytes 786436
  36.1 3.8 %collective-permute-start.5 = (f32[2,512,128]{2,1,0:T(8,128)S(1)}, f32[2,512,128]{2,1,0:T(8,128)S(1)}, u32[]{:S(2)}, u32[]{:S(2)}) collective-permute-start(f32[2,512,128]{2,1,0:T(8,128)S(1)} %shard_map.41), channel_id=1, source_target_pairs={{0,16},{16,0},{1,17},{17,1},{2,18},{18,2},{3,19},{19,3},{4,20},{20... | collective-permute-start | bytes 1572872 | tf_op jit(solution)/shard_map/ppermute | solution.py:240
  39.9 11.7 %collective-permute-start.6 = (f32[512,128]{1,0:T(8,128)S(1)}, f32[512,128]{1,0:T(8,128)S(1)}, u32[]{:S(2)}, u32[]{:S(2)}) collective-permute-start(f32[512,128]{1,0:T(8,128)S(1)} %fusion), channel_id=1, source_target_pairs={{0,256},{256,0},{1,257},{257,1},{2,258},{258,2},{3,259},{259,3},{4... | collective-permute-start | bytes 786440 | tf_op jit(solution)/shard_map/ppermute | solution.py:240
  52.7 31.7 %all-to-all-start.1 = ((bf16[8,512,128]{2,1,0:T(8,128)(2,1)}), bf16[8,512,128]{2,1,0:T(8,128)(2,1)S(1)}, u32[]{:S(2)}, u32[]{:S(2)}) async-start(bf16[8,512,128]{2,1,0:T(8,128)(2,1)} %shard_map.42._), calls=%async_computation.1 | async-start | bytes 2097152 | tf_op jit(solution)/shard_map/all_to_all | solution.py:244
  57.3 27.2 %collective-permute-start.8 = (bf16[2,128,1024]{2,1,0:T(8,128)(2,1)S(1)}, bf16[2,128,1024]{2,1,0:T(8,128)(2,1)S(1)}, u32[]{:S(2)}, u32[]{:S(2)}) collective-permute-start(bf16[2,128,1024]{2,1,0:T(8,128)(2,1)S(1)} %shard_map.40.refs_0_), channel_id=1, source_target_pairs={{0,257},{1,256},{256,1},{257,0},{2,259},{3,258},{258,3},{259,2},{4... | collective-permute-start | bytes 1572872 | tf_op jit(solution)/shard_map/ppermute | solution.py:240
  60.6 23.9 %collective-permute-start.7 = (bf16[2,128,1024]{2,1,0:T(8,128)(2,1)S(1)}, bf16[2,128,1024]{2,1,0:T(8,128)(2,1)S(1)}, u32[]{:S(2)}, u32[]{:S(2)}) collective-permute-start(bf16[2,128,1024]{2,1,0:T(8,128)(2,1)S(1)} %shard_map.40.refs_0_), channel_id=1, source_target_pairs={{0,256},{256,0},{1,257},{257,1},{2,258},{258,2},{3,259},{259,3},{4... | collective-permute-start | bytes 1572872 | tf_op jit(solution)/shard_map/ppermute | solution.py:240
  64.0 17.4 %collective-permute-start.9 = (bf16[128,1024]{1,0:T(8,128)(2,1)S(1)}, bf16[128,1024]{1,0:T(8,128)(2,1)S(1)}, u32[]{:S(2)}, u32[]{:S(2)}) collective-permute-start(bf16[128,1024]{1,0:T(8,128)(2,1)S(1)} %slice_bitcast_fusion), channel_id=1, source_target_pairs={{0,1},{1,0},{2,3},{3,2},{4,5},{5,4},{6,7},{7,6},{8,9},{9,8},{10,11... | collective-permute-start | bytes 786440 | tf_op jit(solution)/shard_map/ppermute | solution.py:240
  86.0 4.6 %collective-permute-start.10 = (f32[4,128,512]{2,1,0:T(8,128)S(1)}, f32[4,128,512]{2,1,0:T(8,128)S(1)}, u32[]{:S(2)}, u32[]{:S(2)}) collective-permute-start(f32[4,128,512]{2,1,0:T(8,128)S(1)} %shard_map.45), channel_id=1, source_target_pairs={{0,16},{16,0},{1,17},{17,1},{2,18},{18,2},{3,19},{19,3},{4,20},{20... | collective-permute-start | bytes 3145736 | tf_op jit(solution)/shard_map/ppermute | solution.py:240

commit v9 on v8

--- a/solution.py
+++ b/solution.py
@@ -265,10 +265,10 @@
     twin, cross = swap(cross, "xh", "xl"), swap(cross, "xh")
     far = swap(score_far(precond, fetch(came, full), swap(came[0], "xl"), cross, twin), "core")
     terms = [score(precond, near0, side, cross, twin), far]
-    last_first = [[z * 2 * nl + x for z in reversed(range(nz)) for x in range(2 * nl)]]
+    last_first = [[z * 2 * nl + x for z in [nz - 1 - i // 2 if i % 2 == 0 else i // 2 for i in range(nz)] for x in range(2 * nl)]]
     scores = trade(meet(me, *terms, nz).reshape(nz * 2 * nl, n // nz, q), "z", "xh", "xl", groups=last_first)
     total = finish(scores.reshape(nz, 2, nl, n // nz, q), 1.0 / math.sqrt(nz * f))
-    return trade(total, "z", groups=[list(reversed(range(nz)))]).reshape(n, nl * q).astype(F32)
+    return trade(total, "z", groups=[[nz - 1 - i // 2 if i % 2 == 0 else i // 2 for i in range(nz)]]).reshape(n, nl * q).astype(F32)
 
 
 def solution(mesh):

time: 135 us -> 135 us (level)
  the two profiles are of different devices: /device:TPU:6 before, /device:TPU:8 now
where the time goes in v9:
time: 135 us; the launch traced here: 134 us
  starting transfers between devices  46 us (34%)
  blocking collectives  40.6 us (30%)
  waiting for transfers between devices  35 us (26%)
  Pallas kernels  11 us (8%)
    all_to_all x2, blocking collectives, trade(): return lax.all_to_all(x, axes, 0, 0, axis_index_groups=groups, tiled=True)  40.6 us
    ppermute x11, waiting for transfers between devices, swap(): return lax.ppermute(x, axes, [(i, n - 1 - i) for i in range(n)])  33.5 us
    ppermute x11, starting transfers between devices, swap(): return lax.ppermute(x, axes, [(i, n - 1 - i) for i in range(n)])  30.9 us
    all_to_all x2, starting transfers between devices, trade(): return lax.all_to_all(x, axes, 0, 0, axis_index_groups=groups, tiled=True)  15.1 us
    pallas_call x8, Pallas kernels, call(): pl.pallas_call(body, out_shape=[jax.ShapeDtypeStruct(s.shape, s.dtype) fo...  6.02 us
  transfers between devices with their start and end apart: 13, of which 9 were waited for; matrix products, arithmetic and copies ran while one was open for 0% of the time, Pallas kernels for 4%

profile of v9, /device:TPU:8, one launch (start us, length us, event | category | flops | bytes accessed | tf_op | source)
XLA Modules:
  0.0 133.9 jit_solution(14034876097435484145)
XLA Ops:
  0.0 2.0 %shard_map.38 = bf16[8,512,128]{2,1,0:T(8,128)(2,1)} custom-call(bf16[512,128]{1,0:T(8,128)(2,1)} %bitcast.21), custom_call_target="tpu_custom_call" | custom-call | tf_op jit(solution)/shard_map/pallas_call | solution.py:79
  2.0 0.0 copy-start.2
  2.0 0.0 copy-start.3
  2.0 9.4 %all-to-all-start = ((bf16[8,512,128]{2,1,0:T(8,128)(2,1)}), bf16[8,512,128]{2,1,0:T(8,128)(2,1)S(1)}, u32[]{:S(2)}, u32[]{:S(2)}) async-start(bf16[8,512,128]{2,1,0:T(8,128)(2,1)} %shard_map.38), calls=%async_computation | async-start | bytes 2097152 | tf_op jit(solution)/shard_map/all_to_all | solution.py:244
  11.4 0.1 pad_add_fusion.me
  11.5 0.0 copy-done.2
  11.5 0.0 copy-done.3
  11.5 1.2 shard_map.37
  12.7 0.0 copy-start.4
  12.7 0.0 copy-start.5
  12.7 1.9 %collective-permute-start.2 = (bf16[2,128,1024]{2,1,0:T(8,128)(2,1)S(1)}, bf16[2,128,1024]{2,1,0:T(8,128)(2,1)S(1)}, u32[]{:S(2)}, u32[]{:S(2)}) collective-permute-start(bf16[2,128,1024]{2,1,0:T(8,128)(2,1)S(1)} %get-tuple-element.19), channel_id=1, source_target_pairs={{0,16},{16,0},{1,17},{17,1},{2,18},{18,2},{3,19},{19,3},{4,20},{20... | collective-permute-start | bytes 1572872 | tf_op jit(solution)/shard_map/ppermute | solution.py:240
  14.6 2.9 %collective-permute-start.1 = (bf16[128,1024]{1,0:T(8,128)(2,1)S(1)}, bf16[128,1024]{1,0:T(8,128)(2,1)S(1)}, u32[]{:S(2)}, u32[]{:S(2)}) collective-permute-start(bf16[128,1024]{1,0:T(8,128)(2,1)S(1)} %get-tuple-element.16), channel_id=1, source_target_pairs={{0,257},{1,256},{256,1},{257,0},{2,259},{3,258},{258,3},{259,2},{4... | collective-permute-start | bytes 786440 | tf_op jit(solution)/shard_map/ppermute | solution.py:240
  17.6 2.1 %collective-permute-start.3 = (bf16[128,1024]{1,0:T(8,128)(2,1)S(1)}, bf16[128,1024]{1,0:T(8,128)(2,1)S(1)}, u32[]{:S(2)}, u32[]{:S(2)}) collective-permute-start(bf16[128,1024]{1,0:T(8,128)(2,1)S(1)} %get-tuple-element.20), channel_id=1, source_target_pairs={{0,16},{16,0},{1,17},{17,1},{2,18},{18,2},{3,19},{19,3},{4,20},{20... | collective-permute-start | bytes 786440 | tf_op jit(solution)/shard_map/ppermute | solution.py:240
  19.7 4.0 %collective-permute-start.4 = (bf16[128,1024]{1,0:T(8,128)(2,1)S(1)}, bf16[128,1024]{1,0:T(8,128)(2,1)S(1)}, u32[]{:S(2)}, u32[]{:S(2)}) collective-permute-start(bf16[128,1024]{1,0:T(8,128)(2,1)S(1)} %get-tuple-element.21), channel_id=1, source_target_pairs={{0,273},{1,272},{16,257},{17,256},{256,17},{257,16},{272,1},{273,0... | collective-permute-start | bytes 786440 | tf_op jit(solution)/shard_map/ppermute | solution.py:240
  23.7 1.9 %collective-permute-start = (bf16[128,1024]{1,0:T(8,128)(2,1)S(1)}, bf16[128,1024]{1,0:T(8,128)(2,1)S(1)}, u32[]{:S(2)}, u32[]{:S(2)}) collective-permute-start(bf16[128,1024]{1,0:T(8,128)(2,1)S(1)} %get-tuple-element.14.same), channel_id=1, source_target_pairs={{0,1},{1,0},{2,3},{3,2},{4,5},{5,4},{6,7},{7,6},{8,9},{9,8},{10,11... | collective-permute-start | bytes 786440 | tf_op jit(solution)/shard_map/ppermute | solution.py:240
  25.7 0.0 collective-permute-done.2.came.refs_0_
  25.7 0.0 copy-start
  25.7 0.0 copy-done.4
  25.8 1.1 collective-permute-done.1.f1.refs_1_
  26.8 0.0 collective-permute-done.3.refs_4_
  26.8 4.8 %collective-permute-done.4.refs_5_ = bf16[128,1024]{1,0:T(8,128)(2,1)S(1)} collective-permute-done((bf16[128,1024]{1,0:T(8,128)(2,1)S(1)}, bf16[128,1024]{1,0:T(8,128)(2,1)S(1)}, u32[]{:S(2)}, u32[]{:S(2)}) %collective-permute-start.4) | collective-permute-done | bytes 262176 | tf_op jit(solution)/shard_map/ppermute | solution.py:240
  31.7 2.4 %collective-permute-done.refs_2_.side = bf16[128,1024]{1,0:T(8,128)(2,1)S(1)} collective-permute-done((bf16[128,1024]{1,0:T(8,128)(2,1)S(1)}, bf16[128,1024]{1,0:T(8,128)(2,1)S(1)}, u32[]{:S(2)}, u32[]{:S(2)}) %collective-permute-start) | collective-permute-done | bytes 262176 | tf_op jit(solution)/shard_map/ppermute | solution.py:240
  34.1 1.5 %all-to-all-done.feats.refs_3_ = bf16[8,512,128]{2,1,0:T(8,128)(2,1)S(1)} async-done(((bf16[8,512,128]{2,1,0:T(8,128)(2,1)}), bf16[8,512,128]{2,1,0:T(8,128)(2,1)S(1)}, u32[]{:S(2)}, u32[]{:S(2)}) %all-to-all-start) | async-done | bytes 1048608 | tf_op jit(solution)/shard_map/all_to_all | solution.py:244
  35.6 0.7 shard_map.41
  36.3 1.9 %collective-permute-start.5 = (f32[2,512,128]{2,1,0:T(8,128)S(1)}, f32[2,512,128]{2,1,0:T(8,128)S(1)}, u32[]{:S(2)}, u32[]{:S(2)}) collective-permute-start(f32[2,512,128]{2,1,0:T(8,128)S(1)} %shard_map.41), channel_id=1, source_target_pairs={{0,16},{16,0},{1,17},{17,1},{2,18},{18,2},{3,19},{19,3},{4,20},{20... | collective-permute-start | bytes 1572872 | tf_op jit(solution)/shard_map/ppermute | solution.py:240
  38.3 0.7 shard_map.39
  39.0 1.1 collective-permute-done.5.came
  40.2 4.3 %collective-permute-start.6 = (f32[512,128]{1,0:T(8,128)S(1)}, f32[512,128]{1,0:T(8,128)S(1)}, u32[]{:S(2)}, u32[]{:S(2)}) collective-permute-start(f32[512,128]{1,0:T(8,128)S(1)} %fusion), channel_id=1, source_target_pairs={{0,256},{256,0},{1,257},{257,1},{2,258},{258,2},{3,259},{259,3},{4... | collective-permute-start | bytes 786440 | tf_op jit(solution)/shard_map/ppermute | solution.py:240
  44.5 7.4 %collective-permute-done.6.last = f32[512,128]{1,0:T(8,128)S(1)} collective-permute-done((f32[512,128]{1,0:T(8,128)S(1)}, f32[512,128]{1,0:T(8,128)S(1)}, u32[]{:S(2)}, u32[]{:S(2)}) %collective-permute-start.6) | collective-permute-done | bytes 262176 | tf_op jit(solution)/shard_map/ppermute | solution.py:240
  51.9 1.1 shard_map.42._
  53.0 5.7 %all-to-all-start.1 = ((bf16[8,512,128]{2,1,0:T(8,128)(2,1)}), bf16[8,512,128]{2,1,0:T(8,128)(2,1)S(1)}, u32[]{:S(2)}, u32[]{:S(2)}) async-start(bf16[8,512,128]{2,1,0:T(8,128)(2,1)} %shard_map.42._), calls=%async_computation.1 | async-start | bytes 2097152 | tf_op jit(solution)/shard_map/all_to_all | solution.py:244
  58.7 3.7 %collective-permute-start.8 = (bf16[2,128,1024]{2,1,0:T(8,128)(2,1)S(1)}, bf16[2,128,1024]{2,1,0:T(8,128)(2,1)S(1)}, u32[]{:S(2)}, u32[]{:S(2)}) collective-permute-start(bf16[2,128,1024]{2,1,0:T(8,128)(2,1)S(1)} %shard_map.40.refs_0_), channel_id=1, source_target_pairs={{0,257},{1,256},{256,1},{257,0},{2,259},{3,258},{258,3},{259,2},{4... | collective-permute-start | bytes 1572872 | tf_op jit(solution)/shard_map/ppermute | solution.py:240
  62.4 2.7 %collective-permute-start.7 = (bf16[2,128,1024]{2,1,0:T(8,128)(2,1)S(1)}, bf16[2,128,1024]{2,1,0:T(8,128)(2,1)S(1)}, u32[]{:S(2)}, u32[]{:S(2)}) collective-permute-start(bf16[2,128,1024]{2,1,0:T(8,128)(2,1)S(1)} %shard_map.40.refs_0_), channel_id=1, source_target_pairs={{0,256},{256,0},{1,257},{257,1},{2,258},{258,2},{3,259},{259,3},{4... | collective-permute-start | bytes 1572872 | tf_op jit(solution)/shard_map/ppermute | solution.py:240
  65.1 3.4 %collective-permute-start.9 = (bf16[128,1024]{1,0:T(8,128)(2,1)S(1)}, bf16[128,1024]{1,0:T(8,128)(2,1)S(1)}, u32[]{:S(2)}, u32[]{:S(2)}) collective-permute-start(bf16[128,1024]{1,0:T(8,128)(2,1)S(1)} %slice_bitcast_fusion), channel_id=1, source_target_pairs={{0,1},{1,0},{2,3},{3,2},{4,5},{5,4},{6,7},{7,6},{8,9},{9,8},{10,11... | collective-permute-start | bytes 786440 | tf_op jit(solution)/shard_map/ppermute | solution.py:240
  68.5 1.0 shard_map.44.same
  69.5 13.0 %collective-permute-done.9.side = bf16[128,1024]{1,0:T(8,128)(2,1)S(1)} collective-permute-done((bf16[128,1024]{1,0:T(8,128)(2,1)S(1)}, bf16[128,1024]{1,0:T(8,128)(2,1)S(1)}, u32[]{:S(2)}, u32[]{:S(2)}) %collective-permute-start.9) | collective-permute-done | bytes 262176 | tf_op jit(solution)/shard_map/ppermute | solution.py:240
  82.5 3.1 %collective-permute-done.8.twin = bf16[2,128,1024]{2,1,0:T(8,128)(2,1)S(1)} collective-permute-done((bf16[2,128,1024]{2,1,0:T(8,128)(2,1)S(1)}, bf16[2,128,1024]{2,1,0:T(8,128)(2,1)S(1)}, u32[]{:S(2)}, u32[]{:S(2)}) %collective-permute-start.8) | collective-permute-done | bytes 524320 | tf_op jit(solution)/shard_map/ppermute | solution.py:240
  85.6 0.0 collective-permute-done.7.cross
  85.6 0.0 all-to-all-done.1.precond
  85.6 1.6 %shard_map.45 = f32[4,128,512]{2,1,0:T(8,128)S(1)} custom-call(bf16[8,512,128]{2,1,0:T(8,128)(2,1)S(1)} %all-to-all-done.1.precond, bf16[128,1024]{1,0:T(8,128)(2,1)S(1)} %shard_map.44.same, bf16[128,1024]{1,0:T(8,128)(2,1)S(1)} %collective-permute-done.9.side, bf16[2,128,1024]{2,1,0:T(8,128)(2,1)S(1)} %collective-permute-done.7.cross, ...), custom_call_target="tpu_custom_call" | custom-call | flops 536870912 | bytes 3670016 | tf_op jit(solution)/shard_map/pallas_call | solution.py:25
  87.2 1.9 %collective-permute-start.10 = (f32[4,128,512]{2,1,0:T(8,128)S(1)}, f32[4,128,512]{2,1,0:T(8,128)S(1)}, u32[]{:S(2)}, u32[]{:S(2)}) collective-permute-start(f32[4,128,512]{2,1,0:T(8,128)S(1)} %shard_map.45), channel_id=1, source_target_pairs={{0,16},{16,0},{1,17},{17,1},{2,18},{18,2},{3,19},{19,3},{4,20},{20... | collective-permute-start | bytes 3145736 | tf_op jit(solution)/shard_map/ppermute | solution.py:240
  89.1 2.1 %shard_map.43.own = f32[4,128,512]{2,1,0:T(8,128)S(1)} custom-call(bf16[128,1024]{1,0:T(8,128)(2,1)} %copy-done.4, bf16[128,1024]{1,0:T(8,128)(2,1)} %copy-done.1, bf16[8,512,128]{2,1,0:T(8,128)(2,1)S(1)} %all-to-all-done.1.precond, bf16[2,128,1024]{2,1,0:T(8,128)(2,1)S(1)} %collective-permute-done.7.cross, bf16[2,128,1024]{2,1,0:T(8,128)(2,1)S(1)} %collective-permute-done.8.twin), custom_call_target="tpu_custom_call" | custom-call | flops 536870912 | bytes 4194304 | tf_op jit(solution)/shard_map/pallas_call | solution.py:171
  91.2 0.6 collective-permute-done.10.came
  91.7 0.6 shard_map.46
  92.4 27.4 %all_to_all.20 = bf16[32,16,512]{2,1,0:T(8,128)(2,1)S(1)} all-to-all(bf16[32,16,512]{2,1,0:T(8,128)(2,1)S(1)} %bitcast.18), channel_id=1, replica_groups={{14,15,270,271,0,1,256,257,12,13,268,269,2,3,258,259,10,11,266,267,4,5,..., dimensions={0} | all-to-all | bytes 1048576 | tf_op jit(solution)/shard_map/all_to_all | solution.py:244
  119.8 0.1 shard_map.47
  119.9 13.2 %all_to_all.21 = bf16[8,16,1024]{2,1,0:T(8,128)(2,1)S(1)} all-to-all(bf16[8,16,1024]{2,1,0:T(8,128)(2,1)S(1)} %shard_map.47), channel_id=1, replica_groups={{14,0,12,2,10,4,8,6},{15,1,13,3,11,5,9,7},{30,16,28,18,26,20,24,22},{31..., dimensions={0} | all-to-all | bytes 524288 | tf_op jit(solution)/shard_map/all_to_all | solution.py:244
  133.1 0.9 bitcast_convert_fusion
  (9 shorter events, 0.1 us)
Async XLA Ops:
  2.0 9.5 %copy-start.2 = (bf16[1,128,4096]{2,1,0:T(8,128)(2,1)S(1)}, bf16[1,128,4096]{2,1,0:T(8,128)(2,1)}, u32[]{:S(2)}) copy-start(bf16[1,128,4096]{2,1,0:T(8,128)(2,1)} %param.5) | copy-start | bytes 3145732
  2.0 9.5 %copy-start.3 = (bf16[128,1,4096]{2,0,1:T(8,128)(2,1)S(1)}, bf16[128,1,4096]{2,0,1:T(8,128)(2,1)}, u32[]{:S(2)}) copy-start(bf16[128,1,4096]{2,0,1:T(8,128)(2,1)} %param.3) | copy-start | bytes 3145732
  2.0 33.6 %all-to-all-start = ((bf16[8,512,128]{2,1,0:T(8,128)(2,1)}), bf16[8,512,128]{2,1,0:T(8,128)(2,1)S(1)}, u32[]{:S(2)}, u32[]{:S(2)}) async-start(bf16[8,512,128]{2,1,0:T(8,128)(2,1)} %shard_map.38), calls=%async_computation | async-start | bytes 2097152 | tf_op jit(solution)/shard_map/all_to_all | solution.py:244
  12.7 13.0 %copy-start.4 = (bf16[128,1024]{1,0:T(8,128)(2,1)}, bf16[128,1024]{1,0:T(8,128)(2,1)S(1)}, u32[]{:S(2)}) copy-start(bf16[128,1024]{1,0:T(8,128)(2,1)S(1)} %get-tuple-element.14.same) | copy-start | bytes 786436
  12.7 13.0 %copy-start.5 = (bf16[128,1024]{1,0:T(8,128)(2,1)}, bf16[128,1024]{1,0:T(8,128)(2,1)S(1)}, u32[]{:S(2)}) copy-start(bf16[128,1024]{1,0:T(8,128)(2,1)S(1)} %get-tuple-element.15.f0) | copy-start | bytes 786436
  12.7 13.0 %collective-permute-start.2 = (bf16[2,128,1024]{2,1,0:T(8,128)(2,1)S(1)}, bf16[2,128,1024]{2,1,0:T(8,128)(2,1)S(1)}, u32[]{:S(2)}, u32[]{:S(2)}) collective-permute-start(bf16[2,128,1024]{2,1,0:T(8,128)(2,1)S(1)} %get-tuple-element.19), channel_id=1, source_target_pairs={{0,16},{16,0},{1,17},{17,1},{2,18},{18,2},{3,19},{19,3},{4,20},{20... | collective-permute-start | bytes 1572872 | tf_op jit(solution)/shard_map/ppermute | solution.py:240
  14.6 12.2 %collective-permute-start.1 = (bf16[128,1024]{1,0:T(8,128)(2,1)S(1)}, bf16[128,1024]{1,0:T(8,128)(2,1)S(1)}, u32[]{:S(2)}, u32[]{:S(2)}) collective-permute-start(bf16[128,1024]{1,0:T(8,128)(2,1)S(1)} %get-tuple-element.16), channel_id=1, source_target_pairs={{0,257},{1,256},{256,1},{257,0},{2,259},{3,258},{258,3},{259,2},{4... | collective-permute-start | bytes 786440 | tf_op jit(solution)/shard_map/ppermute | solution.py:240
  17.6 9.3 %collective-permute-start.3 = (bf16[128,1024]{1,0:T(8,128)(2,1)S(1)}, bf16[128,1024]{1,0:T(8,128)(2,1)S(1)}, u32[]{:S(2)}, u32[]{:S(2)}) collective-permute-start(bf16[128,1024]{1,0:T(8,128)(2,1)S(1)} %get-tuple-element.20), channel_id=1, source_target_pairs={{0,16},{16,0},{1,17},{17,1},{2,18},{18,2},{3,19},{19,3},{4,20},{20... | collective-permute-start | bytes 786440 | tf_op jit(solution)/shard_map/ppermute | solution.py:240
  19.7 12.0 %collective-permute-start.4 = (bf16[128,1024]{1,0:T(8,128)(2,1)S(1)}, bf16[128,1024]{1,0:T(8,128)(2,1)S(1)}, u32[]{:S(2)}, u32[]{:S(2)}) collective-permute-start(bf16[128,1024]{1,0:T(8,128)(2,1)S(1)} %get-tuple-element.21), channel_id=1, source_target_pairs={{0,273},{1,272},{16,257},{17,256},{256,17},{257,16},{272,1},{273,0... | collective-permute-start | bytes 786440 | tf_op jit(solution)/shard_map/ppermute | solution.py:240
  23.7 10.3 %collective-permute-start = (bf16[128,1024]{1,0:T(8,128)(2,1)S(1)}, bf16[128,1024]{1,0:T(8,128)(2,1)S(1)}, u32[]{:S(2)}, u32[]{:S(2)}) collective-permute-start(bf16[128,1024]{1,0:T(8,128)(2,1)S(1)} %get-tuple-element.14.same), channel_id=1, source_target_pairs={{0,1},{1,0},{2,3},{3,2},{4,5},{5,4},{6,7},{7,6},{8,9},{9,8},{10,11... | collective-permute-start | bytes 786440 | tf_op jit(solution)/shard_map/ppermute | solution.py:240
  25.7 39.4 %copy-start = (bf16[2,128,1024]{2,1,0:T(8,128)(2,1)}, bf16[2,128,1024]{2,1,0:T(8,128)(2,1)S(1)}, u32[]{:S(2)}) copy-start(bf16[2,128,1024]{2,1,0:T(8,128)(2,1)S(1)} %collective-permute-done.2.came.refs_0_) | copy-start | bytes 1572868
  34.1 2.2 %copy-start.1 = (bf16[128,1024]{1,0:T(8,128)(2,1)}, bf16[128,1024]{1,0:T(8,128)(2,1)S(1)}, u32[]{:S(2)}) copy-start(bf16[128,1024]{1,0:T(8,128)(2,1)S(1)} %collective-permute-done.refs_2_.side) | copy-start | bytes 786436
  35.6 2.7 %copy-start.6 = (bf16[128,1024]{1,0:T(8,128)(2,1)S(1)}, bf16[128,1024]{1,0:T(8,128)(2,1)}, u32[]{:S(2)}) copy-start(bf16[128,1024]{1,0:T(8,128)(2,1)} %copy-done.5) | copy-start | bytes 786436
  36.3 3.8 %collective-permute-start.5 = (f32[2,512,128]{2,1,0:T(8,128)S(1)}, f32[2,512,128]{2,1,0:T(8,128)S(1)}, u32[]{:S(2)}, u32[]{:S(2)}) collective-permute-start(f32[2,512,128]{2,1,0:T(8,128)S(1)} %shard_map.41), channel_id=1, source_target_pairs={{0,16},{16,0},{1,17},{17,1},{2,18},{18,2},{3,19},{19,3},{4,20},{20... | collective-permute-start | bytes 1572872 | tf_op jit(solution)/shard_map/ppermute | solution.py:240
  40.2 11.7 %collective-permute-start.6 = (f32[512,128]{1,0:T(8,128)S(1)}, f32[512,128]{1,0:T(8,128)S(1)}, u32[]{:S(2)}, u32[]{:S(2)}) collective-permute-start(f32[512,128]{1,0:T(8,128)S(1)} %fusion), channel_id=1, source_target_pairs={{0,256},{256,0},{1,257},{257,1},{2,258},{258,2},{3,259},{259,3},{4... | collective-permute-start | bytes 786440 | tf_op jit(solution)/shard_map/ppermute | solution.py:240
  53.0 32.6 %all-to-all-start.1 = ((bf16[8,512,128]{2,1,0:T(8,128)(2,1)}), bf16[8,512,128]{2,1,0:T(8,128)(2,1)S(1)}, u32[]{:S(2)}, u32[]{:S(2)}) async-start(bf16[8,512,128]{2,1,0:T(8,128)(2,1)} %shard_map.42._), calls=%async_computation.1 | async-start | bytes 2097152 | tf_op jit(solution)/shard_map/all_to_all | solution.py:244
  58.7 26.9 %collective-permute-start.8 = (bf16[2,128,1024]{2,1,0:T(8,128)(2,1)S(1)}, bf16[2,128,1024]{2,1,0:T(8,128)(2,1)S(1)}, u32[]{:S(2)}, u32[]{:S(2)}) collective-permute-start(bf16[2,128,1024]{2,1,0:T(8,128)(2,1)S(1)} %shard_map.40.refs_0_), channel_id=1, source_target_pairs={{0,257},{1,256},{256,1},{257,0},{2,259},{3,258},{258,3},{259,2},{4... | collective-permute-start | bytes 1572872 | tf_op jit(solution)/shard_map/ppermute | solution.py:240
  62.4 23.2 %collective-permute-start.7 = (bf16[2,128,1024]{2,1,0:T(8,128)(2,1)S(1)}, bf16[2,128,1024]{2,1,0:T(8,128)(2,1)S(1)}, u32[]{:S(2)}, u32[]{:S(2)}) collective-permute-start(bf16[2,128,1024]{2,1,0:T(8,128)(2,1)S(1)} %shard_map.40.refs_0_), channel_id=1, source_target_pairs={{0,256},{256,0},{1,257},{257,1},{2,258},{258,2},{3,259},{259,3},{4... | collective-permute-start | bytes 1572872 | tf_op jit(solution)/shard_map/ppermute | solution.py:240
  65.1 17.4 %collective-permute-start.9 = (bf16[128,1024]{1,0:T(8,128)(2,1)S(1)}, bf16[128,1024]{1,0:T(8,128)(2,1)S(1)}, u32[]{:S(2)}, u32[]{:S(2)}) collective-permute-start(bf16[128,1024]{1,0:T(8,128)(2,1)S(1)} %slice_bitcast_fusion), channel_id=1, source_target_pairs={{0,1},{1,0},{2,3},{3,2},{4,5},{5,4},{6,7},{7,6},{8,9},{9,8},{10,11... | collective-permute-start | bytes 786440 | tf_op jit(solution)/shard_map/ppermute | solution.py:240
  87.2 4.6 %collective-permute-start.10 = (f32[4,128,512]{2,1,0:T(8,128)S(1)}, f32[4,128,512]{2,1,0:T(8,128)S(1)}, u32[]{:S(2)}, u32[]{:S(2)}) collective-permute-start(f32[4,128,512]{2,1,0:T(8,128)S(1)} %shard_map.45), channel_id=1, source_target_pairs={{0,16},{16,0},{1,17},{17,1},{2,18},{18,2},{3,19},{19,3},{4,20},{20... | collective-permute-start | bytes 3145736 | tf_op jit(solution)/shard_map/ppermute | solution.py:240
